TPU v7x, 32 devices: a whole 2x2x4 slice. The times are simulated.
32 devices in a mesh: case: 2 (over y), region: 4 (over x, core), sub: 4 (over z).
Axes of the slice: x: 2, y: 2, z: 4, core: 2. Of those that a mesh axis runs over, the one named last changes fastest.
Arguments:
- vol_feat: bfloat16 [16384, 128], P(('case', 'region', 'sub')), parts along dimension 0, may hold values from -6 to 6
- cotangent: bfloat16 [16384, 512], P(('case', 'region', 'sub')), parts along dimension 0, may hold values from -6 to 6
- surface: bfloat16 [16384, 128], P(('case', 'sub')), parts along dimension 0, may hold values from -6 to 6
- enc_weight: bfloat16 [128, 512], replicated, may hold values from -0.5 to 0.5
- enc_bias: float32 [512], replicated, may hold values from -3 to 3
- in_weight: bfloat16 [128, 512], replicated, may hold values from -0.5 to 0.5
- mid_weight: bfloat16 [512, 512], replicated, may hold values from -0.25 to 0.25
- first_bias: float32 [512], replicated, may hold values from -3 to 3
- out_weight: bfloat16 [512, 512], replicated, may hold values from -0.25 to 0.25
- second_bias: float32 [512], replicated, may hold values from -3 to 3
- block_owner: int32 [32, 4], P(('case', 'region', 'sub')), parts along dimension 0, may hold values from 0 to 3, each once within a row
- block_local: int32 [32, 4], P(('case', 'region', 'sub')), parts along dimension 0, may hold values from 0 to 15
- block_count: int32 [32], P(('case', 'region', 'sub')), parts along dimension 0, may hold values from 1 to 4, as said below
- entry_row: int32 [32, 512], P(('case', 'region', 'sub')), parts along dimension 0, may hold values from 0 to 127
- entry_cell: int32 [32, 512], P(('case', 'region', 'sub')), parts along dimension 0, may hold values from 0 to 511
Outputs:
- grad_surface: float32 [16384, 128], P(('case', 'sub')), parts along dimension 0
- grad_enc_weight: bfloat16 [256, 512], P('case'), parts along dimension 0
- grad_enc_bias: float32 [1024], P('case'), parts along dimension 0
- grad_in_weight: bfloat16 [256, 512], P('case'), parts along dimension 0
- grad_mid_weight: bfloat16 [1024, 512], P('case'), parts along dimension 0
- grad_first_bias: float32 [1024], P('case'), parts along dimension 0
- grad_out_weight: bfloat16 [1024, 512], P('case'), parts along dimension 0
- grad_second_bias: float32 [1024], P('case'), parts along dimension 0
There are 2 independent parts, one for each index of `case`. A program takes and returns all parts, laid end to end along the dimension named above; an argument that names none is the same for every part. Nothing has to cross between parts.
Inputs may be any that keep to these rules, and one draw needn't show every extreme that they name: `block_owner`: each row lists every sub index once. `block_count`: some device's count is 4.
All inputs are finite; a program needn't handle non-finite values.
Results may differ from a plain program's by a relative error of at most 0.0077.
Values may be sent and summed in bfloat16 or wider, within the bound.
No kernel may reach another device: no remote copies, remote signals or barrier semaphores. Data moves between devices by JAX's collectives and lax.ppermute only.
A program may use at most 64 MiB of HBM per device.

v0:
```python
import jax
import jax.numpy as jnp
from jax import lax
from jax.sharding import PartitionSpec as P

HIGHEST = lax.Precision.HIGHEST


def gelu_slope(values):
    return jax.vjp(jax.nn.gelu, values)[1](jnp.ones_like(values))[0]


def per_device(
    vol_feat,
    cotangent,
    surface,
    enc_weight,
    enc_bias,
    in_weight,
    mid_weight,
    first_bias,
    out_weight,
    second_bias,
    block_owner,
    block_local,
    block_count,
    entry_row,
    entry_cell,
):
    sub_count = lax.axis_size("sub")
    cell_count = vol_feat.shape[0]
    block_rows = entry_row.shape[1] // sub_count
    channels = surface.shape[1]
    hidden = enc_weight.shape[1]
    owners = block_owner[0]
    local_ids = block_local[0]
    live_blocks = (jnp.arange(sub_count) < block_count[0]).astype(jnp.int32)
    owner_match = (owners[:, None] == jnp.arange(sub_count)[None, :]).astype(
        jnp.int32
    ) * live_blocks[:, None]
    wanted = jnp.sum(owner_match * local_ids[:, None], axis=0)[:, None]
    asked = lax.all_to_all(wanted, "sub", split_axis=0, concat_axis=0, tiled=True)
    stored = surface.reshape(surface.shape[0] // block_rows, block_rows, channels)
    served = jnp.take(stored, asked[:, 0], axis=0)
    fetched = lax.all_to_all(served, "sub", split_axis=0, concat_axis=0, tiled=True)
    request_blocks = jnp.take(fetched, owners, axis=0)
    entry_live = jnp.repeat(live_blocks.astype(jnp.float32), block_rows)
    entry_cells = entry_cell[0]
    neighbours = jax.ops.segment_sum(entry_live, entry_cells, num_segments=cell_count)
    cell_scale = 1.0 / jnp.maximum(neighbours, 1.0)
    group_count = sub_count // 4
    group_rows = 4 * block_rows
    row_groups = entry_row[0].reshape(group_count, 4, block_rows)
    block_groups = request_blocks.reshape(group_count, 4, block_rows, channels)
    cell_groups = entry_cells.reshape(group_count, group_rows)
    live_groups = entry_live.reshape(group_count, group_rows)
    row_ids = jnp.arange(block_rows, dtype=jnp.int32)

    def pick_rows(group_row, group_blocks):
        row_pick = (group_row[:, :, None] == row_ids[None, None, :]).astype(jnp.bfloat16)
        gathered = jnp.einsum(
            "kij,kjc->kic", row_pick, group_blocks, preferred_element_type=jnp.float32
        )
        return (row_pick, gathered.astype(jnp.bfloat16).reshape(group_rows, channels))

    def encode(running, pieces):
        group_row, group_blocks, group_cell, group_live = pieces
        row_pick, gathered = pick_rows(group_row, group_blocks)
        pre_act = jnp.dot(gathered, enc_weight, preferred_element_type=jnp.float32) + enc_bias
        activated = jax.nn.gelu(pre_act) * group_live[:, None]
        return (running + jax.ops.segment_sum(activated, group_cell, num_segments=cell_count), None)

    enc_sum, _ = lax.scan(
        encode,
        jnp.zeros((cell_count, hidden), jnp.float32),
        (row_groups, block_groups, cell_groups, live_groups),
    )
    encoded = (enc_sum * cell_scale[:, None]).astype(jnp.bfloat16)
    pre_first = (
        jnp.dot(vol_feat, in_weight, preferred_element_type=jnp.float32)
        + jnp.dot(encoded, mid_weight, preferred_element_type=jnp.float32)
        + first_bias
    )
    first_out = jax.nn.gelu(pre_first).astype(jnp.bfloat16)
    pre_second = jnp.dot(first_out, out_weight, preferred_element_type=jnp.float32) + second_bias
    grad_second = (cotangent.astype(jnp.float32) * gelu_slope(pre_second)).astype(jnp.bfloat16)
    grad_out = jnp.einsum("ca,ch->ah", first_out, grad_second, preferred_element_type=jnp.float32)
    grad_sbias = jnp.sum(grad_second.astype(jnp.float32), axis=0)
    grad_hidden = jnp.einsum(
        "ch,ah->ca", grad_second, out_weight, preferred_element_type=jnp.float32
    )
    grad_first = (grad_hidden * gelu_slope(pre_first)).astype(jnp.bfloat16)
    grad_in = jnp.einsum("ca,ch->ah", vol_feat, grad_first, preferred_element_type=jnp.float32)
    grad_mid = jnp.einsum("ca,ch->ah", encoded, grad_first, preferred_element_type=jnp.float32)
    grad_fbias = jnp.sum(grad_first.astype(jnp.float32), axis=0)
    cell_grad = (
        jnp.einsum("ch,ah->ca", grad_first, mid_weight, preferred_element_type=jnp.float32)
        * cell_scale[:, None]
    )

    def reverse(running, pieces):
        grad_wenc, grad_benc = running
        group_row, group_blocks, group_cell, group_live = pieces
        row_pick, gathered = pick_rows(group_row, group_blocks)
        pre_act = jnp.dot(gathered, enc_weight, preferred_element_type=jnp.float32) + enc_bias
        picked = jnp.take(cell_grad, group_cell, axis=0)
        entry_grad = (picked * gelu_slope(pre_act) * group_live[:, None]).astype(jnp.bfloat16)
        grad_wenc = grad_wenc + jnp.einsum(
            "ec,eh->ch", gathered, entry_grad, preferred_element_type=jnp.float32
        )
        grad_benc = grad_benc + jnp.sum(entry_grad.astype(jnp.float32), axis=0)
        row_grad = jnp.einsum(
            "eh,ch->ec", entry_grad, enc_weight, preferred_element_type=jnp.float32
        )
        block_grad = jnp.einsum(
            "kij,kic->kjc",
            row_pick.astype(jnp.float32),
            row_grad.reshape(4, block_rows, channels),
            precision=HIGHEST,
        )
        return ((grad_wenc, grad_benc), block_grad)

    start_state = (jnp.zeros((channels, hidden), jnp.float32), jnp.zeros((hidden,), jnp.float32))
    final_state, block_grads = lax.scan(
        reverse, start_state, (row_groups, block_groups, cell_groups, live_groups)
    )
    grad_wenc, grad_benc = final_state
    slot_grads = (
        jnp.zeros((sub_count, block_rows, channels), jnp.float32)
        .at[owners]
        .set(block_grads.reshape(sub_count, block_rows, channels))
    )
    returned = lax.all_to_all(slot_grads, "sub", split_axis=0, concat_axis=0, tiled=True)
    grad_local = (
        jnp.zeros(stored.shape, jnp.float32)
        .at[asked[:, 0]]
        .add(returned)
        .reshape(surface.shape[0], channels)
    )
    summed = lax.psum(
        (grad_wenc, grad_benc, grad_in, grad_mid, grad_fbias, grad_out, grad_sbias),
        ("region", "sub"),
    )
    total_wenc, total_benc, total_in, total_mid, total_fbias, total_out, total_sbias = summed
    surface_total = lax.psum(grad_local, "region")
    return (
        surface_total,
        total_wenc.astype(jnp.bfloat16),
        total_benc,
        total_in.astype(jnp.bfloat16),
        total_mid.astype(jnp.bfloat16),
        total_fbias,
        total_out.astype(jnp.bfloat16),
        total_sbias,
    )


def solution(mesh):
    in_specs = (
        P(("case", "region", "sub"), None),
        P(("case", "region", "sub"), None),
        P(("case", "sub"), None),
        P(),
        P(),
        P(),
        P(),
        P(),
        P(),
        P(),
        P(("case", "region", "sub"), None),
        P(("case", "region", "sub"), None),
        P(("case", "region", "sub")),
        P(("case", "region", "sub"), None),
        P(("case", "region", "sub"), None),
    )
    out_specs = (
        P(("case", "sub"), None),
        P("case", None),
        P("case"),
        P("case", None),
        P("case", None),
        P("case"),
        P("case", None),
        P("case"),
    )
    return jax.shard_map(
        per_device, mesh=mesh, in_specs=in_specs, out_specs=out_specs, check_vma=False
    )
```

profile of v0, /device:TPU:0, one launch (start us, length us, event | category | flops | bytes accessed | tf_op | source)
XLA Modules:
  0.0 200.2 jit_solution(804355898432494323)
XLA Ops:
  7.2 0.0 copy-start
  7.9 0.0 copy-start.18
  7.9 0.0 copy-start.19
  7.9 0.6 copy-done.18
  8.6 0.0 copy-done.19
  8.6 0.1 multiply_reduce_fusion
  8.7 0.7 copy.33
  9.3 6.4 %all-to-all-start = ((s32[4,1,1]{2,1,0:T(1,128)}), s32[4,1,1]{2,1,0:T(1,128)S(1)}, u32[]{:S(2)}, u32[]{:S(2)}) async-start(s32[4,1,1]{2,1,0:T(1,128)} %copy.33), calls=%async_computation | async-start | bytes 4096 | tf_op jit(solution)/shard_map/all_to_all | solution.py:42
  15.8 0.1 broadcast_bitcast_fusion
  15.9 4.1 %scatter_custom_fusion.1 = f32[512]{0:T(512)S(1)} fusion(s32[512]{0:T(512)S(1)} %bitcast.54, f32[512]{0:T(512)S(1)} %broadcast_bitcast_fusion, f32[]{:T(128)} %constant.73.clone.1), kind=kCustom, calls=%fused_computation.85 | custom fusion | flops 512 | bytes 2052 | tf_op jit(solution)/shard_map/scatter-add | solution.py:49
  20.0 2.2 %fusion.52 = f32[512,512]{1,0:T(8,128)} fusion(bf16[512,128]{1,0:T(8,128)(2,1)} %param.15, bf16[128,512]{1,0:T(8,128)(2,1)} %param.20), kind=kOutput, calls=%fused_computation.94 | convolution fusion | flops 67108864 | bytes 1310720 | tf_op jit(solution)/shard_map/dot_general | solution.py:80
  22.2 0.2 reduce
  22.4 1.6 gather_fusion
  24.1 0.7 broadcast_select_fusion
  24.8 5.1 %all-to-all-start.1 = ((bf16[4,128,128]{2,1,0:T(8,128)(2,1)}), bf16[4,128,128]{2,1,0:T(8,128)(2,1)S(1)}, u32[]{:S(2)}, u32[]{:S(2)}) async-start(bf16[4,128,128]{2,1,0:T(8,128)(2,1)} %broadcast_select_fusion), calls=%async_computation.1 | async-start | bytes 262144 | tf_op jit(solution)/shard_map/all_to_all | solution.py:45
  29.9 0.0 copy-start.17
  29.9 5.9 %all-to-all-done.1 = bf16[4,128,128]{2,1,0:T(8,128)(2,1)S(1)} async-done(((bf16[4,128,128]{2,1,0:T(8,128)(2,1)}), bf16[4,128,128]{2,1,0:T(8,128)(2,1)S(1)}, u32[]{:S(2)}, u32[]{:S(2)}) %all-to-all-start.1) | async-done | bytes 131104 | tf_op jit(solution)/shard_map/all_to_all | solution.py:45
  35.8 0.6 gather_fusion.1
  36.4 0.0 copy-start.11
  36.4 0.0 copy-start.15
  36.4 0.3 convolution_convert_fusion
  36.7 0.0 copy-start.13
  36.7 0.6 copy-done.13
  37.3 0.3 convolution_add_fusion.2
  37.6 0.0 copy-start.6
  37.6 0.0 copy-start.16
  37.7 4.2 %scatter_custom_fusion = f32[512,512]{1,0:T(8,128)S(1)} fusion(s32[512]{0:T(512)S(1)} %bitcast.55, f32[512,512]{1,0:T(8,128)S(1)} %convolution_add_fusion.2, f32[512]{0:T(512)S(1)} %broadcast_bitcast_fusion, f32[]{:T(128)} %constant.117.clone.1, f32[]{:T(128)} %constant.116.clone.1, f32[]{:T(128)} %constant.115.clone.1, f32[]{:T(128)} %constant.114.clone.1, ...), kind=kCustom, calls=%fused_computation.50 | custom fusion | flops 2621440 | bytes 2099220 | tf_op jit(solution)/shard_map/while/body/eval_jaxpr/scatter-add | solution.py:71
  41.9 0.0 copy-start.20
  41.9 0.0 copy-start.21
  41.9 2.1 %fusion = f32[512,512]{1,0:T(8,128)S(1)} fusion(f32[512,512]{1,0:T(8,128)} %fusion.52, bf16[512,512]{1,0:T(8,128)(2,1)S(1)} %copy-done.6, f32[512]{0:T(512)S(1)} %copy-done.16, f32[512,512]{1,0:T(8,128)S(1)} %scatter_custom_fusion, f32[512]{0:T(512)S(1)} %maximum_divide_fusion), kind=kOutput, calls=%fused_computation.17 | convolution fusion | flops 269484032 | bytes 3674112 | tf_op jit(solution)/shard_map/dot_general | solution.py:81
  44.1 1.2 convert_reduce_fusion
  45.3 0.0 copy-start.22
  45.3 0.0 copy-start.7
  45.3 1.0 convert_reduce_fusion.1
  46.3 0.2 copy-done.7
  46.5 0.5 convolution_multiply_fusion
  47.0 2.3 %gather_fusion.2 = f32[512,512]{1,0:T(8,128)} fusion(f32[512,512]{1,0:T(8,128)S(1)} %convolution_multiply_fusion, s32[1024]{0:T(1024)S(1)} %pad_clamp_fusion), kind=kCustom, calls=%fused_computation.2 | custom fusion | bytes 2099200 | tf_op jit(solution)/shard_map/while/body/eval_jaxpr/jit(_take)/gather | solution.py:106
  49.3 2.0 %convert_reduce_fusion.2 = (f32[512]{0:T(512)S(1)}, bf16[512,512]{1,0:T(8,128)(2,1)S(1)}) fusion(f32[512]{0:T(512)S(1)} %broadcast_bitcast_fusion, f32[512,512]{1,0:T(8,128)S(1)} %convolution_add_fusion.2, f32[512,512]{1,0:T(8,128)} %gather_fusion.2, pred[512]{0:T(512)(128)(4,1)S(1)} %compare_and_fusion.2), kind=kLoop, calls=%fused_computation.47 | loop fusion | flops 6028800 | bytes 2626048 | tf_op jit(solution)/shard_map/while/body/eval_jaxpr/reduce_sum | solution.py:111
  51.4 0.3 fusion.53
  51.7 0.5 copy-done.4
  52.1 0.3 fusion.37
  52.4 0.7 broadcast_in_dim.75
  53.1 2.2 %scatter_fusion = f32[4,128,128]{2,1,0:T(8,128)} fusion(f32[4,128,128]{2,1,0:T(8,128)} %broadcast_in_dim.75, s32[4]{0:T(128)S(1)} %fusion.46, f32[4,128,128]{2,1,0:T(8,128)S(1)} %fusion.37), kind=kCustom, calls=%fused_computation.5 | custom fusion | bytes 786448 | tf_op jit(solution)/shard_map/scatter | solution.py:131
  55.3 3.4 %all-to-all-start.2 = ((f32[4,128,128]{2,1,0:T(8,128)}), f32[4,128,128]{2,1,0:T(8,128)S(1)}, u32[]{:S(2)}, u32[]{:S(2)}) async-start(f32[4,128,128]{2,1,0:T(8,128)} %scatter_fusion), calls=%async_computation.2 | async-start | bytes 524288 | tf_op jit(solution)/shard_map/all_to_all | solution.py:133
  58.8 0.2 all-reduce.4.cloned.1.call-start
  59.0 0.0 copy-start.23
  59.0 0.6 fusion.49
  59.6 0.6 copy-done.10
  60.2 0.1 copy-done.23
  60.4 1.6 fusion.50
  62.0 3.5 %all-to-all-done.2 = f32[4,128,128]{2,1,0:T(8,128)S(1)} async-done(((f32[4,128,128]{2,1,0:T(8,128)}), f32[4,128,128]{2,1,0:T(8,128)S(1)}, u32[]{:S(2)}, u32[]{:S(2)}) %all-to-all-start.2) | async-done | bytes 262176 | tf_op jit(solution)/shard_map/all_to_all | solution.py:133
  65.5 0.1 broadcast_in_dim.74
  65.6 0.8 scatter_fusion.1
  66.4 0.0 copy-start.3
  66.4 0.0 copy-start.12
  66.4 0.9 copy-done.3
  67.3 0.0 all-reduce.4.cloned.1.call-update
  67.4 0.1 copy-done.12
  67.4 0.3 convolution_bitcast_fusion
  67.8 0.7 copy-done.5
  68.5 1.2 fusion.54
  69.6 120.7 %all-reduce.5 = (bf16[128,512]{1,0:T(8,128)(2,1)}, f32[512]{0:T(512)}, bf16[128,512]{0,1:T(8,128)(2,1)S(1)}, bf16[512,512]{1,0:T(8,128)(2,1)}, f32[512]{0:T(512)}, /*index=5*/bf16[512,512]{1,0:T(8,128)(2,1)}, f32[512]{0:T(512)}) all-reduce(f32[128,512]{1,0:T(8,128)S(1)} %fusion.54, ...), channel_id=1, replica_groups=mesh['case'=2,'region'=4,'sub'=4] {'region','sub'}, use_global_device_ids=true, to_apply=%region_6.7 | all-reduce | flops 656896 | bytes 3944448 | tf_op jit(solution)/shard_map/psum | solution.py:140
  190.3 0.8 copy.35
  191.1 2.3 %copy.52 = f32[2048,128]{1,0:T(8,128)} copy(f32[2048,128]{1,0:T(8,128)} %all-reduce.4.cloned.1.call-done) | data formatting | bytes 2097152
  (35 shorter events, 0.1 us)
Async XLA Ops:
  7.2 36.9 %copy-start = (bf16[512,512]{1,0:T(8,128)(2,1)S(1)}, bf16[512,512]{1,0:T(8,128)(2,1)}, u32[]{:S(2)}) copy-start(bf16[512,512]{1,0:T(8,128)(2,1)} %param.23) | copy-start | bytes 1572868
  7.9 0.7 copy-start.18
  7.9 0.7 copy-start.19
  9.3 6.5 %copy-start.14 = (s32[1,512]{1,0:T(1,128)S(1)}, s32[1,512]{1,0:T(1,128)}, u32[]{:S(2)}) copy-start(s32[1,512]{1,0:T(1,128)} %param.29) | copy-start | bytes 6148
  9.3 12.9 %all-to-all-start = ((s32[4,1,1]{2,1,0:T(1,128)}), s32[4,1,1]{2,1,0:T(1,128)S(1)}, u32[]{:S(2)}, u32[]{:S(2)}) async-start(s32[4,1,1]{2,1,0:T(1,128)} %copy.33), calls=%async_computation | async-start | bytes 4096 | tf_op jit(solution)/shard_map/all_to_all | solution.py:42
  24.8 11.0 %all-to-all-start.1 = ((bf16[4,128,128]{2,1,0:T(8,128)(2,1)}), bf16[4,128,128]{2,1,0:T(8,128)(2,1)S(1)}, u32[]{:S(2)}, u32[]{:S(2)}) async-start(bf16[4,128,128]{2,1,0:T(8,128)(2,1)} %broadcast_select_fusion), calls=%async_computation.1 | async-start | bytes 262144 | tf_op jit(solution)/shard_map/all_to_all | solution.py:45
  29.9 6.5 %copy-start.17 = (s32[1,512]{1,0:T(1,128)S(1)}, s32[1,512]{1,0:T(1,128)}, u32[]{:S(2)}) copy-start(s32[1,512]{1,0:T(1,128)} %param.28) | copy-start | bytes 6148
  36.4 1.0 copy-start.11
  36.4 1.0 copy-start.15
  36.7 0.7 copy-start.13
  37.6 4.2 %copy-start.6 = (bf16[512,512]{1,0:T(8,128)(2,1)S(1)}, bf16[512,512]{1,0:T(8,128)(2,1)}, u32[]{:S(2)}) copy-start(bf16[512,512]{1,0:T(8,128)(2,1)} %param.21) | copy-start | bytes 1572868
  37.6 4.2 %copy-start.16 = (f32[512]{0:T(512)S(1)}, f32[512]{0:T(512)}, u32[]{:S(2)}) copy-start(f32[512]{0:T(512)} %param.22) | copy-start | bytes 6148
  41.9 2.1 %copy-start.1 = (f32[512,512]{1,0:T(8,128)}, f32[512,512]{1,0:T(8,128)S(1)}, u32[]{:S(2)}) copy-start(f32[512,512]{1,0:T(8,128)S(1)} %scatter_custom_fusion) | copy-start | bytes 3145732
  41.9 2.2 %copy-start.20 = (bf16[512,512]{1,0:T(8,128)(2,1)S(1)}, bf16[512,512]{1,0:T(8,128)(2,1)}, u32[]{:S(2)}) copy-start(bf16[512,512]{1,0:T(8,128)(2,1)} %param.16) | copy-start | bytes 1572868
  41.9 2.2 %copy-start.21 = (f32[512]{0:T(512)S(1)}, f32[512]{0:T(512)}, u32[]{:S(2)}) copy-start(f32[512]{0:T(512)} %param.24) | copy-start | bytes 6148
  44.1 1.2 copy-start.9
  45.3 1.0 copy-start.22
  45.3 1.2 copy-start.7
  51.3 0.8 copy-start.4
  52.1 6.9 %copy-start.2 = (f32[512,512]{1,0:T(8,128)S(1)}, f32[512,512]{1,0:T(8,128)}, u32[]{:S(2)}) copy-start(f32[512,512]{1,0:T(8,128)} %copy-done.1) | copy-start | bytes 3145732
  55.3 10.2 %all-to-all-start.2 = ((f32[4,128,128]{2,1,0:T(8,128)}), f32[4,128,128]{2,1,0:T(8,128)S(1)}, u32[]{:S(2)}, u32[]{:S(2)}) async-start(f32[4,128,128]{2,1,0:T(8,128)} %scatter_fusion), calls=%async_computation.2 | async-start | bytes 524288 | tf_op jit(solution)/shard_map/all_to_all | solution.py:133
  58.8 132.3 %all-reduce.4.cloned.1.call-start = ((), (), s32[]{:S(2)}) async-start(), calls=%async_computation.3 | async-start | bytes 2097152 | tf_op jit(solution)/shard_map/psum | solution.py:145
  59.0 1.2 copy-start.10
  59.0 1.3 copy-start.23
  66.4 1.0 copy-start.3
  66.4 1.0 copy-start.12
  67.4 1.0 copy-start.5
  67.4 2.2 %copy-start.8 = (f32[512,512]{1,0:T(8,128)S(1)}, f32[512,512]{1,0:T(8,128)}, u32[]{:S(2)}) copy-start(f32[512,512]{1,0:T(8,128)} %fusion.50) | copy-start | bytes 3145732
Sparse Core Ops, SparseCore 0:
  67.5 39.6 all-reduce.3
where the time goes:
time: 201 us; the launch traced here: 200 us
  blocking collectives  121 us (60%)
  local copies, waits for them, and re-layouts  15.9 us (8%)
  starting transfers between devices  15.2 us (8%)
  between operations  15.2 us (8%)
  other arithmetic  12.1 us (6%)
  matrix products  11.8 us (6%)
  waiting for transfers between devices  9.45 us (5%)
    psum x1, blocking collectives, per_device(): lax.psum((grad_wenc, grad_benc, grad_in, grad_mid, grad_fbias, grad_out,...  121 us
    unnamed x50, local copies, waits for them, and re-layouts  7.65 us
    all_to_all x1, starting transfers between devices, per_device(): lax.all_to_all(wanted, 'sub', split_axis=0, concat_axis=0, tiled=True)  6.45 us
    all_to_all x1, waiting for transfers between devices, per_device(): lax.all_to_all(served, 'sub', split_axis=0, concat_axis=0, tiled=True)  5.9 us
    all_to_all x1, starting transfers between devices, per_device(): lax.all_to_all(served, 'sub', split_axis=0, concat_axis=0, tiled=True)  5.08 us
    scatter-add x1, other arithmetic, encode(): jax.ops.segment_sum(activated, group_cell, num_segments=cell_count)  4.19 us
    scatter-add x1, other arithmetic, per_device(): jax.ops.segment_sum(entry_live, entry_cells, num_segments=cell_count)  4.08 us
  transfers between devices with their start and end apart: 4, of which 2 were waited for; matrix products, arithmetic and copies ran while one was open for 5% of the time, Pallas kernels for 0%

commit v1 on v0

v1 whole, which is shorter than its diff:
```python
import functools

import jax
import jax.numpy as jnp
from jax import lax
from jax.experimental import pallas as pl
from jax.experimental.pallas import tpu as pltpu
from jax.sharding import PartitionSpec as P

BF16 = jnp.bfloat16
F32 = jnp.float32
VMEM = pl.BlockSpec(memory_space=pltpu.VMEM)
SMEM = pl.BlockSpec(memory_space=pltpu.SMEM)
ANY = pl.BlockSpec(memory_space=pl.ANY)
GROUP = 4
LIMIT = 48 * 1024 * 1024
PARAMS = pltpu.CompilerParams(vmem_limit_bytes=LIMIT)


def nn(a, b):
    return jnp.dot(a, b, preferred_element_type=F32)


def tn(a, b):
    return lax.dot_general(a, b, (((0,), (0,)), ((), ())), preferred_element_type=F32)


def nt(a, b):
    return lax.dot_general(a, b, (((1,), (1,)), ((), ())), preferred_element_type=F32)


def gelu_pair(v):
    square = v * v
    t = jnp.tanh(0.7978845608028654 * v * (1.0 + 0.044715 * square))
    half = 0.5 * (1.0 + t)
    inner = 0.7978845608028654 * (1.0 + 0.134145 * square)
    return v * half, half + 0.5 * v * (1.0 - t * t) * inner


def col_sum(a):
    return jnp.sum(a.astype(F32), axis=0, keepdims=True)


def loop(count, body):
    if count == 1:
        body(0)
    else:
        lax.fori_loop(0, count, lambda i, c: (body(i), c)[1], 0)


def serve_kernel(me_ref, *refs):
    count = (len(refs) - 3) // 2
    requests, surface, blocks = refs[:count], refs[count], refs[count + 1 : 2 * count + 1]
    ids_ref, sems = refs[2 * count + 1], refs[2 * count + 2]
    rows = blocks[0].shape[0]
    me = me_ref[0]
    copies = []
    for m, request in enumerate(requests):
        wanted = jnp.int32(0)
        for k in range(count):
            wanted = wanted + jnp.where(request[0, k] == me, request[0, count + k], 0)
        ids_ref[m] = wanted
        copy = pltpu.make_async_copy(
            surface.at[pl.ds(pl.multiple_of(wanted * rows, rows), rows), :], blocks[m], sems.at[m]
        )
        copy.start()
        copies.append(copy)
    for copy in copies:
        copy.wait()


def main_kernel(n_pieces, place_ref, owner_ref, count_ref, *refs):
    pieces = refs[:n_pieces]
    (
        row_ref,
        cell_ref,
        vol_ref,
        cot_ref,
        wenc_ref,
        benc_ref,
        win_ref,
        wmid_ref,
        b1_ref,
        wout_ref,
        b2_ref,
        keep_ref,
        send_ref,
        surf_ref,
        bias_ref,
        blocks,
        gathered_ref,
        slope_ref,
        hot_ref,
        total_ref,
        count_sum,
        wenc_sum,
        benc_sum,
    ) = refs[n_pieces:]
    half, mask = place_ref[0], place_ref[1]
    groups = row_ref.shape[0]
    cells, hidden = cot_ref.shape
    block_rows, channels = blocks.shape[1:]
    entries = GROUP * block_rows
    base = 0
    for piece in pieces:
        if len(piece.shape) == 2:
            blocks[base] = piece[...]
            base += 1
        else:
            blocks[...] = piece[...]
    live_count = count_ref[0]

    def row_hot(g, k):
        rows = lax.broadcasted_iota(jnp.int32, (block_rows, block_rows), 0)
        named = row_ref[g][:, k * block_rows : (k + 1) * block_rows]
        return (rows == named).astype(BF16)

    total_ref[...] = jnp.zeros_like(total_ref)
    count_sum[...] = jnp.zeros_like(count_sum)

    def encode(g):
        lane = lax.broadcasted_iota(jnp.int32, (1, entries), 1) // block_rows + g * GROUP
        named = jnp.where(lane < live_count, cell_ref[g], -1)
        hot = (lax.broadcasted_iota(jnp.int32, (cells, entries), 0) == named).astype(BF16)
        hot_ref[g] = hot
        for k in range(GROUP):
            block = blocks[owner_ref[g * GROUP + k] ^ mask]
            gathered_ref[g, k * block_rows : (k + 1) * block_rows, :] = tn(
                row_hot(g, k), block
            ).astype(BF16)
        act, slope = gelu_pair(nn(gathered_ref[g], wenc_ref[...]) + benc_ref[...])
        slope_ref[g] = slope
        total_ref[...] += nn(hot, act.astype(BF16))
        count_sum[...] += nn(hot, jnp.ones((entries, channels), BF16))

    loop(groups, encode)
    scale = 1.0 / jnp.maximum(count_sum[...], 1.0)
    scale = jnp.concatenate([scale] * (hidden // channels), axis=1)
    encoded = (total_ref[...] * scale).astype(BF16)
    pre_first = nn(vol_ref[...], win_ref[...]) + nn(encoded, wmid_ref[...]) + b1_ref[...]
    first, first_slope = gelu_pair(pre_first)
    first = first.astype(BF16)
    _, second_slope = gelu_pair(nn(first, wout_ref[...]) + b2_ref[...])
    grad_second = (cot_ref[...].astype(F32) * second_slope).astype(BF16)
    grad_first = (nt(grad_second, wout_ref[...]) * first_slope).astype(BF16)
    grad_cell = (nt(grad_first, wmid_ref[...]) * scale).astype(BF16)
    wenc_sum[...] = jnp.zeros_like(wenc_sum)
    benc_sum[...] = jnp.zeros_like(benc_sum)

    def reverse(g):
        grad_entry = (tn(hot_ref[g], grad_cell) * slope_ref[g]).astype(BF16)
        wenc_sum[...] += tn(gathered_ref[g], grad_entry)
        benc_sum[0:1, :] += col_sum(grad_entry)
        grad_row = nt(grad_entry, wenc_ref[...]).astype(BF16)
        for k in range(GROUP):
            grad_block = nn(row_hot(g, k), grad_row[k * block_rows : (k + 1) * block_rows, :])
            grad_block = grad_block.astype(BF16)
            slot = owner_ref[g * GROUP + k] ^ mask
            quarter = block_rows // 4
            for q in range(4):
                surf_ref[slot, :, q * channels : (q + 1) * channels] = grad_block[
                    q * quarter : (q + 1) * quarter, :
                ]

    loop(groups, reverse)
    benc_sum[1:2, :] = col_sum(grad_first)
    benc_sum[2:3, :] = col_sum(grad_second)
    sums = benc_sum[...]
    high = sums.astype(BF16).astype(F32)
    bias_ref[...] = jnp.concatenate([high, sums - high], axis=0).astype(BF16)

    def put(first_at, rows, values, twin=None):
        values = values.astype(BF16)
        low = values[: values.shape[0] // 2] if twin is None else values
        top = values[values.shape[0] // 2 :] if twin is None else twin.astype(BF16)

        @pl.when(half == 0)
        def _():
            for i in range(keep_ref.shape[0]):
                keep_ref[i, first_at : first_at + rows, :] = low[i * rows : (i + 1) * rows, :]
                send_ref[i, first_at : first_at + rows, :] = top[i * rows : (i + 1) * rows, :]

        @pl.when(half != 0)
        def _():
            for i in range(keep_ref.shape[0]):
                send_ref[i, first_at : first_at + rows, :] = low[i * rows : (i + 1) * rows, :]
                keep_ref[i, first_at : first_at + rows, :] = top[i * rows : (i + 1) * rows, :]

    put(0, 32, tn(first, grad_second))
    put(32, 32, tn(encoded, grad_first))
    put(64, 16, tn(vol_ref[...], grad_first), wenc_sum[...])


def halve_kernel(place_ref, keep_ref, got_ref, next_keep, next_send):
    mine = place_ref[0]
    quarter = next_keep.shape[0]
    for out, at in ((next_keep, mine), (next_send, 1 - mine)):
        rows = pl.ds(at * quarter, quarter)
        out[...] = (keep_ref[rows].astype(F32) + got_ref[rows].astype(F32)).astype(BF16)


def split_kernel(place_ref, keep_ref, got_ref, surf_ref, bias_ref, *outs):
    mine = place_ref[0]
    rows = keep_ref.shape[1]
    more = surf_ref.shape[1]
    for m, out in enumerate(outs):
        at = mine ^ m
        out[0:rows, :] = (keep_ref[at].astype(F32) + got_ref[at].astype(F32)).astype(BF16)
        out[rows : rows + more, :] = surf_ref[m]
        out[rows + more :, :] = bias_ref[...]


def sum_kernel(*refs):
    out = refs[-1]
    rows = out.shape[0]
    total = refs[0][0:rows, :].astype(F32)
    for ref in refs[1:-1]:
        total = total + ref[0:rows, :].astype(F32)
    out[...] = total.astype(BF16)


def join_kernel(*refs):
    out = refs[-1]
    count = out.shape[0]
    for m in range(count):
        rows = refs[m].shape[0]
        out[m, 0:rows, :] = refs[m][...]
        out[m, rows:, :] = refs[count + m][rows:, :]


def final_kernel(
    place_ref, ids_ref, own, over_x, over_core, over_both, surf, wenc, benc, win, wmid, b1, wout, b2
):
    c, x, z = place_ref[0], place_ref[1], place_ref[2]
    surf[...] = jnp.zeros_like(surf)
    block_rows, channels = surf.shape[1:]
    bias = None
    for at, (ref, core, chip) in enumerate(
        ((own, c, x), (over_x, c, 1 - x), (over_core, 1 - c, x), (over_both, 1 - c, 1 - x))
    ):
        for m in range(4):
            spot = chip * 4 + (z ^ m)
            shard = core * 8 + spot
            wout[pl.ds(pl.multiple_of(shard * 32, 32), 32), :] = ref[m, 0:32, :]
            wmid[pl.ds(pl.multiple_of(shard * 32, 32), 32), :] = ref[m, 32:64, :]
            narrow = pl.ds(pl.multiple_of(spot * 16, 16), 16)

            @pl.when(core == 0)
            def _():
                win[narrow, :] = ref[m, 64:80, :]

            @pl.when(core != 0)
            def _():
                wenc[narrow, :] = ref[m, 64:80, :]

            block = ids_ref[at, m]
            quarter = block_rows // 4
            for q in range(4):
                surf[block, q * quarter : (q + 1) * quarter, :] += ref[
                    m, 80:112, q * channels : (q + 1) * channels
                ].astype(F32)
            term = ref[m, 112:128, :].astype(F32)
            bias = term if bias is None else bias + term
    bias = bias[0:8, :] + bias[8:16, :]
    benc[...] = bias[0:1, :]
    b1[...] = bias[1:2, :]
    b2[...] = bias[2:3, :]


def call(kernel, out_shape, in_specs, *args, out_specs=None, scratch=(), flops=0):
    many = isinstance(out_shape, (list, tuple))
    return pl.pallas_call(
        kernel,
        out_shape=out_shape,
        in_specs=in_specs,
        out_specs=out_specs or ([VMEM] * len(out_shape) if many else VMEM),
        scratch_shapes=scratch,
        compiler_params=PARAMS,
        cost_estimate=pl.CostEstimate(flops=flops, bytes_accessed=1 << 20, transcendentals=0),
    )(*args)


def shape(dims, kind=BF16):
    return jax.ShapeDtypeStruct(dims, kind)


def compute(place, owner, count, pieces, entry_row, entry_cell, arrays):
    vol, cot, wenc, benc, win, wmid, b1, wout, b2 = arrays
    n_sub = owner.shape[0]
    block_rows = entry_row.shape[1] // n_sub
    cells, channels = vol.shape
    hidden = cot.shape[1]
    groups = n_sub // GROUP
    entries = GROUP * block_rows
    return call(
        functools.partial(main_kernel, len(pieces)),
        [
            shape((8, 80, hidden)),
            shape((8, 80, hidden)),
            shape((n_sub, block_rows // 4, hidden)),
            shape((16, hidden)),
        ],
        [SMEM] * 3 + [VMEM] * (len(pieces) + 11),
        place,
        owner,
        count,
        *pieces,
        entry_row.reshape(groups, 1, entries),
        entry_cell.reshape(groups, 1, entries),
        vol,
        cot,
        wenc,
        benc.reshape(1, hidden),
        win,
        wmid,
        b1.reshape(1, hidden),
        wout,
        b2.reshape(1, hidden),
        scratch=[
            pltpu.VMEM((n_sub, block_rows, channels), BF16),
            pltpu.VMEM((groups, entries, channels), BF16),
            pltpu.VMEM((groups, entries, hidden), F32),
            pltpu.VMEM((groups, cells, entries), BF16),
            pltpu.VMEM((cells, hidden), F32),
            pltpu.VMEM((cells, channels), F32),
            pltpu.VMEM((channels, hidden), F32),
            pltpu.VMEM((8, hidden), F32),
        ],
        flops=1 << 31,
    )


def swap(value, axis, mask, size):
    return lax.ppermute(value, axis, [(i, i ^ mask) for i in range(size)])


def on_block(surface, owner, local, count, entry_row, entry_cell, arrays):
    region, me = lax.axis_index("region"), lax.axis_index("sub")
    core, chip = region % 2, region // 2
    n_sub = owner.shape[0]
    block_rows = entry_row.shape[1] // n_sub
    channels = surface.shape[1]
    hidden = arrays[1].shape[1]
    along_z = range(1, n_sub)

    request = jnp.concatenate([owner, local]).reshape(1, 2 * n_sub)
    requests = [request] + [swap(request, "sub", m, n_sub) for m in along_z]
    *blocks, ids = call(
        serve_kernel,
        [shape((block_rows, channels))] * n_sub + [shape((n_sub,), jnp.int32)],
        [SMEM] * (n_sub + 1) + [ANY],
        me.reshape(1),
        *requests,
        surface,
        out_specs=[VMEM] * n_sub + [SMEM],
        scratch=[pltpu.SemaphoreType.DMA((n_sub,))],
    )
    blocks = [blocks[0]] + [swap(blocks[m], "sub", m, n_sub) for m in along_z]
    ids = ids.reshape(1, n_sub)
    ids = jnp.concatenate([ids, swap(ids, "region", 2, 4)])
    ids = jnp.concatenate([ids, swap(ids, "region", 1, 4)])

    keep, send, surf, bias = compute(
        jnp.stack([core, me]), owner, count, blocks, entry_row, entry_cell, arrays
    )
    got = swap(send, "region", 1, 4)
    keep, send = call(
        halve_kernel, [shape((4, 80, hidden))] * 2, [SMEM, VMEM, VMEM], chip.reshape(1), keep, got
    )
    got = swap(send, "region", 2, 4)
    messages = call(
        split_kernel,
        [shape((128, hidden))] * n_sub,
        [SMEM] + [VMEM] * 4,
        me.reshape(1),
        keep,
        got,
        surf,
        bias,
    )
    messages = [messages[0]] + [swap(messages[m], "sub", m, n_sub) for m in along_z]
    total = call(sum_kernel, shape((80, hidden)), [VMEM] * n_sub, *messages)
    totals = [total] + [swap(total, "sub", m, n_sub) for m in along_z]
    own = call(join_kernel, shape((n_sub, 128, hidden)), [VMEM] * (2 * n_sub), *totals, *messages)
    over_x = swap(own, "region", 2, 4)
    over_core = swap(own, "region", 1, 4)
    over_both = swap(over_x, "region", 1, 4)
    surf, wenc, benc, win, wmid, b1, wout, b2 = call(
        final_kernel,
        [
            shape((surface.shape[0] // block_rows, block_rows, channels), F32),
            shape((128, hidden)),
            shape((1, hidden), F32),
            shape((128, hidden)),
            shape((512, hidden)),
            shape((1, hidden), F32),
            shape((512, hidden)),
            shape((1, hidden), F32),
        ],
        [SMEM, SMEM] + [VMEM] * 4,
        jnp.stack([core, chip, me]),
        ids,
        own,
        over_x,
        over_core,
        over_both,
    )
    return (
        surf.reshape(surface.shape),
        wenc,
        benc.reshape(hidden),
        win,
        wmid,
        b1.reshape(hidden),
        wout,
        b2.reshape(hidden),
    )


def on_any(surface, owner, local, count, entry_row, entry_cell, arrays):
    n_sub = owner.shape[0]
    block_rows = entry_row.shape[1] // n_sub
    channels = surface.shape[1]
    hidden = arrays[1].shape[1]
    to_all = functools.partial(lax.all_to_all, axis_name="sub", split_axis=0, concat_axis=0, tiled=True)
    wanted = jnp.zeros((n_sub,), jnp.int32).at[owner].set(local)
    asked = to_all(wanted)
    stored = surface.reshape(surface.shape[0] // block_rows, block_rows, channels)
    fetched = to_all(jnp.take(stored, asked, axis=0))
    keep, send, surf, bias = compute(
        jnp.zeros((2,), jnp.int32), owner, count, [fetched], entry_row, entry_cell, arrays
    )
    surf = to_all(surf).astype(F32).reshape(n_sub, block_rows // 4, 4, channels)
    surf = surf.transpose(0, 2, 1, 3).reshape(n_sub, block_rows, channels)
    surf = jnp.zeros(stored.shape, F32).at[asked].add(surf).reshape(surface.shape)
    bias = bias[0:8].astype(F32) + bias[8:16].astype(F32)
    shards, bias = lax.psum(
        (jnp.concatenate([keep, send]).astype(F32), bias), ("region", "sub")
    )
    shards = shards.astype(BF16)
    small = shards[:, 64:80].reshape(256, hidden)
    return (
        lax.psum(surf, "region"),
        small[128:],
        bias[0],
        small[:128],
        shards[:, 32:64].reshape(512, hidden),
        bias[1],
        shards[:, 0:32].reshape(512, hidden),
        bias[2],
    )


def per_device(
    vol_feat,
    cotangent,
    surface,
    enc_weight,
    enc_bias,
    in_weight,
    mid_weight,
    first_bias,
    out_weight,
    second_bias,
    block_owner,
    block_local,
    block_count,
    entry_row,
    entry_cell,
):
    arrays = (
        vol_feat,
        cotangent,
        enc_weight,
        enc_bias,
        in_weight,
        mid_weight,
        first_bias,
        out_weight,
        second_bias,
    )
    small = lax.axis_size("region") == 4 and lax.axis_size("sub") == 4
    run = on_block if small else on_any
    return run(
        surface, block_owner[0], block_local[0], block_count, entry_row, entry_cell, arrays
    )


def solution(mesh):
    by_cell = P(("case", "region", "sub"), None)
    in_specs = (
        (by_cell, by_cell, P(("case", "sub"), None))
        + (P(),) * 7
        + (by_cell, by_cell, P(("case", "region", "sub")), by_cell, by_cell)
    )
    rows, line = P("case", None), P("case")
    out_specs = (P(("case", "sub"), None), rows, line, rows, rows, line, rows, line)
    return jax.shard_map(
        per_device, mesh=mesh, in_specs=in_specs, out_specs=out_specs, check_vma=False
    )
```

time: 201 us -> 84.5 us (0.42)
  blocking collectives: 121 us -> 0 us
  waiting for transfers between devices: 9.45 us -> 41.1 us
  between operations: 15.2 us -> 1.45 us
  other arithmetic: 12.1 us -> 0.24 us
  matrix products: 11.8 us -> 0 us
  Pallas kernels: 0 us -> 10.3 us
  local copies, waits for them, and re-layouts: 15.9 us -> 7.22 us
  starting transfers between devices: 15.2 us -> 23.8 us
    psum x1 -> x0, blocking collectives: 121 us -> none  [per_device(): lax.psum((grad_wenc, grad_benc, grad_in, grad_mid, grad_fbias, grad_out,...]
    ppermute x0 -> x19, waiting for transfers between devices: none -> 41.1 us  [swap(): return lax.ppermute(value, axis, [(i, i ^ mask) for i in range(size)])]
    ppermute x0 -> x19, starting transfers between devices: none -> 23.8 us  [swap(): return lax.ppermute(value, axis, [(i, i ^ mask) for i in range(size)])]
    all_to_all x3 -> x0, starting transfers between devices: 14.9 us -> none  [the longest x1 6.45 us: per_device(): lax.all_to_all(wanted, 'sub', split_axis=0, concat_axis=0, tiled=True)]
    dot_general x13 -> x0, matrix products: 11.8 us -> none  [the longest x1 2.22 us: per_device(): jnp.dot(vol_feat, in_weight, preferred_element_type=jnp.float32)]
    pallas_call x0 -> x7, Pallas kernels: none -> 10.3 us  [call(): pl.pallas_call(kernel, out_shape=out_shape, in_specs=in_specs, out_specs=...]
    all_to_all x3 -> x0, waiting for transfers between devices: 9.43 us -> none  [the longest x1 5.9 us: per_device(): lax.all_to_all(served, 'sub', split_axis=0, concat_axis=0, tiled=True)]
    scatter-add x3 -> x0, other arithmetic: 9.02 us -> none  [the longest x1 4.19 us: encode(): jax.ops.segment_sum(activated, group_cell, num_segments=cell_count)]
  transfers between devices with their start and end apart: 4 -> 19, of which waited for: 2 -> 12; matrix products, arithmetic and copies ran while one was open for 5% -> 0% of each run, Pallas kernels for 0% -> 0%
where the time goes in v1:
time: 84.5 us; the launch traced here: 84.1 us
  waiting for transfers between devices  41.1 us (49%)
  starting transfers between devices  23.8 us (28%)
  Pallas kernels  10.3 us (12%)
  local copies, waits for them, and re-layouts  7.22 us (9%)
  between operations  1.45 us (2%)
    ppermute x19, waiting for transfers between devices, swap(): return lax.ppermute(value, axis, [(i, i ^ mask) for i in range(size)])  41.1 us
    ppermute x19, starting transfers between devices, swap(): return lax.ppermute(value, axis, [(i, i ^ mask) for i in range(size)])  23.8 us
    pallas_call x7, Pallas kernels, call(): pl.pallas_call(kernel, out_shape=out_shape, in_specs=in_specs, out_specs=...  10.3 us
    unnamed x28, local copies, waits for them, and re-layouts  7.22 us
  transfers between devices with their start and end apart: 19, of which 12 were waited for; matrix products, arithmetic and copies ran while one was open for 0% of the time, Pallas kernels for 0%

profile of v1, /device:TPU:0, one launch (start us, length us, event | category | flops | bytes accessed | tf_op | source)
XLA Modules:
  0.0 84.1 jit_solution(15235638892748832277)
XLA Ops:
  0.6 0.0 copy-start.12
  0.6 0.0 copy-start.13
  0.7 0.6 copy-done.12
  1.3 0.0 copy-done.13
  1.3 0.1 add_bitcast_fusion.refs_0_
  1.4 5.0 %collective-permute-start.2 = (s32[1,8]{1,0:T(1,128)S(1)}, s32[1,8]{1,0:T(1,128)S(1)}, u32[]{:S(2)}, u32[]{:S(2)}) collective-permute-start(s32[1,8]{1,0:T(1,128)S(1)} %add_bitcast_fusion.refs_0_), channel_id=1, source_target_pairs={{0,3},{1,2},{2,1},{3,0},{4,7},{5,6},{6,5},{7,4},{8,11},{9,10},{10,... | collective-permute-start | bytes 104 | tf_op jit(solution)/shard_map/ppermute | solution.py:334
  6.4 0.0 collective-permute-start.1
  6.4 0.6 collective-permute-start
  7.1 0.9 %collective-permute-done.2.refs_3_ = s32[1,8]{1,0:T(1,128)S(1)} collective-permute-done((s32[1,8]{1,0:T(1,128)S(1)}, s32[1,8]{1,0:T(1,128)S(1)}, u32[]{:S(2)}, u32[]{:S(2)}) %collective-permute-start.2) | collective-permute-done | bytes 64 | tf_op jit(solution)/shard_map/ppermute | solution.py:334
  7.9 2.9 %collective-permute-done.1.refs_2_ = s32[1,8]{1,0:T(1,128)S(1)} collective-permute-done((s32[1,8]{1,0:T(1,128)S(1)}, s32[1,8]{1,0:T(1,128)S(1)}, u32[]{:S(2)}, u32[]{:S(2)}) %collective-permute-start.1) | collective-permute-done | bytes 64 | tf_op jit(solution)/shard_map/ppermute | solution.py:334
  10.9 0.0 collective-permute-done.refs_1_
  10.9 0.0 copy-start
  10.9 1.0 %copy-done = bf16[2048,128]{1,0:T(8,128)(2,1)S(1)} copy-done((bf16[2048,128]{1,0:T(8,128)(2,1)S(1)}, bf16[2048,128]{1,0:T(8,128)(2,1)}, u32[]{:S(2)}) %copy-start) | copy-done | bytes 524312
  11.9 1.4 %shard_map.206 = (bf16[128,128]{1,0:T(8,128)(2,1)S(1)}, bf16[128,128]{1,0:T(8,128)(2,1)S(1)}, bf16[128,128]{1,0:T(8,128)(2,1)S(1)}, bf16[128,128]{1,0:T(8,128)(2,1)S(1)}, s32[4]{0:T(128)S(1)}) custom-call(s32[1]{0:T(128)} %bitcast.2.me_ref.place_ref, s32[1,8]{1,0:T(1,128)S(1)} %add_bitcast_fusion.refs_0_, s32[1,8]{1,0:T(1,128)S(1)} %collective-permute-done.refs_1_, ...), custom_call_target="tpu_custom_call" | custom-call | bytes 1048576 | tf_op jit(solution)/shard_map/pallas_call | solution.py:272
  13.3 0.1 collective-permute-start.5
  13.4 2.1 %collective-permute-start.6 = (bf16[128,128]{1,0:T(8,128)(2,1)S(1)}, bf16[128,128]{1,0:T(8,128)(2,1)S(1)}, u32[]{:S(2)}, u32[]{:S(2)}) collective-permute-start(bf16[128,128]{1,0:T(8,128)(2,1)S(1)} %get-tuple-element.34), channel_id=1, source_target_pairs={{0,2},{1,3},{2,0},{3,1},{4,6},{5,7},{6,4},{7,5},{8,10},{9,11},{10,... | collective-permute-start | bytes 98312 | tf_op jit(solution)/shard_map/ppermute | solution.py:334
  15.5 2.3 %collective-permute-start.7 = (bf16[128,128]{1,0:T(8,128)(2,1)S(1)}, bf16[128,128]{1,0:T(8,128)(2,1)S(1)}, u32[]{:S(2)}, u32[]{:S(2)}) collective-permute-start(bf16[128,128]{1,0:T(8,128)(2,1)S(1)} %get-tuple-element.35), channel_id=1, source_target_pairs={{0,3},{1,2},{2,1},{3,0},{4,7},{5,6},{6,5},{7,4},{8,11},{9,10},{10,... | collective-permute-start | bytes 98312 | tf_op jit(solution)/shard_map/ppermute | solution.py:334
  17.8 0.1 pad_add_fusion.3.place_ref
  18.5 0.0 collective-permute-done.5.refs_1_
  18.5 0.0 collective-permute-done.6.refs_2_
  18.5 2.7 %collective-permute-done.7.refs_3_ = bf16[128,128]{1,0:T(8,128)(2,1)S(1)} collective-permute-done((bf16[128,128]{1,0:T(8,128)(2,1)S(1)}, bf16[128,128]{1,0:T(8,128)(2,1)S(1)}, u32[]{:S(2)}, u32[]{:S(2)}) %collective-permute-start.7) | collective-permute-done | bytes 32800 | tf_op jit(solution)/shard_map/ppermute | solution.py:334
  21.2 0.0 copy-start.7
  21.2 0.0 copy-done.1
  21.2 0.6 copy-done.8
  21.9 0.0 copy-done.9
  21.9 0.0 copy-done.10
  21.9 0.0 copy-done.11
  21.9 0.0 copy-done.7
  21.9 1.0 %copy-done.2 = bf16[512,512]{1,0:T(8,128)(2,1)S(1)} copy-done((bf16[512,512]{1,0:T(8,128)(2,1)S(1)}, bf16[512,512]{1,0:T(8,128)(2,1)}, u32[]{:S(2)}) %copy-start.2) | copy-done | bytes 524312
  23.0 1.0 %copy-done.3 = bf16[512,512]{1,0:T(8,128)(2,1)S(1)} copy-done((bf16[512,512]{1,0:T(8,128)(2,1)S(1)}, bf16[512,512]{1,0:T(8,128)(2,1)}, u32[]{:S(2)}) %copy-start.3) | copy-done | bytes 524312
  24.0 0.9 %copy-done.4 = bf16[512,128]{1,0:T(8,128)(2,1)S(1)} copy-done((bf16[512,128]{1,0:T(8,128)(2,1)S(1)}, bf16[512,128]{1,0:T(8,128)(2,1)}, u32[]{:S(2)}) %copy-start.4) | copy-done | bytes 131096
  24.9 0.9 %copy-done.5 = bf16[128,512]{1,0:T(8,128)(2,1)S(1)} copy-done((bf16[128,512]{1,0:T(8,128)(2,1)S(1)}, bf16[128,512]{1,0:T(8,128)(2,1)}, u32[]{:S(2)}) %copy-start.5) | copy-done | bytes 131096
  25.8 0.9 %copy-done.6 = bf16[128,512]{1,0:T(8,128)(2,1)S(1)} copy-done((bf16[128,512]{1,0:T(8,128)(2,1)S(1)}, bf16[128,512]{1,0:T(8,128)(2,1)}, u32[]{:S(2)}) %copy-start.6) | copy-done | bytes 131096
  26.7 6.3 %shard_map.207 = (bf16[8,80,512]{2,1,0:T(8,128)(2,1)S(1)}, bf16[8,80,512]{2,1,0:T(8,128)(2,1)S(1)}, bf16[4,32,512]{2,1,0:T(8,128)(2,1)S(1)}, bf16[16,512]{1,0:T(8,128)(2,1)S(1)}) custom-call(s32[2]{0:T(128)S(1)} %pad_add_fusion.3.place_ref, s32[4]{0:T(128)S(1)} %bitcast.26, s32[1]{0:T(128)S(6)} %copy.23.count_ref, ...), custom_call_target="tpu_custom_call" | custom-call | flops 2147483648 | bytes 1048576 | tf_op jit(solution)/shard_map/pallas_call | solution.py:272
  33.0 0.1 collective-permute-start.8
  33.1 2.1 %collective-permute-done.8.got_ref = bf16[8,80,512]{2,1,0:T(8,128)(2,1)S(1)} collective-permute-done((bf16[8,80,512]{2,1,0:T(8,128)(2,1)S(1)}, bf16[8,80,512]{2,1,0:T(8,128)(2,1)S(1)}, u32[]{:S(2)}, u32[]{:S(2)}) %collective-permute-start.8) | collective-permute-done | bytes 655392 | tf_op jit(solution)/shard_map/ppermute | solution.py:334
  35.2 0.2 shard_map.208
  35.3 1.6 %collective-permute-start.9 = (bf16[4,80,512]{2,1,0:T(8,128)(2,1)S(1)}, bf16[4,80,512]{2,1,0:T(8,128)(2,1)S(1)}, u32[]{:S(2)}, u32[]{:S(2)}) collective-permute-start(bf16[4,80,512]{2,1,0:T(8,128)(2,1)S(1)} %get-tuple-element.39), channel_id=1, source_target_pairs={{0,8},{4,12},{8,0},{12,4},{1,9},{5,13},{9,1},{13,5},{2,10},{6,14},... | collective-permute-start | bytes 983048 | tf_op jit(solution)/shard_map/ppermute | solution.py:334
  36.9 8.3 %collective-permute-done.9.got_ref = bf16[4,80,512]{2,1,0:T(8,128)(2,1)S(1)} collective-permute-done((bf16[4,80,512]{2,1,0:T(8,128)(2,1)S(1)}, bf16[4,80,512]{2,1,0:T(8,128)(2,1)S(1)}, u32[]{:S(2)}, u32[]{:S(2)}) %collective-permute-start.9) | collective-permute-done | bytes 327712 | tf_op jit(solution)/shard_map/ppermute | solution.py:334
  45.1 0.1 shard_map.209
  45.2 0.2 collective-permute-start.10
  45.4 2.7 %collective-permute-start.11 = (bf16[128,512]{1,0:T(8,128)(2,1)S(1)}, bf16[128,512]{1,0:T(8,128)(2,1)S(1)}, u32[]{:S(2)}, u32[]{:S(2)}) collective-permute-start(bf16[128,512]{1,0:T(8,128)(2,1)S(1)} %get-tuple-element.44), channel_id=1, source_target_pairs={{0,2},{1,3},{2,0},{3,1},{4,6},{5,7},{6,4},{7,5},{8,10},{9,11},{10,... | collective-permute-start | bytes 393224 | tf_op jit(solution)/shard_map/ppermute | solution.py:334
  48.2 1.5 %collective-permute-start.12 = (bf16[128,512]{1,0:T(8,128)(2,1)S(1)}, bf16[128,512]{1,0:T(8,128)(2,1)S(1)}, u32[]{:S(2)}, u32[]{:S(2)}) collective-permute-start(bf16[128,512]{1,0:T(8,128)(2,1)S(1)} %get-tuple-element.45), channel_id=1, source_target_pairs={{0,3},{1,2},{2,1},{3,0},{4,7},{5,6},{6,5},{7,4},{8,11},{9,10},{10,... | collective-permute-start | bytes 393224 | tf_op jit(solution)/shard_map/ppermute | solution.py:334
  49.7 2.2 %collective-permute-done.10.refs_1_.refs_5_ = bf16[128,512]{1,0:T(8,128)(2,1)S(1)} collective-permute-done((bf16[128,512]{1,0:T(8,128)(2,1)S(1)}, bf16[128,512]{1,0:T(8,128)(2,1)S(1)}, u32[]{:S(2)}, u32[]{:S(2)}) %collective-permute-start.10) | collective-permute-done | bytes 131104 | tf_op jit(solution)/shard_map/ppermute | solution.py:334
  51.9 6.2 %collective-permute-done.11.refs_2_.refs_6_ = bf16[128,512]{1,0:T(8,128)(2,1)S(1)} collective-permute-done((bf16[128,512]{1,0:T(8,128)(2,1)S(1)}, bf16[128,512]{1,0:T(8,128)(2,1)S(1)}, u32[]{:S(2)}, u32[]{:S(2)}) %collective-permute-start.11) | collective-permute-done | bytes 131104 | tf_op jit(solution)/shard_map/ppermute | solution.py:334
  58.1 0.0 collective-permute-done.12.refs_3_.refs_7_
  58.1 2.3 %collective-permute-start.15 = (bf16[80,512]{1,0:T(8,128)(2,1)S(1)}, bf16[80,512]{1,0:T(8,128)(2,1)S(1)}, u32[]{:S(2)}, u32[]{:S(2)}) collective-permute-start(bf16[80,512]{1,0:T(8,128)(2,1)S(1)} %shard_map.210.refs_0_), channel_id=1, source_target_pairs={{0,3},{1,2},{2,1},{3,0},{4,7},{5,6},{6,5},{7,4},{8,11},{9,10},{10,... | collective-permute-start | bytes 245768 | tf_op jit(solution)/shard_map/ppermute | solution.py:334
  60.4 1.5 %collective-permute-start.14 = (bf16[80,512]{1,0:T(8,128)(2,1)S(1)}, bf16[80,512]{1,0:T(8,128)(2,1)S(1)}, u32[]{:S(2)}, u32[]{:S(2)}) collective-permute-start(bf16[80,512]{1,0:T(8,128)(2,1)S(1)} %shard_map.210.refs_0_), channel_id=1, source_target_pairs={{0,2},{1,3},{2,0},{3,1},{4,6},{5,7},{6,4},{7,5},{8,10},{9,11},{10,... | collective-permute-start | bytes 245768 | tf_op jit(solution)/shard_map/ppermute | solution.py:334
  61.9 0.6 collective-permute-start.13
  62.6 2.7 %collective-permute-done.15.refs_3_ = bf16[80,512]{1,0:T(8,128)(2,1)S(1)} collective-permute-done((bf16[80,512]{1,0:T(8,128)(2,1)S(1)}, bf16[80,512]{1,0:T(8,128)(2,1)S(1)}, u32[]{:S(2)}, u32[]{:S(2)}) %collective-permute-start.15) | collective-permute-done | bytes 81952 | tf_op jit(solution)/shard_map/ppermute | solution.py:334
  65.2 2.1 %collective-permute-done.14.refs_2_ = bf16[80,512]{1,0:T(8,128)(2,1)S(1)} collective-permute-done((bf16[80,512]{1,0:T(8,128)(2,1)S(1)}, bf16[80,512]{1,0:T(8,128)(2,1)S(1)}, u32[]{:S(2)}, u32[]{:S(2)}) %collective-permute-start.14) | collective-permute-done | bytes 81952 | tf_op jit(solution)/shard_map/ppermute | solution.py:334
  67.3 0.0 collective-permute-done.13.refs_1_
  67.3 1.6 %collective-permute-start.16 = (bf16[4,128,512]{2,1,0:T(8,128)(2,1)S(1)}, bf16[4,128,512]{2,1,0:T(8,128)(2,1)S(1)}, u32[]{:S(2)}, u32[]{:S(2)}) collective-permute-start(bf16[4,128,512]{2,1,0:T(8,128)(2,1)S(1)} %shard_map.211.own), channel_id=1, source_target_pairs={{0,8},{4,12},{8,0},{12,4},{1,9},{5,13},{9,1},{13,5},{2,10},{6,14},... | collective-permute-start | bytes 1572872 | tf_op jit(solution)/shard_map/ppermute | solution.py:334
  68.9 0.0 collective-permute-start.17
  68.9 8.0 %collective-permute-done.16.over_x = bf16[4,128,512]{2,1,0:T(8,128)(2,1)S(1)} collective-permute-done((bf16[4,128,512]{2,1,0:T(8,128)(2,1)S(1)}, bf16[4,128,512]{2,1,0:T(8,128)(2,1)S(1)}, u32[]{:S(2)}, u32[]{:S(2)}) %collective-permute-start.16) | collective-permute-done | bytes 524320 | tf_op jit(solution)/shard_map/ppermute | solution.py:334
  76.9 0.0 collective-permute-start.18
  76.9 0.1 pad_add_fusion.2.place_ref
  77.0 1.5 %collective-permute-start.3 = (s32[1,4]{1,0:T(1,128)S(1)}, s32[1,4]{1,0:T(1,128)S(1)}, u32[]{:S(2)}, u32[]{:S(2)}) collective-permute-start(s32[1,4]{1,0:T(1,128)S(1)} %bitcast.17), channel_id=1, source_target_pairs={{0,8},{4,12},{8,0},{12,4},{1,9},{5,13},{9,1},{13,5},{2,10},{6,14},... | collective-permute-start | bytes 56 | tf_op jit(solution)/shard_map/ppermute | solution.py:334
  78.5 2.0 %collective-permute-done.3 = s32[1,4]{1,0:T(1,128)S(1)} collective-permute-done((s32[1,4]{1,0:T(1,128)S(1)}, s32[1,4]{1,0:T(1,128)S(1)}, u32[]{:S(2)}, u32[]{:S(2)}) %collective-permute-start.3) | collective-permute-done | bytes 48 | tf_op jit(solution)/shard_map/ppermute | solution.py:334
  80.6 0.1 collective-permute-start.4
  80.6 1.1 %collective-permute-done.4 = s32[2,4]{1,0:T(2,128)S(1)} collective-permute-done((s32[2,4]{1,0:T(2,128)S(1)}, s32[2,4]{1,0:T(2,128)S(1)}, u32[]{:S(2)}, u32[]{:S(2)}) %collective-permute-start.4) | collective-permute-done | bytes 64 | tf_op jit(solution)/shard_map/ppermute | solution.py:334
  81.8 0.0 collective-permute-done.17.over_core
  81.8 0.0 collective-permute-done.18.over_both
  81.8 2.3 %shard_map.212 = (f32[16,128,128]{2,1,0:T(8,128)}, bf16[128,512]{1,0:T(8,128)(2,1)}, f32[1,512]{1,0:T(1,128)}, bf16[128,512]{1,0:T(8,128)(2,1)}, bf16[512,512]{1...) custom-call(s32[3]{0:T(128)S(1)} %pad_add_fusion.2.place_ref, ...), custom_call_target="tpu_custom_call" | custom-call | bytes 1048576 | tf_op jit(solution)/shard_map/pallas_call | solution.py:272
  (14 shorter events, 0.1 us)
Async XLA Ops:
  0.6 0.7 copy-start.12
  0.6 0.7 copy-start.13
  1.4 6.6 %collective-permute-start.2 = (s32[1,8]{1,0:T(1,128)S(1)}, s32[1,8]{1,0:T(1,128)S(1)}, u32[]{:S(2)}, u32[]{:S(2)}) collective-permute-start(s32[1,8]{1,0:T(1,128)S(1)} %add_bitcast_fusion.refs_0_), channel_id=1, source_target_pairs={{0,3},{1,2},{2,1},{3,0},{4,7},{5,6},{6,5},{7,4},{8,11},{9,10},{10,... | collective-permute-start | bytes 104 | tf_op jit(solution)/shard_map/ppermute | solution.py:334
  6.4 4.4 %collective-permute-start.1 = (s32[1,8]{1,0:T(1,128)S(1)}, s32[1,8]{1,0:T(1,128)S(1)}, u32[]{:S(2)}, u32[]{:S(2)}) collective-permute-start(s32[1,8]{1,0:T(1,128)S(1)} %add_bitcast_fusion.refs_0_), channel_id=1, source_target_pairs={{0,2},{1,3},{2,0},{3,1},{4,6},{5,7},{6,4},{7,5},{8,10},{9,11},{10,... | collective-permute-start | bytes 104 | tf_op jit(solution)/shard_map/ppermute | solution.py:334
  6.4 4.4 %collective-permute-start = (s32[1,8]{1,0:T(1,128)S(1)}, s32[1,8]{1,0:T(1,128)S(1)}, u32[]{:S(2)}, u32[]{:S(2)}) collective-permute-start(s32[1,8]{1,0:T(1,128)S(1)} %add_bitcast_fusion.refs_0_), channel_id=1, source_target_pairs={{0,1},{1,0},{2,3},{3,2},{4,5},{5,4},{6,7},{7,6},{8,9},{9,8},{10,11... | collective-permute-start | bytes 104 | tf_op jit(solution)/shard_map/ppermute | solution.py:334
  10.9 1.0 %copy-start = (bf16[2048,128]{1,0:T(8,128)(2,1)S(1)}, bf16[2048,128]{1,0:T(8,128)(2,1)}, u32[]{:S(2)}) copy-start(bf16[2048,128]{1,0:T(8,128)(2,1)} %refs_4_.1) | copy-start | bytes 1572868
  11.9 9.3 %copy-start.1 = (bf16[512,512]{1,0:T(8,128)(2,1)S(1)}, bf16[512,512]{1,0:T(8,128)(2,1)}, u32[]{:S(2)}) copy-start(bf16[512,512]{1,0:T(8,128)(2,1)} %refs_7_.1) | copy-start | bytes 1572868
  13.3 5.2 %collective-permute-start.5 = (bf16[128,128]{1,0:T(8,128)(2,1)S(1)}, bf16[128,128]{1,0:T(8,128)(2,1)S(1)}, u32[]{:S(2)}, u32[]{:S(2)}) collective-permute-start(bf16[128,128]{1,0:T(8,128)(2,1)S(1)} %get-tuple-element.33), channel_id=1, source_target_pairs={{0,1},{1,0},{2,3},{3,2},{4,5},{5,4},{6,7},{7,6},{8,9},{9,8},{10,11... | collective-permute-start | bytes 98312 | tf_op jit(solution)/shard_map/ppermute | solution.py:334
  13.4 5.1 %collective-permute-start.6 = (bf16[128,128]{1,0:T(8,128)(2,1)S(1)}, bf16[128,128]{1,0:T(8,128)(2,1)S(1)}, u32[]{:S(2)}, u32[]{:S(2)}) collective-permute-start(bf16[128,128]{1,0:T(8,128)(2,1)S(1)} %get-tuple-element.34), channel_id=1, source_target_pairs={{0,2},{1,3},{2,0},{3,1},{4,6},{5,7},{6,4},{7,5},{8,10},{9,11},{10,... | collective-permute-start | bytes 98312 | tf_op jit(solution)/shard_map/ppermute | solution.py:334
  15.5 5.7 %collective-permute-start.7 = (bf16[128,128]{1,0:T(8,128)(2,1)S(1)}, bf16[128,128]{1,0:T(8,128)(2,1)S(1)}, u32[]{:S(2)}, u32[]{:S(2)}) collective-permute-start(bf16[128,128]{1,0:T(8,128)(2,1)S(1)} %get-tuple-element.35), channel_id=1, source_target_pairs={{0,3},{1,2},{2,1},{3,0},{4,7},{5,6},{6,5},{7,4},{8,11},{9,10},{10,... | collective-permute-start | bytes 98312 | tf_op jit(solution)/shard_map/ppermute | solution.py:334
  21.2 0.7 copy-start.8
  21.2 0.7 copy-start.9
  21.2 0.7 copy-start.10
  21.2 0.7 copy-start.11
  21.2 0.7 copy-start.7
  21.9 1.0 %copy-start.2 = (bf16[512,512]{1,0:T(8,128)(2,1)S(1)}, bf16[512,512]{1,0:T(8,128)(2,1)}, u32[]{:S(2)}) copy-start(bf16[512,512]{1,0:T(8,128)(2,1)} %refs_11_.1) | copy-start | bytes 1572868
  23.0 1.0 %copy-start.3 = (bf16[512,512]{1,0:T(8,128)(2,1)S(1)}, bf16[512,512]{1,0:T(8,128)(2,1)}, u32[]{:S(2)}) copy-start(bf16[512,512]{1,0:T(8,128)(2,1)} %refs_13_.1) | copy-start | bytes 1572868
  24.0 0.9 %copy-start.4 = (bf16[512,128]{1,0:T(8,128)(2,1)S(1)}, bf16[512,128]{1,0:T(8,128)(2,1)}, u32[]{:S(2)}) copy-start(bf16[512,128]{1,0:T(8,128)(2,1)} %refs_6_.1) | copy-start | bytes 393220
  24.9 0.9 %copy-start.5 = (bf16[128,512]{1,0:T(8,128)(2,1)S(1)}, bf16[128,512]{1,0:T(8,128)(2,1)}, u32[]{:S(2)}) copy-start(bf16[128,512]{1,0:T(8,128)(2,1)} %refs_8_.1) | copy-start | bytes 393220
  25.8 0.9 %copy-start.6 = (bf16[128,512]{1,0:T(8,128)(2,1)S(1)}, bf16[128,512]{1,0:T(8,128)(2,1)}, u32[]{:S(2)}) copy-start(bf16[128,512]{1,0:T(8,128)(2,1)} %refs_10_.1) | copy-start | bytes 393220
  33.0 2.2 %collective-permute-start.8 = (bf16[8,80,512]{2,1,0:T(8,128)(2,1)S(1)}, bf16[8,80,512]{2,1,0:T(8,128)(2,1)S(1)}, u32[]{:S(2)}, u32[]{:S(2)}) collective-permute-start(bf16[8,80,512]{2,1,0:T(8,128)(2,1)S(1)} %get-tuple-element.37), channel_id=1, source_target_pairs={{0,4},{4,0},{8,12},{12,8},{1,5},{5,1},{9,13},{13,9},{2,6},{6,2},{1... | collective-permute-start | bytes 1966088 | tf_op jit(solution)/shard_map/ppermute | solution.py:334
  35.3 9.8 %collective-permute-start.9 = (bf16[4,80,512]{2,1,0:T(8,128)(2,1)S(1)}, bf16[4,80,512]{2,1,0:T(8,128)(2,1)S(1)}, u32[]{:S(2)}, u32[]{:S(2)}) collective-permute-start(bf16[4,80,512]{2,1,0:T(8,128)(2,1)S(1)} %get-tuple-element.39), channel_id=1, source_target_pairs={{0,8},{4,12},{8,0},{12,4},{1,9},{5,13},{9,1},{13,5},{2,10},{6,14},... | collective-permute-start | bytes 983048 | tf_op jit(solution)/shard_map/ppermute | solution.py:334
  45.2 6.6 %collective-permute-start.10 = (bf16[128,512]{1,0:T(8,128)(2,1)S(1)}, bf16[128,512]{1,0:T(8,128)(2,1)S(1)}, u32[]{:S(2)}, u32[]{:S(2)}) collective-permute-start(bf16[128,512]{1,0:T(8,128)(2,1)S(1)} %get-tuple-element.43), channel_id=1, source_target_pairs={{0,1},{1,0},{2,3},{3,2},{4,5},{5,4},{6,7},{7,6},{8,9},{9,8},{10,11... | collective-permute-start | bytes 393224 | tf_op jit(solution)/shard_map/ppermute | solution.py:334
  45.4 12.6 %collective-permute-start.11 = (bf16[128,512]{1,0:T(8,128)(2,1)S(1)}, bf16[128,512]{1,0:T(8,128)(2,1)S(1)}, u32[]{:S(2)}, u32[]{:S(2)}) collective-permute-start(bf16[128,512]{1,0:T(8,128)(2,1)S(1)} %get-tuple-element.44), channel_id=1, source_target_pairs={{0,2},{1,3},{2,0},{3,1},{4,6},{5,7},{6,4},{7,5},{8,10},{9,11},{10,... | collective-permute-start | bytes 393224 | tf_op jit(solution)/shard_map/ppermute | solution.py:334
  48.2 9.9 %collective-permute-start.12 = (bf16[128,512]{1,0:T(8,128)(2,1)S(1)}, bf16[128,512]{1,0:T(8,128)(2,1)S(1)}, u32[]{:S(2)}, u32[]{:S(2)}) collective-permute-start(bf16[128,512]{1,0:T(8,128)(2,1)S(1)} %get-tuple-element.45), channel_id=1, source_target_pairs={{0,3},{1,2},{2,1},{3,0},{4,7},{5,6},{6,5},{7,4},{8,11},{9,10},{10,... | collective-permute-start | bytes 393224 | tf_op jit(solution)/shard_map/ppermute | solution.py:334
  58.1 7.1 %collective-permute-start.15 = (bf16[80,512]{1,0:T(8,128)(2,1)S(1)}, bf16[80,512]{1,0:T(8,128)(2,1)S(1)}, u32[]{:S(2)}, u32[]{:S(2)}) collective-permute-start(bf16[80,512]{1,0:T(8,128)(2,1)S(1)} %shard_map.210.refs_0_), channel_id=1, source_target_pairs={{0,3},{1,2},{2,1},{3,0},{4,7},{5,6},{6,5},{7,4},{8,11},{9,10},{10,... | collective-permute-start | bytes 245768 | tf_op jit(solution)/shard_map/ppermute | solution.py:334
  60.4 6.9 %collective-permute-start.14 = (bf16[80,512]{1,0:T(8,128)(2,1)S(1)}, bf16[80,512]{1,0:T(8,128)(2,1)S(1)}, u32[]{:S(2)}, u32[]{:S(2)}) collective-permute-start(bf16[80,512]{1,0:T(8,128)(2,1)S(1)} %shard_map.210.refs_0_), channel_id=1, source_target_pairs={{0,2},{1,3},{2,0},{3,1},{4,6},{5,7},{6,4},{7,5},{8,10},{9,11},{10,... | collective-permute-start | bytes 245768 | tf_op jit(solution)/shard_map/ppermute | solution.py:334
  61.9 5.4 %collective-permute-start.13 = (bf16[80,512]{1,0:T(8,128)(2,1)S(1)}, bf16[80,512]{1,0:T(8,128)(2,1)S(1)}, u32[]{:S(2)}, u32[]{:S(2)}) collective-permute-start(bf16[80,512]{1,0:T(8,128)(2,1)S(1)} %shard_map.210.refs_0_), channel_id=1, source_target_pairs={{0,1},{1,0},{2,3},{3,2},{4,5},{5,4},{6,7},{7,6},{8,9},{9,8},{10,11... | collective-permute-start | bytes 245768 | tf_op jit(solution)/shard_map/ppermute | solution.py:334
  67.3 9.6 %collective-permute-start.16 = (bf16[4,128,512]{2,1,0:T(8,128)(2,1)S(1)}, bf16[4,128,512]{2,1,0:T(8,128)(2,1)S(1)}, u32[]{:S(2)}, u32[]{:S(2)}) collective-permute-start(bf16[4,128,512]{2,1,0:T(8,128)(2,1)S(1)} %shard_map.211.own), channel_id=1, source_target_pairs={{0,8},{4,12},{8,0},{12,4},{1,9},{5,13},{9,1},{13,5},{2,10},{6,14},... | collective-permute-start | bytes 1572872 | tf_op jit(solution)/shard_map/ppermute | solution.py:334
  68.9 12.9 %collective-permute-start.17 = (bf16[4,128,512]{2,1,0:T(8,128)(2,1)S(1)}, bf16[4,128,512]{2,1,0:T(8,128)(2,1)S(1)}, u32[]{:S(2)}, u32[]{:S(2)}) collective-permute-start(bf16[4,128,512]{2,1,0:T(8,128)(2,1)S(1)} %shard_map.211.own), channel_id=1, source_target_pairs={{0,4},{4,0},{8,12},{12,8},{1,5},{5,1},{9,13},{13,9},{2,6},{6,2},{1... | collective-permute-start | bytes 1572872 | tf_op jit(solution)/shard_map/ppermute | solution.py:334
  76.9 4.9 %collective-permute-start.18 = (bf16[4,128,512]{2,1,0:T(8,128)(2,1)S(1)}, bf16[4,128,512]{2,1,0:T(8,128)(2,1)S(1)}, u32[]{:S(2)}, u32[]{:S(2)}) collective-permute-start(bf16[4,128,512]{2,1,0:T(8,128)(2,1)S(1)} %collective-permute-done.16.over_x), channel_id=1, source_target_pairs={{0,4},{4,0},{8,12},{12,8},{1,5},{5,1},{9,13},{13,9},{2,6},{6,2},{1... | collective-permute-start | bytes 1572872 | tf_op jit(solution)/shard_map/ppermute | solution.py:334
  77.0 3.5 %collective-permute-start.3 = (s32[1,4]{1,0:T(1,128)S(1)}, s32[1,4]{1,0:T(1,128)S(1)}, u32[]{:S(2)}, u32[]{:S(2)}) collective-permute-start(s32[1,4]{1,0:T(1,128)S(1)} %bitcast.17), channel_id=1, source_target_pairs={{0,8},{4,12},{8,0},{12,4},{1,9},{5,13},{9,1},{13,5},{2,10},{6,14},... | collective-permute-start | bytes 56 | tf_op jit(solution)/shard_map/ppermute | solution.py:334
  80.6 1.2 %collective-permute-start.4 = (s32[2,4]{1,0:T(2,128)S(1)}, s32[2,4]{1,0:T(2,128)S(1)}, u32[]{:S(2)}, u32[]{:S(2)}) collective-permute-start(s32[2,4]{1,0:T(2,128)S(1)} %pad_add_fusion.1), channel_id=1, source_target_pairs={{0,4},{4,0},{8,12},{12,8},{1,5},{5,1},{9,13},{13,9},{2,6},{6,2},{1... | collective-permute-start | bytes 104 | tf_op jit(solution)/shard_map/ppermute | solution.py:334

commit v2 on v1

--- a/solution.py
+++ b/solution.py
@@ -12,9 +12,9 @@
 VMEM = pl.BlockSpec(memory_space=pltpu.VMEM)
 SMEM = pl.BlockSpec(memory_space=pltpu.SMEM)
 ANY = pl.BlockSpec(memory_space=pl.ANY)
+HBM = pl.BlockSpec(memory_space=pltpu.HBM)
 GROUP = 4
-LIMIT = 48 * 1024 * 1024
-PARAMS = pltpu.CompilerParams(vmem_limit_bytes=LIMIT)
+LIMIT = 16 * 1024 * 1024
 
 
 def nn(a, b):
@@ -49,9 +49,9 @@
 
 
 def serve_kernel(me_ref, *refs):
-    count = (len(refs) - 3) // 2
-    requests, surface, blocks = refs[:count], refs[count], refs[count + 1 : 2 * count + 1]
-    ids_ref, sems = refs[2 * count + 1], refs[2 * count + 2]
+    count = (len(refs) - 4) // 2
+    requests, surface, blocks = refs[:count], refs[count], refs[count + 2 : 2 * count + 2]
+    ids_ref, sems = refs[2 * count + 2], refs[2 * count + 3]
     rows = blocks[0].shape[0]
     me = me_ref[0]
     copies = []
@@ -69,38 +69,53 @@
         copy.wait()
 
 
-def main_kernel(n_pieces, place_ref, owner_ref, count_ref, *refs):
+def fill(out, surf_ref, bias, m):
+    rows = surf_ref.shape[1]
+    out[m, 0:rows, :] = surf_ref[m]
+    out[m, rows:, :] = bias
+
+
+def early_kernel(block_rows, count_ref, cell_ref, b1_ref, *refs):
+    far, near = refs[:6], refs[6:11]
+    hot_ref, scale_ref, base_ref, win_ref, sems = refs[11:]
+    near = (win_ref,) + tuple(near)
+    loads = [pltpu.make_async_copy(a, b, sems.at[i]) for i, (a, b) in enumerate(zip(far, near))]
+    for load in loads:
+        load.start()
+    groups, cells, entries = hot_ref.shape
+    channels = scale_ref.shape[1]
+    live_count = count_ref[0]
+    scale_ref[...] = jnp.zeros_like(scale_ref)
+
+    def group(g):
+        lane = lax.broadcasted_iota(jnp.int32, (1, entries), 1) // block_rows + g * GROUP
+        named = jnp.where(lane < live_count, cell_ref[g], -1)
+        hot = (lax.broadcasted_iota(jnp.int32, (cells, entries), 0) == named).astype(BF16)
+        hot_ref[g] = hot
+        scale_ref[...] += nn(hot, jnp.ones((entries, channels), BF16))
+
+    loop(groups, group)
+    scale_ref[...] = 1.0 / jnp.maximum(scale_ref[...], 1.0)
+    loads[0].wait()
+    loads[1].wait()
+    base_ref[...] = nn(near[1][...], win_ref[...]) + b1_ref[...]
+    for load in loads[2:]:
+        load.wait()
+
+
+def main_kernel(n_pieces, n_out, place_ref, owner_ref, *refs):
     pieces = refs[:n_pieces]
-    (
-        row_ref,
-        cell_ref,
-        vol_ref,
-        cot_ref,
-        wenc_ref,
-        benc_ref,
-        win_ref,
-        wmid_ref,
-        b1_ref,
-        wout_ref,
-        b2_ref,
-        keep_ref,
-        send_ref,
-        surf_ref,
-        bias_ref,
-        blocks,
-        gathered_ref,
-        slope_ref,
-        hot_ref,
-        total_ref,
-        count_sum,
-        wenc_sum,
-        benc_sum,
-    ) = refs[n_pieces:]
+    row_ref, benc_ref, b2_ref = refs[n_pieces : n_pieces + 3]
+    wenc_ref, vol_ref, wmid_ref, wout_ref, cot_ref = refs[n_pieces + 3 : n_pieces + 8]
+    hot_ref, scale_ref, base_ref, keep_ref, send_ref = refs[n_pieces + 8 : n_pieces + 13]
+    surf_refs = refs[n_pieces + 13 : n_pieces + 13 + n_out]
+    blocks, gathered_ref, slope_ref, total_ref, wenc_sum, benc_sum, surf_ref = refs[
+        n_pieces + 13 + n_out :
+    ]
     half, mask = place_ref[0], place_ref[1]
     groups = row_ref.shape[0]
     cells, hidden = cot_ref.shape
     block_rows, channels = blocks.shape[1:]
-    entries = GROUP * block_rows
     base = 0
     for piece in pieces:
         if len(piece.shape) == 2:
@@ -108,7 +123,6 @@
             base += 1
         else:
             blocks[...] = piece[...]
-    live_count = count_ref[0]
 
     def row_hot(g, k):
         rows = lax.broadcasted_iota(jnp.int32, (block_rows, block_rows), 0)
@@ -116,13 +130,8 @@
         return (rows == named).astype(BF16)
 
     total_ref[...] = jnp.zeros_like(total_ref)
-    count_sum[...] = jnp.zeros_like(count_sum)
 
     def encode(g):
-        lane = lax.broadcasted_iota(jnp.int32, (1, entries), 1) // block_rows + g * GROUP
-        named = jnp.where(lane < live_count, cell_ref[g], -1)
-        hot = (lax.broadcasted_iota(jnp.int32, (cells, entries), 0) == named).astype(BF16)
-        hot_ref[g] = hot
         for k in range(GROUP):
             block = blocks[owner_ref[g * GROUP + k] ^ mask]
             gathered_ref[g, k * block_rows : (k + 1) * block_rows, :] = tn(
@@ -130,14 +139,12 @@
             ).astype(BF16)
         act, slope = gelu_pair(nn(gathered_ref[g], wenc_ref[...]) + benc_ref[...])
         slope_ref[g] = slope
-        total_ref[...] += nn(hot, act.astype(BF16))
-        count_sum[...] += nn(hot, jnp.ones((entries, channels), BF16))
+        total_ref[...] += nn(hot_ref[g], act.astype(BF16))
 
     loop(groups, encode)
-    scale = 1.0 / jnp.maximum(count_sum[...], 1.0)
-    scale = jnp.concatenate([scale] * (hidden // channels), axis=1)
+    scale = jnp.concatenate([scale_ref[...]] * (hidden // channels), axis=1)
     encoded = (total_ref[...] * scale).astype(BF16)
-    pre_first = nn(vol_ref[...], win_ref[...]) + nn(encoded, wmid_ref[...]) + b1_ref[...]
+    pre_first = base_ref[...] + nn(encoded, wmid_ref[...])
     first, first_slope = gelu_pair(pre_first)
     first = first.astype(BF16)
     _, second_slope = gelu_pair(nn(first, wout_ref[...]) + b2_ref[...])
@@ -167,7 +174,14 @@
     benc_sum[2:3, :] = col_sum(grad_second)
     sums = benc_sum[...]
     high = sums.astype(BF16).astype(F32)
-    bias_ref[...] = jnp.concatenate([high, sums - high], axis=0).astype(BF16)
+    bias = jnp.concatenate([high, sums - high], axis=0).astype(BF16)
+    rows = surf_ref.shape[1]
+    for m, out in enumerate(surf_refs):
+        if len(out.shape) == 2:
+            out[0:rows, :] = surf_ref[m]
+            out[rows:, :] = bias
+        else:
+            loop(out.shape[0], functools.partial(fill, out, surf_ref, bias))
 
     def put(first_at, rows, values, twin=None):
         values = values.astype(BF16)
@@ -199,44 +213,62 @@
         out[...] = (keep_ref[rows].astype(F32) + got_ref[rows].astype(F32)).astype(BF16)
 
 
-def split_kernel(place_ref, keep_ref, got_ref, surf_ref, bias_ref, *outs):
+def split_kernel(place_ref, keep_ref, got_ref, _, *outs):
     mine = place_ref[0]
-    rows = keep_ref.shape[1]
-    more = surf_ref.shape[1]
     for m, out in enumerate(outs):
         at = mine ^ m
-        out[0:rows, :] = (keep_ref[at].astype(F32) + got_ref[at].astype(F32)).astype(BF16)
-        out[rows : rows + more, :] = surf_ref[m]
-        out[rows + more :, :] = bias_ref[...]
-
-
-def sum_kernel(*refs):
+        out[...] = (keep_ref[at].astype(F32) + got_ref[at].astype(F32)).astype(BF16)
+
+
+def sum_kernel(_, *refs):
+    total = refs[0][...].astype(F32)
+    for ref in refs[1:-1]:
+        total = total + ref[...].astype(F32)
+    refs[-1][...] = total.astype(BF16)
+
+
+def join_kernel(*refs):
+    for m, ref in enumerate(refs[:-1]):
+        refs[-1][m] = ref[...]
+
+
+def label_kernel(ids_ref, *refs):
     out = refs[-1]
-    rows = out.shape[0]
-    total = refs[0][0:rows, :].astype(F32)
-    for ref in refs[1:-1]:
-        total = total + ref[0:rows, :].astype(F32)
-    out[...] = total.astype(BF16)
-
-
-def join_kernel(*refs):
-    out = refs[-1]
-    count = out.shape[0]
-    for m in range(count):
-        rows = refs[m].shape[0]
-        out[m, 0:rows, :] = refs[m][...]
-        out[m, rows:, :] = refs[count + m][rows:, :]
-
-
-def final_kernel(
-    place_ref, ids_ref, own, over_x, over_core, over_both, surf, wenc, benc, win, wmid, b1, wout, b2
-):
-    c, x, z = place_ref[0], place_ref[1], place_ref[2]
+    for m, ref in enumerate(refs[:-1]):
+        rows = ref.shape[0] - 16
+        out[m, 0:rows, :] = ref[0:rows, :]
+        place = lax.broadcasted_iota(jnp.int32, (16, ref.shape[1]), 0)
+        tail = ref[rows:, :].astype(F32)
+        out[m, rows:, :] = jnp.where(place == 3, ids_ref[m].astype(F32), tail).astype(BF16)
+
+
+def surface_kernel(own, over_x, over_core, over_both, surf, benc, b1, b2):
     surf[...] = jnp.zeros_like(surf)
     block_rows, channels = surf.shape[1:]
+    quarter = block_rows // 4
     bias = None
-    for at, (ref, core, chip) in enumerate(
-        ((own, c, x), (over_x, c, 1 - x), (over_core, 1 - c, x), (over_both, 1 - c, 1 - x))
+    for ref in (own, over_x, over_core, over_both):
+        for m in range(ref.shape[0]):
+            tail = ref[m, quarter:, :].astype(F32)
+            block = jnp.max(tail[3:4, 0:channels]).astype(jnp.int32)
+            for q in range(4):
+                surf[block, q * quarter : (q + 1) * quarter, :] += ref[
+                    m, 0:quarter, q * channels : (q + 1) * channels
+                ].astype(F32)
+            bias = tail if bias is None else bias + tail
+    bias = bias[0:8, :] + bias[8:16, :]
+    benc[...] = bias[0:1, :]
+    b1[...] = bias[1:2, :]
+    b2[...] = bias[2:3, :]
+
+
+def weights_kernel(place_ref, own, over_x, over_core, over_both, wenc, win, wmid, wout):
+    c, x, z = place_ref[0], place_ref[1], place_ref[2]
+    for ref, core, chip in (
+        (own, c, x),
+        (over_x, c, 1 - x),
+        (over_core, 1 - c, x),
+        (over_both, 1 - c, 1 - x),
     ):
         for m in range(4):
             spot = chip * 4 + (z ^ m)
@@ -253,21 +285,8 @@
             def _():
                 wenc[narrow, :] = ref[m, 64:80, :]
 
-            block = ids_ref[at, m]
-            quarter = block_rows // 4
-            for q in range(4):
-                surf[block, q * quarter : (q + 1) * quarter, :] += ref[
-                    m, 80:112, q * channels : (q + 1) * channels
-                ].astype(F32)
-            term = ref[m, 112:128, :].astype(F32)
-            bias = term if bias is None else bias + term
-    bias = bias[0:8, :] + bias[8:16, :]
-    benc[...] = bias[0:1, :]
-    b1[...] = bias[1:2, :]
-    b2[...] = bias[2:3, :]
-
-
-def call(kernel, out_shape, in_specs, *args, out_specs=None, scratch=(), flops=0):
+
+def call(kernel, out_shape, in_specs, *args, out_specs=None, scratch=(), flops=0, limit=LIMIT):
     many = isinstance(out_shape, (list, tuple))
     return pl.pallas_call(
         kernel,
@@ -275,7 +294,7 @@
         in_specs=in_specs,
         out_specs=out_specs or ([VMEM] * len(out_shape) if many else VMEM),
         scratch_shapes=scratch,
-        compiler_params=PARAMS,
+        compiler_params=pltpu.CompilerParams(vmem_limit_bytes=limit),
         cost_estimate=pl.CostEstimate(flops=flops, bytes_accessed=1 << 20, transcendentals=0),
     )(*args)
 
@@ -284,7 +303,33 @@
     return jax.ShapeDtypeStruct(dims, kind)
 
 
-def compute(place, owner, count, pieces, entry_row, entry_cell, arrays):
+def prepare(count, entry_cell, n_sub, arrays):
+    vol, cot, wenc, benc, win, wmid, b1, wout, b2 = arrays
+    block_rows = entry_cell.shape[1] // n_sub
+    cells, channels = vol.shape
+    hidden = cot.shape[1]
+    groups = n_sub // GROUP
+    entries = GROUP * block_rows
+    far = [pltpu.with_memory_space_constraint(a, pltpu.HBM) for a in (win, vol, wenc, wmid, wout, cot)]
+    return call(
+        functools.partial(early_kernel, block_rows),
+        [shape(a.shape) for a in far[1:]]
+        + [
+            shape((groups, cells, entries)),
+            shape((cells, channels), F32),
+            shape((cells, hidden), F32),
+        ],
+        [SMEM, VMEM, VMEM] + [HBM] * 6,
+        count,
+        entry_cell.reshape(groups, 1, entries),
+        b1.reshape(1, hidden),
+        *far,
+        scratch=[pltpu.VMEM(win.shape, BF16), pltpu.SemaphoreType.DMA((6,))],
+        flops=1 << 30,
+    )
+
+
+def compute(place, owner, pieces, entry_row, early, arrays):
     vol, cot, wenc, benc, win, wmid, b1, wout, b2 = arrays
     n_sub = owner.shape[0]
     block_rows = entry_row.shape[1] // n_sub
@@ -292,42 +337,40 @@
     hidden = cot.shape[1]
     groups = n_sub // GROUP
     entries = GROUP * block_rows
-    return call(
-        functools.partial(main_kernel, len(pieces)),
-        [
-            shape((8, 80, hidden)),
-            shape((8, 80, hidden)),
-            shape((n_sub, block_rows // 4, hidden)),
-            shape((16, hidden)),
-        ],
-        [SMEM] * 3 + [VMEM] * (len(pieces) + 11),
+    message = (block_rows // 4 + 16, hidden)
+    messages = [shape(message)] * n_sub if len(pieces) > 1 else [shape((n_sub,) + message)]
+    near_vol, near_wenc, near_wmid, near_wout, near_cot, hot, scale, base = early
+    keep, send, *messages = call(
+        functools.partial(main_kernel, len(pieces), len(messages)),
+        [shape((8, 80, hidden)), shape((8, 80, hidden))] + messages,
+        [SMEM] * 2 + [VMEM] * (len(pieces) + 11),
         place,
         owner,
-        count,
         *pieces,
         entry_row.reshape(groups, 1, entries),
-        entry_cell.reshape(groups, 1, entries),
-        vol,
-        cot,
-        wenc,
         benc.reshape(1, hidden),
-        win,
-        wmid,
-        b1.reshape(1, hidden),
-        wout,
         b2.reshape(1, hidden),
+        near_wenc,
+        near_vol,
+        near_wmid,
+        near_wout,
+        near_cot,
+        hot,
+        scale,
+        base,
         scratch=[
             pltpu.VMEM((n_sub, block_rows, channels), BF16),
             pltpu.VMEM((groups, entries, channels), BF16),
             pltpu.VMEM((groups, entries, hidden), F32),
-            pltpu.VMEM((groups, cells, entries), BF16),
             pltpu.VMEM((cells, hidden), F32),
-            pltpu.VMEM((cells, channels), F32),
             pltpu.VMEM((channels, hidden), F32),
             pltpu.VMEM((8, hidden), F32),
+            pltpu.VMEM((n_sub, block_rows // 4, hidden), BF16),
         ],
         flops=1 << 31,
-    )
+        limit=32 * 1024 * 1024,
+    )
+    return keep, send, messages
 
 
 def swap(value, axis, mask, size):
@@ -345,61 +388,69 @@
 
     request = jnp.concatenate([owner, local]).reshape(1, 2 * n_sub)
     requests = [request] + [swap(request, "sub", m, n_sub) for m in along_z]
+    early = prepare(count, entry_cell, n_sub, arrays)
     *blocks, ids = call(
         serve_kernel,
         [shape((block_rows, channels))] * n_sub + [shape((n_sub,), jnp.int32)],
-        [SMEM] * (n_sub + 1) + [ANY],
+        [SMEM] * (n_sub + 1) + [HBM, ANY],
         me.reshape(1),
         *requests,
-        surface,
+        pltpu.with_memory_space_constraint(surface, pltpu.HBM),
+        early[6],
         out_specs=[VMEM] * n_sub + [SMEM],
         scratch=[pltpu.SemaphoreType.DMA((n_sub,))],
     )
     blocks = [blocks[0]] + [swap(blocks[m], "sub", m, n_sub) for m in along_z]
-    ids = ids.reshape(1, n_sub)
-    ids = jnp.concatenate([ids, swap(ids, "region", 2, 4)])
-    ids = jnp.concatenate([ids, swap(ids, "region", 1, 4)])
-
-    keep, send, surf, bias = compute(
-        jnp.stack([core, me]), owner, count, blocks, entry_row, entry_cell, arrays
+    keep, send, messages = compute(
+        jnp.stack([core, me]), owner, blocks, entry_row, early, arrays
     )
     got = swap(send, "region", 1, 4)
     keep, send = call(
         halve_kernel, [shape((4, 80, hidden))] * 2, [SMEM, VMEM, VMEM], chip.reshape(1), keep, got
     )
     got = swap(send, "region", 2, 4)
-    messages = call(
+    messages = [messages[0]] + [swap(messages[m], "sub", m, n_sub) for m in along_z]
+    terms = call(
+        label_kernel,
+        shape((n_sub,) + messages[0].shape),
+        [SMEM] + [VMEM] * n_sub,
+        ids,
+        *messages,
+    )
+    shards = call(
         split_kernel,
-        [shape((128, hidden))] * n_sub,
-        [SMEM] + [VMEM] * 4,
+        [shape((80, hidden))] * n_sub,
+        [SMEM, VMEM, VMEM, ANY],
         me.reshape(1),
         keep,
         got,
-        surf,
-        bias,
-    )
-    messages = [messages[0]] + [swap(messages[m], "sub", m, n_sub) for m in along_z]
-    total = call(sum_kernel, shape((80, hidden)), [VMEM] * n_sub, *messages)
+        terms,
+    )
+    shards = [shards[0]] + [swap(shards[m], "sub", m, n_sub) for m in along_z]
+    terms_x = swap(terms, "region", 2, 4)
+    terms_core = swap(terms, "region", 1, 4)
+    terms_both = swap(terms_x, "region", 1, 4)
+    surf, benc, b1, b2 = call(
+        surface_kernel,
+        [shape((surface.shape[0] // block_rows, block_rows, channels), F32)]
+        + [shape((1, hidden), F32)] * 3,
+        [VMEM] * 4,
+        terms,
+        terms_x,
+        terms_core,
+        terms_both,
+    )
+    total = call(sum_kernel, shape((80, hidden)), [ANY] + [VMEM] * n_sub, terms_x, *shards)
     totals = [total] + [swap(total, "sub", m, n_sub) for m in along_z]
-    own = call(join_kernel, shape((n_sub, 128, hidden)), [VMEM] * (2 * n_sub), *totals, *messages)
+    own = call(join_kernel, shape((n_sub, 80, hidden)), [VMEM] * n_sub, *totals)
     over_x = swap(own, "region", 2, 4)
     over_core = swap(own, "region", 1, 4)
     over_both = swap(over_x, "region", 1, 4)
-    surf, wenc, benc, win, wmid, b1, wout, b2 = call(
-        final_kernel,
-        [
-            shape((surface.shape[0] // block_rows, block_rows, channels), F32),
-            shape((128, hidden)),
-            shape((1, hidden), F32),
-            shape((128, hidden)),
-            shape((512, hidden)),
-            shape((1, hidden), F32),
-            shape((512, hidden)),
-            shape((1, hidden), F32),
-        ],
-        [SMEM, SMEM] + [VMEM] * 4,
+    wenc, win, wmid, wout = call(
+        weights_kernel,
+        [shape((128, hidden)), shape((128, hidden)), shape((512, hidden)), shape((512, hidden))],
+        [SMEM] + [VMEM] * 4,
         jnp.stack([core, chip, me]),
-        ids,
         own,
         over_x,
         over_core,
@@ -427,13 +478,19 @@
     asked = to_all(wanted)
     stored = surface.reshape(surface.shape[0] // block_rows, block_rows, channels)
     fetched = to_all(jnp.take(stored, asked, axis=0))
-    keep, send, surf, bias = compute(
-        jnp.zeros((2,), jnp.int32), owner, count, [fetched], entry_row, entry_cell, arrays
-    )
-    surf = to_all(surf).astype(F32).reshape(n_sub, block_rows // 4, 4, channels)
+    keep, send, (messages,) = compute(
+        jnp.zeros((2,), jnp.int32),
+        owner,
+        [fetched],
+        entry_row,
+        prepare(count, entry_cell, n_sub, arrays),
+        arrays,
+    )
+    bias = messages[0, block_rows // 4 :].astype(F32)
+    bias = bias[0:8] + bias[8:16]
+    surf = to_all(messages[:, : block_rows // 4]).astype(F32).reshape(n_sub, block_rows // 4, 4, channels)
     surf = surf.transpose(0, 2, 1, 3).reshape(n_sub, block_rows, channels)
     surf = jnp.zeros(stored.shape, F32).at[asked].add(surf).reshape(surface.shape)
-    bias = bias[0:8].astype(F32) + bias[8:16].astype(F32)
     shards, bias = lax.psum(
         (jnp.concatenate([keep, send]).astype(F32), bias), ("region", "sub")
     )

time: 84.5 us -> 71.7 us (0.85)
  waiting for transfers between devices: 41.1 us -> 26.8 us
  local copies, waits for them, and re-layouts: 7.22 us -> 2.02 us
  starting transfers between devices: 23.8 us -> 27.8 us
  Pallas kernels: 10.3 us -> 13.1 us
    ppermute x19 -> x23, waiting for transfers between devices: 41.1 us -> 26.8 us  [swap(): return lax.ppermute(value, axis, [(i, i ^ mask) for i in range(size)])]
    unnamed x28 -> x14, local copies, waits for them, and re-layouts: 7.22 us -> 2.02 us
    ppermute x19 -> x23, starting transfers between devices: 23.8 us -> 27.8 us  [swap(): return lax.ppermute(value, axis, [(i, i ^ mask) for i in range(size)])]
    pallas_call x7 -> x10, Pallas kernels: 10.3 us -> 13.1 us  [call(): pl.pallas_call(kernel, out_shape=out_shape, in_specs=in_specs, out_specs=...]
  transfers between devices with their start and end apart: 19 -> 23, of which waited for: 12 -> 14; matrix products, arithmetic and copies ran while one was open for 0% -> 0% of each run, Pallas kernels for 0% -> 5%
where the time goes in v2:
time: 71.7 us; the launch traced here: 71.4 us
  starting transfers between devices  27.8 us (39%)
  waiting for transfers between devices  26.8 us (37%)
  Pallas kernels  13.1 us (18%)
  local copies, waits for them, and re-layouts  2.02 us (3%)
  between operations  1.43 us (2%)
    ppermute x23, starting transfers between devices, swap(): return lax.ppermute(value, axis, [(i, i ^ mask) for i in range(size)])  27.8 us
    ppermute x23, waiting for transfers between devices, swap(): return lax.ppermute(value, axis, [(i, i ^ mask) for i in range(size)])  26.8 us
    pallas_call x10, Pallas kernels, call(): pl.pallas_call(kernel, out_shape=out_shape, in_specs=in_specs, out_specs=...  13.1 us
    unnamed x14, local copies, waits for them, and re-layouts  2.02 us
  transfers between devices with their start and end apart: 23, of which 14 were waited for; matrix products, arithmetic and copies ran while one was open for 0% of the time, Pallas kernels for 5%

profile of v2, /device:TPU:0, one launch (start us, length us, event | category | flops | bytes accessed | tf_op | source)
XLA Modules:
  0.0 71.4 jit_solution(5746681745712510603)
XLA Ops:
  0.7 0.6 copy-done.5
  1.3 0.0 copy-done.6
  1.3 0.1 add_bitcast_fusion.refs_0_
  1.4 5.0 %collective-permute-start.2 = (s32[1,8]{1,0:T(1,128)S(1)}, s32[1,8]{1,0:T(1,128)S(1)}, u32[]{:S(2)}, u32[]{:S(2)}) collective-permute-start(s32[1,8]{1,0:T(1,128)S(1)} %add_bitcast_fusion.refs_0_), channel_id=1, source_target_pairs={{0,3},{1,2},{2,1},{3,0},{4,7},{5,6},{6,5},{7,4},{8,11},{9,10},{10,... | collective-permute-start | bytes 104 | tf_op jit(solution)/shard_map/ppermute | solution.py:377
  6.4 0.0 collective-permute-start.1
  6.4 0.6 collective-permute-start
  7.7 0.0 copy-start.1
  7.7 0.0 copy-start
  7.7 0.7 copy-done.1
  8.4 0.0 copy-done
  8.4 1.6 %shard_map.206 = (bf16[512,128]{1,0:T(8,128)(2,1)S(1)}, bf16[128,512]{1,0:T(8,128)(2,1)S(1)}, bf16[512,512]{1,0:T(8,128)(2,1)S(1)}, bf16[512,512]{1,0:T(8,128)(2...) custom-call(s32[1]{0:T(128)S(6)} %copy.23.count_ref, ...), custom_call_target="tpu_custom_call" | custom-call | flops 1073741824 | bytes 1048576 | tf_op jit(solution)/shard_map/pallas_call | solution.py:291
  10.0 0.0 collective-permute-done.2.refs_3_
  10.0 0.8 %collective-permute-done.1.refs_2_ = s32[1,8]{1,0:T(1,128)S(1)} collective-permute-done((s32[1,8]{1,0:T(1,128)S(1)}, s32[1,8]{1,0:T(1,128)S(1)}, u32[]{:S(2)}, u32[]{:S(2)}) %collective-permute-start.1) | collective-permute-done | bytes 64 | tf_op jit(solution)/shard_map/ppermute | solution.py:377
  10.9 0.0 collective-permute-done.refs_1_
  10.9 2.0 %shard_map.207 = (bf16[128,128]{1,0:T(8,128)(2,1)S(1)}, bf16[128,128]{1,0:T(8,128)(2,1)S(1)}, bf16[128,128]{1,0:T(8,128)(2,1)S(1)}, bf16[128,128]{1,0:T(8,128)(2,1)S(1)}, s32[4]{0:T(128)S(1)}) custom-call(s32[1]{0:T(128)} %bitcast.me_ref.place_ref, s32[1,8]{1,0:T(1,128)S(1)} %add_bitcast_fusion.refs_0_, s32[1,8]{1,0:T(1,128)S(1)} %collective-permute-done.refs_1_, ...), custom_call_target="tpu_custom_call" | custom-call | bytes 1048576 | tf_op jit(solution)/shard_map/pallas_call | solution.py:291
  12.9 0.7 collective-permute-start.3
  13.6 2.9 %collective-permute-start.4 = (bf16[128,128]{1,0:T(8,128)(2,1)S(1)}, bf16[128,128]{1,0:T(8,128)(2,1)S(1)}, u32[]{:S(2)}, u32[]{:S(2)}) collective-permute-start(bf16[128,128]{1,0:T(8,128)(2,1)S(1)} %get-tuple-element.45), channel_id=1, source_target_pairs={{0,2},{1,3},{2,0},{3,1},{4,6},{5,7},{6,4},{7,5},{8,10},{9,11},{10,... | collective-permute-start | bytes 98312 | tf_op jit(solution)/shard_map/ppermute | solution.py:377
  16.5 0.9 %collective-permute-start.5 = (bf16[128,128]{1,0:T(8,128)(2,1)S(1)}, bf16[128,128]{1,0:T(8,128)(2,1)S(1)}, u32[]{:S(2)}, u32[]{:S(2)}) collective-permute-start(bf16[128,128]{1,0:T(8,128)(2,1)S(1)} %get-tuple-element.46), channel_id=1, source_target_pairs={{0,3},{1,2},{2,1},{3,0},{4,7},{5,6},{6,5},{7,4},{8,11},{9,10},{10,... | collective-permute-start | bytes 98312 | tf_op jit(solution)/shard_map/ppermute | solution.py:377
  17.3 0.1 pad_add_fusion.place_ref
  17.4 0.0 collective-permute-done.3.refs_1_
  17.4 1.0 %collective-permute-done.4.refs_2_ = bf16[128,128]{1,0:T(8,128)(2,1)S(1)} collective-permute-done((bf16[128,128]{1,0:T(8,128)(2,1)S(1)}, bf16[128,128]{1,0:T(8,128)(2,1)S(1)}, u32[]{:S(2)}, u32[]{:S(2)}) %collective-permute-start.4) | collective-permute-done | bytes 32800 | tf_op jit(solution)/shard_map/ppermute | solution.py:377
  18.4 3.8 %collective-permute-done.5.refs_3_ = bf16[128,128]{1,0:T(8,128)(2,1)S(1)} collective-permute-done((bf16[128,128]{1,0:T(8,128)(2,1)S(1)}, bf16[128,128]{1,0:T(8,128)(2,1)S(1)}, u32[]{:S(2)}, u32[]{:S(2)}) %collective-permute-start.5) | collective-permute-done | bytes 32800 | tf_op jit(solution)/shard_map/ppermute | solution.py:377
  22.2 0.7 copy-done.2
  22.9 5.7 %shard_map.208 = (bf16[8,80,512]{2,1,0:T(8,128)(2,1)S(1)}, bf16[8,80,512]{2,1,0:T(8,128)(2,1)S(1)}, bf16[48,512]{1,0:T(8,128)(2,1)S(1)}, bf16[48,512]{1,0:T(8,12...) custom-call(s32[2]{0:T(128)S(1)} %pad_add_fusion.place_ref, s32[4]{0:T(128)S(1)} %bitcast.22, ...), custom_call_target="tpu_custom_call" | custom-call | flops 2147483648 | bytes 1048576 | tf_op jit(solution)/shard_map/pallas_call | solution.py:291
  28.6 0.1 collective-permute-start.12
  28.7 2.1 %collective-permute-done.12.got_ref = bf16[8,80,512]{2,1,0:T(8,128)(2,1)S(1)} collective-permute-done((bf16[8,80,512]{2,1,0:T(8,128)(2,1)S(1)}, bf16[8,80,512]{2,1,0:T(8,128)(2,1)S(1)}, u32[]{:S(2)}, u32[]{:S(2)}) %collective-permute-start.12) | collective-permute-done | bytes 655392 | tf_op jit(solution)/shard_map/ppermute | solution.py:377
  30.7 0.2 shard_map.211
  30.9 1.6 %collective-permute-start.13 = (bf16[4,80,512]{2,1,0:T(8,128)(2,1)S(1)}, bf16[4,80,512]{2,1,0:T(8,128)(2,1)S(1)}, u32[]{:S(2)}, u32[]{:S(2)}) collective-permute-start(bf16[4,80,512]{2,1,0:T(8,128)(2,1)S(1)} %get-tuple-element.62), channel_id=1, source_target_pairs={{0,8},{4,12},{8,0},{12,4},{1,9},{5,13},{9,1},{13,5},{2,10},{6,14},... | collective-permute-start | bytes 983048 | tf_op jit(solution)/shard_map/ppermute | solution.py:377
  32.5 0.0 collective-permute-start.6
  32.5 1.4 %collective-permute-start.7 = (bf16[48,512]{1,0:T(8,128)(2,1)S(1)}, bf16[48,512]{1,0:T(8,128)(2,1)S(1)}, u32[]{:S(2)}, u32[]{:S(2)}) collective-permute-start(bf16[48,512]{1,0:T(8,128)(2,1)S(1)} %get-tuple-element.56), channel_id=1, source_target_pairs={{0,2},{1,3},{2,0},{3,1},{4,6},{5,7},{6,4},{7,5},{8,10},{9,11},{10,... | collective-permute-start | bytes 147464 | tf_op jit(solution)/shard_map/ppermute | solution.py:377
  33.8 3.0 %collective-permute-start.8 = (bf16[48,512]{1,0:T(8,128)(2,1)S(1)}, bf16[48,512]{1,0:T(8,128)(2,1)S(1)}, u32[]{:S(2)}, u32[]{:S(2)}) collective-permute-start(bf16[48,512]{1,0:T(8,128)(2,1)S(1)} %get-tuple-element.57), channel_id=1, source_target_pairs={{0,3},{1,2},{2,1},{3,0},{4,7},{5,6},{6,5},{7,4},{8,11},{9,10},{10,... | collective-permute-start | bytes 147464 | tf_op jit(solution)/shard_map/ppermute | solution.py:377
  36.9 0.0 collective-permute-done.6.refs_1_
  36.9 2.2 %collective-permute-done.7.refs_2_ = bf16[48,512]{1,0:T(8,128)(2,1)S(1)} collective-permute-done((bf16[48,512]{1,0:T(8,128)(2,1)S(1)}, bf16[48,512]{1,0:T(8,128)(2,1)S(1)}, u32[]{:S(2)}, u32[]{:S(2)}) %collective-permute-start.7) | collective-permute-done | bytes 49184 | tf_op jit(solution)/shard_map/ppermute | solution.py:377
  39.0 0.7 %collective-permute-done.8.refs_3_ = bf16[48,512]{1,0:T(8,128)(2,1)S(1)} collective-permute-done((bf16[48,512]{1,0:T(8,128)(2,1)S(1)}, bf16[48,512]{1,0:T(8,128)(2,1)S(1)}, u32[]{:S(2)}, u32[]{:S(2)}) %collective-permute-start.8) | collective-permute-done | bytes 49184 | tf_op jit(solution)/shard_map/ppermute | solution.py:377
  39.8 0.6 shard_map.209.own._
  40.4 0.6 collective-permute-start.9
  41.0 0.0 collective-permute-done.13.got_ref
  41.0 0.1 shard_map.212
  41.0 0.9 %collective-permute-start.14 = (bf16[80,512]{1,0:T(8,128)(2,1)S(1)}, bf16[80,512]{1,0:T(8,128)(2,1)S(1)}, u32[]{:S(2)}, u32[]{:S(2)}) collective-permute-start(bf16[80,512]{1,0:T(8,128)(2,1)S(1)} %get-tuple-element.64), channel_id=1, source_target_pairs={{0,1},{1,0},{2,3},{3,2},{4,5},{5,4},{6,7},{7,6},{8,9},{9,8},{10,11... | collective-permute-start | bytes 245768 | tf_op jit(solution)/shard_map/ppermute | solution.py:377
  41.9 2.7 %collective-permute-start.15 = (bf16[80,512]{1,0:T(8,128)(2,1)S(1)}, bf16[80,512]{1,0:T(8,128)(2,1)S(1)}, u32[]{:S(2)}, u32[]{:S(2)}) collective-permute-start(bf16[80,512]{1,0:T(8,128)(2,1)S(1)} %get-tuple-element.65), channel_id=1, source_target_pairs={{0,2},{1,3},{2,0},{3,1},{4,6},{5,7},{6,4},{7,5},{8,10},{9,11},{10,... | collective-permute-start | bytes 245768 | tf_op jit(solution)/shard_map/ppermute | solution.py:377
  44.6 0.9 %collective-permute-start.16 = (bf16[80,512]{1,0:T(8,128)(2,1)S(1)}, bf16[80,512]{1,0:T(8,128)(2,1)S(1)}, u32[]{:S(2)}, u32[]{:S(2)}) collective-permute-start(bf16[80,512]{1,0:T(8,128)(2,1)S(1)} %get-tuple-element.66), channel_id=1, source_target_pairs={{0,3},{1,2},{2,1},{3,0},{4,7},{5,6},{6,5},{7,4},{8,11},{9,10},{10,... | collective-permute-start | bytes 245768 | tf_op jit(solution)/shard_map/ppermute | solution.py:377
  45.5 0.6 collective-permute-done.9.over_x._
  46.1 0.0 collective-permute-done.14.refs_1_
  46.1 2.9 %collective-permute-done.15.refs_2_ = bf16[80,512]{1,0:T(8,128)(2,1)S(1)} collective-permute-done((bf16[80,512]{1,0:T(8,128)(2,1)S(1)}, bf16[80,512]{1,0:T(8,128)(2,1)S(1)}, u32[]{:S(2)}, u32[]{:S(2)}) %collective-permute-start.15) | collective-permute-done | bytes 81952 | tf_op jit(solution)/shard_map/ppermute | solution.py:377
  49.0 1.9 %collective-permute-done.16.refs_3_ = bf16[80,512]{1,0:T(8,128)(2,1)S(1)} collective-permute-done((bf16[80,512]{1,0:T(8,128)(2,1)S(1)}, bf16[80,512]{1,0:T(8,128)(2,1)S(1)}, u32[]{:S(2)}, u32[]{:S(2)}) %collective-permute-start.16) | collective-permute-done | bytes 81952 | tf_op jit(solution)/shard_map/ppermute | solution.py:377
  51.0 1.1 %collective-permute-start.19 = (bf16[80,512]{1,0:T(8,128)(2,1)S(1)}, bf16[80,512]{1,0:T(8,128)(2,1)S(1)}, u32[]{:S(2)}, u32[]{:S(2)}) collective-permute-start(bf16[80,512]{1,0:T(8,128)(2,1)S(1)} %shard_map.213.refs_0_), channel_id=1, source_target_pairs={{0,3},{1,2},{2,1},{3,0},{4,7},{5,6},{6,5},{7,4},{8,11},{9,10},{10,... | collective-permute-start | bytes 245768 | tf_op jit(solution)/shard_map/ppermute | solution.py:377
  52.1 1.5 %collective-permute-start.18 = (bf16[80,512]{1,0:T(8,128)(2,1)S(1)}, bf16[80,512]{1,0:T(8,128)(2,1)S(1)}, u32[]{:S(2)}, u32[]{:S(2)}) collective-permute-start(bf16[80,512]{1,0:T(8,128)(2,1)S(1)} %shard_map.213.refs_0_), channel_id=1, source_target_pairs={{0,2},{1,3},{2,0},{3,1},{4,6},{5,7},{6,4},{7,5},{8,10},{9,11},{10,... | collective-permute-start | bytes 245768 | tf_op jit(solution)/shard_map/ppermute | solution.py:377
  53.6 1.8 %collective-permute-start.17 = (bf16[80,512]{1,0:T(8,128)(2,1)S(1)}, bf16[80,512]{1,0:T(8,128)(2,1)S(1)}, u32[]{:S(2)}, u32[]{:S(2)}) collective-permute-start(bf16[80,512]{1,0:T(8,128)(2,1)S(1)} %shard_map.213.refs_0_), channel_id=1, source_target_pairs={{0,1},{1,0},{2,3},{3,2},{4,5},{5,4},{6,7},{7,6},{8,9},{9,8},{10,11... | collective-permute-start | bytes 245768 | tf_op jit(solution)/shard_map/ppermute | solution.py:377
  55.4 1.9 %collective-permute-done.19.refs_3_ = bf16[80,512]{1,0:T(8,128)(2,1)S(1)} collective-permute-done((bf16[80,512]{1,0:T(8,128)(2,1)S(1)}, bf16[80,512]{1,0:T(8,128)(2,1)S(1)}, u32[]{:S(2)}, u32[]{:S(2)}) %collective-permute-start.19) | collective-permute-done | bytes 81952 | tf_op jit(solution)/shard_map/ppermute | solution.py:377
  57.4 1.7 %collective-permute-done.18.refs_2_ = bf16[80,512]{1,0:T(8,128)(2,1)S(1)} collective-permute-done((bf16[80,512]{1,0:T(8,128)(2,1)S(1)}, bf16[80,512]{1,0:T(8,128)(2,1)S(1)}, u32[]{:S(2)}, u32[]{:S(2)}) %collective-permute-start.18) | collective-permute-done | bytes 81952 | tf_op jit(solution)/shard_map/ppermute | solution.py:377
  59.0 0.0 collective-permute-done.17.refs_1_
  59.1 1.6 %collective-permute-start.20 = (bf16[4,80,512]{2,1,0:T(8,128)(2,1)S(1)}, bf16[4,80,512]{2,1,0:T(8,128)(2,1)S(1)}, u32[]{:S(2)}, u32[]{:S(2)}) collective-permute-start(bf16[4,80,512]{2,1,0:T(8,128)(2,1)S(1)} %shard_map.214.own), channel_id=1, source_target_pairs={{0,8},{4,12},{8,0},{12,4},{1,9},{5,13},{9,1},{13,5},{2,10},{6,14},... | collective-permute-start | bytes 983048 | tf_op jit(solution)/shard_map/ppermute | solution.py:377
  60.7 0.0 collective-permute-start.21
  60.7 5.5 %collective-permute-done.20.over_x = bf16[4,80,512]{2,1,0:T(8,128)(2,1)S(1)} collective-permute-done((bf16[4,80,512]{2,1,0:T(8,128)(2,1)S(1)}, bf16[4,80,512]{2,1,0:T(8,128)(2,1)S(1)}, u32[]{:S(2)}, u32[]{:S(2)}) %collective-permute-start.20) | collective-permute-done | bytes 327712 | tf_op jit(solution)/shard_map/ppermute | solution.py:377
  66.2 0.0 collective-permute-start.22
  66.2 0.5 collective-permute-start.10
  66.7 0.0 collective-permute-start.11
  66.7 0.1 pad_add_fusion.1.place_ref
  66.8 1.3 %collective-permute-done.10.over_core = bf16[4,48,512]{2,1,0:T(8,128)(2,1)S(1)} collective-permute-done((bf16[4,48,512]{2,1,0:T(8,128)(2,1)S(1)}, bf16[4,48,512]{2,1,0:T(8,128)(2,1)S(1)}, u32[]{:S(2)}, u32[]{:S(2)}) %collective-permute-start.10) | collective-permute-done | bytes 196640 | tf_op jit(solution)/shard_map/ppermute | solution.py:377
  68.1 0.3 collective-permute-done.11.over_both
  68.4 1.2 %shard_map.210 = (f32[16,128,128]{2,1,0:T(8,128)}, f32[1,512]{1,0:T(1,128)}, f32[1,512]{1,0:T(1,128)}, f32[1,512]{1,0:T(1,128)}) custom-call(bf16[4,48,512]{2,1,0:T(8,128)(2,1)S(1)} %shard_map.209.own._, bf16[4,48,512]{2,1,0:T(8,128)(2,1)S(1)} %collective-permute-done.9.over_x._, bf16[4,48,512]{2,1,0:T(8,128)(2,1)S(1)} %collective-permute-done.10.over_core, ...), custom_call_target="tpu_custom_call" | custom-call | bytes 1048576 | tf_op jit(solution)/shard_map/pallas_call | solution.py:291
  69.6 0.0 collective-permute-done.21.over_core
  69.6 0.0 collective-permute-done.22.over_both
  69.6 1.8 %shard_map.215 = (bf16[128,512]{1,0:T(8,128)(2,1)}, bf16[128,512]{1,0:T(8,128)(2,1)}, bf16[512,512]{1,0:T(8,128)(2,1)}, bf16[512,512]{1,0:T(8,128)(2,1)}) custom-call(s32[3]{0:T(128)S(1)} %pad_add_fusion.1.place_ref, bf16[4,80,512]{2,1,0:T(8,128)(2,1)S(1)} %shard_map.214.own, bf16[4,80,512]{2,1,0:T(8,128)(2,1)S(1)} %collective-permute-done.20.over_x, ...), custom_call_target="tpu_custom_call" | custom-call | bytes 1048576 | tf_op jit(solution)/shard_map/pallas_call | solution.py:291
  (9 shorter events, 0.1 us)
Async XLA Ops:
  0.6 0.7 copy-start.5
  0.6 0.7 copy-start.6
  1.4 8.7 %collective-permute-start.2 = (s32[1,8]{1,0:T(1,128)S(1)}, s32[1,8]{1,0:T(1,128)S(1)}, u32[]{:S(2)}, u32[]{:S(2)}) collective-permute-start(s32[1,8]{1,0:T(1,128)S(1)} %add_bitcast_fusion.refs_0_), channel_id=1, source_target_pairs={{0,3},{1,2},{2,1},{3,0},{4,7},{5,6},{6,5},{7,4},{8,11},{9,10},{10,... | collective-permute-start | bytes 104 | tf_op jit(solution)/shard_map/ppermute | solution.py:377
  6.4 4.4 %collective-permute-start.1 = (s32[1,8]{1,0:T(1,128)S(1)}, s32[1,8]{1,0:T(1,128)S(1)}, u32[]{:S(2)}, u32[]{:S(2)}) collective-permute-start(s32[1,8]{1,0:T(1,128)S(1)} %add_bitcast_fusion.refs_0_), channel_id=1, source_target_pairs={{0,2},{1,3},{2,0},{3,1},{4,6},{5,7},{6,4},{7,5},{8,10},{9,11},{10,... | collective-permute-start | bytes 104 | tf_op jit(solution)/shard_map/ppermute | solution.py:377
  6.4 4.4 %collective-permute-start = (s32[1,8]{1,0:T(1,128)S(1)}, s32[1,8]{1,0:T(1,128)S(1)}, u32[]{:S(2)}, u32[]{:S(2)}) collective-permute-start(s32[1,8]{1,0:T(1,128)S(1)} %add_bitcast_fusion.refs_0_), channel_id=1, source_target_pairs={{0,1},{1,0},{2,3},{3,2},{4,5},{5,4},{6,7},{7,6},{8,9},{9,8},{10,11... | collective-permute-start | bytes 104 | tf_op jit(solution)/shard_map/ppermute | solution.py:377
  7.7 0.7 copy-start.1
  7.7 0.7 copy-start
  10.9 11.3 %copy-start.3 = (f32[512]{0:T(512)S(1)}, f32[512]{0:T(512)}, u32[]{:S(2)}) copy-start(f32[512]{0:T(512)} %param.19) | copy-start | bytes 6148
  10.9 11.3 %copy-start.4 = (f32[512]{0:T(512)S(1)}, f32[512]{0:T(512)}, u32[]{:S(2)}) copy-start(f32[512]{0:T(512)} %param.24) | copy-start | bytes 6148
  12.9 4.5 %collective-permute-start.3 = (bf16[128,128]{1,0:T(8,128)(2,1)S(1)}, bf16[128,128]{1,0:T(8,128)(2,1)S(1)}, u32[]{:S(2)}, u32[]{:S(2)}) collective-permute-start(bf16[128,128]{1,0:T(8,128)(2,1)S(1)} %get-tuple-element.44), channel_id=1, source_target_pairs={{0,1},{1,0},{2,3},{3,2},{4,5},{5,4},{6,7},{7,6},{8,9},{9,8},{10,11... | collective-permute-start | bytes 98312 | tf_op jit(solution)/shard_map/ppermute | solution.py:377
  13.6 4.8 %collective-permute-start.4 = (bf16[128,128]{1,0:T(8,128)(2,1)S(1)}, bf16[128,128]{1,0:T(8,128)(2,1)S(1)}, u32[]{:S(2)}, u32[]{:S(2)}) collective-permute-start(bf16[128,128]{1,0:T(8,128)(2,1)S(1)} %get-tuple-element.45), channel_id=1, source_target_pairs={{0,2},{1,3},{2,0},{3,1},{4,6},{5,7},{6,4},{7,5},{8,10},{9,11},{10,... | collective-permute-start | bytes 98312 | tf_op jit(solution)/shard_map/ppermute | solution.py:377
  16.5 5.7 %collective-permute-start.5 = (bf16[128,128]{1,0:T(8,128)(2,1)S(1)}, bf16[128,128]{1,0:T(8,128)(2,1)S(1)}, u32[]{:S(2)}, u32[]{:S(2)}) collective-permute-start(bf16[128,128]{1,0:T(8,128)(2,1)S(1)} %get-tuple-element.46), channel_id=1, source_target_pairs={{0,3},{1,2},{2,1},{3,0},{4,7},{5,6},{6,5},{7,4},{8,11},{9,10},{10,... | collective-permute-start | bytes 98312 | tf_op jit(solution)/shard_map/ppermute | solution.py:377
  22.2 0.7 copy-start.2
  28.6 2.2 %collective-permute-start.12 = (bf16[8,80,512]{2,1,0:T(8,128)(2,1)S(1)}, bf16[8,80,512]{2,1,0:T(8,128)(2,1)S(1)}, u32[]{:S(2)}, u32[]{:S(2)}) collective-permute-start(bf16[8,80,512]{2,1,0:T(8,128)(2,1)S(1)} %get-tuple-element.60), channel_id=1, source_target_pairs={{0,4},{4,0},{8,12},{12,8},{1,5},{5,1},{9,13},{13,9},{2,6},{6,2},{1... | collective-permute-start | bytes 1966088 | tf_op jit(solution)/shard_map/ppermute | solution.py:377
  30.9 10.1 %collective-permute-start.13 = (bf16[4,80,512]{2,1,0:T(8,128)(2,1)S(1)}, bf16[4,80,512]{2,1,0:T(8,128)(2,1)S(1)}, u32[]{:S(2)}, u32[]{:S(2)}) collective-permute-start(bf16[4,80,512]{2,1,0:T(8,128)(2,1)S(1)} %get-tuple-element.62), channel_id=1, source_target_pairs={{0,8},{4,12},{8,0},{12,4},{1,9},{5,13},{9,1},{13,5},{2,10},{6,14},... | collective-permute-start | bytes 983048 | tf_op jit(solution)/shard_map/ppermute | solution.py:377
  32.5 4.4 %collective-permute-start.6 = (bf16[48,512]{1,0:T(8,128)(2,1)S(1)}, bf16[48,512]{1,0:T(8,128)(2,1)S(1)}, u32[]{:S(2)}, u32[]{:S(2)}) collective-permute-start(bf16[48,512]{1,0:T(8,128)(2,1)S(1)} %get-tuple-element.55), channel_id=1, source_target_pairs={{0,1},{1,0},{2,3},{3,2},{4,5},{5,4},{6,7},{7,6},{8,9},{9,8},{10,11... | collective-permute-start | bytes 147464 | tf_op jit(solution)/shard_map/ppermute | solution.py:377
  32.5 6.6 %collective-permute-start.7 = (bf16[48,512]{1,0:T(8,128)(2,1)S(1)}, bf16[48,512]{1,0:T(8,128)(2,1)S(1)}, u32[]{:S(2)}, u32[]{:S(2)}) collective-permute-start(bf16[48,512]{1,0:T(8,128)(2,1)S(1)} %get-tuple-element.56), channel_id=1, source_target_pairs={{0,2},{1,3},{2,0},{3,1},{4,6},{5,7},{6,4},{7,5},{8,10},{9,11},{10,... | collective-permute-start | bytes 147464 | tf_op jit(solution)/shard_map/ppermute | solution.py:377
  33.8 5.9 %collective-permute-start.8 = (bf16[48,512]{1,0:T(8,128)(2,1)S(1)}, bf16[48,512]{1,0:T(8,128)(2,1)S(1)}, u32[]{:S(2)}, u32[]{:S(2)}) collective-permute-start(bf16[48,512]{1,0:T(8,128)(2,1)S(1)} %get-tuple-element.57), channel_id=1, source_target_pairs={{0,3},{1,2},{2,1},{3,0},{4,7},{5,6},{6,5},{7,4},{8,11},{9,10},{10,... | collective-permute-start | bytes 147464 | tf_op jit(solution)/shard_map/ppermute | solution.py:377
  40.4 5.7 %collective-permute-start.9 = (bf16[4,48,512]{2,1,0:T(8,128)(2,1)S(1)}, bf16[4,48,512]{2,1,0:T(8,128)(2,1)S(1)}, u32[]{:S(2)}, u32[]{:S(2)}) collective-permute-start(bf16[4,48,512]{2,1,0:T(8,128)(2,1)S(1)} %shard_map.209.own._), channel_id=1, source_target_pairs={{0,8},{4,12},{8,0},{12,4},{1,9},{5,13},{9,1},{13,5},{2,10},{6,14},... | collective-permute-start | bytes 589832 | tf_op jit(solution)/shard_map/ppermute | solution.py:377
  41.0 5.0 %collective-permute-start.14 = (bf16[80,512]{1,0:T(8,128)(2,1)S(1)}, bf16[80,512]{1,0:T(8,128)(2,1)S(1)}, u32[]{:S(2)}, u32[]{:S(2)}) collective-permute-start(bf16[80,512]{1,0:T(8,128)(2,1)S(1)} %get-tuple-element.64), channel_id=1, source_target_pairs={{0,1},{1,0},{2,3},{3,2},{4,5},{5,4},{6,7},{7,6},{8,9},{9,8},{10,11... | collective-permute-start | bytes 245768 | tf_op jit(solution)/shard_map/ppermute | solution.py:377
  41.9 7.1 %collective-permute-start.15 = (bf16[80,512]{1,0:T(8,128)(2,1)S(1)}, bf16[80,512]{1,0:T(8,128)(2,1)S(1)}, u32[]{:S(2)}, u32[]{:S(2)}) collective-permute-start(bf16[80,512]{1,0:T(8,128)(2,1)S(1)} %get-tuple-element.65), channel_id=1, source_target_pairs={{0,2},{1,3},{2,0},{3,1},{4,6},{5,7},{6,4},{7,5},{8,10},{9,11},{10,... | collective-permute-start | bytes 245768 | tf_op jit(solution)/shard_map/ppermute | solution.py:377
  44.6 6.3 %collective-permute-start.16 = (bf16[80,512]{1,0:T(8,128)(2,1)S(1)}, bf16[80,512]{1,0:T(8,128)(2,1)S(1)}, u32[]{:S(2)}, u32[]{:S(2)}) collective-permute-start(bf16[80,512]{1,0:T(8,128)(2,1)S(1)} %get-tuple-element.66), channel_id=1, source_target_pairs={{0,3},{1,2},{2,1},{3,0},{4,7},{5,6},{6,5},{7,4},{8,11},{9,10},{10,... | collective-permute-start | bytes 245768 | tf_op jit(solution)/shard_map/ppermute | solution.py:377
  51.0 6.4 %collective-permute-start.19 = (bf16[80,512]{1,0:T(8,128)(2,1)S(1)}, bf16[80,512]{1,0:T(8,128)(2,1)S(1)}, u32[]{:S(2)}, u32[]{:S(2)}) collective-permute-start(bf16[80,512]{1,0:T(8,128)(2,1)S(1)} %shard_map.213.refs_0_), channel_id=1, source_target_pairs={{0,3},{1,2},{2,1},{3,0},{4,7},{5,6},{6,5},{7,4},{8,11},{9,10},{10,... | collective-permute-start | bytes 245768 | tf_op jit(solution)/shard_map/ppermute | solution.py:377
  52.1 6.9 %collective-permute-start.18 = (bf16[80,512]{1,0:T(8,128)(2,1)S(1)}, bf16[80,512]{1,0:T(8,128)(2,1)S(1)}, u32[]{:S(2)}, u32[]{:S(2)}) collective-permute-start(bf16[80,512]{1,0:T(8,128)(2,1)S(1)} %shard_map.213.refs_0_), channel_id=1, source_target_pairs={{0,2},{1,3},{2,0},{3,1},{4,6},{5,7},{6,4},{7,5},{8,10},{9,11},{10,... | collective-permute-start | bytes 245768 | tf_op jit(solution)/shard_map/ppermute | solution.py:377
  53.6 5.5 %collective-permute-start.17 = (bf16[80,512]{1,0:T(8,128)(2,1)S(1)}, bf16[80,512]{1,0:T(8,128)(2,1)S(1)}, u32[]{:S(2)}, u32[]{:S(2)}) collective-permute-start(bf16[80,512]{1,0:T(8,128)(2,1)S(1)} %shard_map.213.refs_0_), channel_id=1, source_target_pairs={{0,1},{1,0},{2,3},{3,2},{4,5},{5,4},{6,7},{7,6},{8,9},{9,8},{10,11... | collective-permute-start | bytes 245768 | tf_op jit(solution)/shard_map/ppermute | solution.py:377
  59.1 7.1 %collective-permute-start.20 = (bf16[4,80,512]{2,1,0:T(8,128)(2,1)S(1)}, bf16[4,80,512]{2,1,0:T(8,128)(2,1)S(1)}, u32[]{:S(2)}, u32[]{:S(2)}) collective-permute-start(bf16[4,80,512]{2,1,0:T(8,128)(2,1)S(1)} %shard_map.214.own), channel_id=1, source_target_pairs={{0,8},{4,12},{8,0},{12,4},{1,9},{5,13},{9,1},{13,5},{2,10},{6,14},... | collective-permute-start | bytes 983048 | tf_op jit(solution)/shard_map/ppermute | solution.py:377
  60.7 9.0 %collective-permute-start.21 = (bf16[4,80,512]{2,1,0:T(8,128)(2,1)S(1)}, bf16[4,80,512]{2,1,0:T(8,128)(2,1)S(1)}, u32[]{:S(2)}, u32[]{:S(2)}) collective-permute-start(bf16[4,80,512]{2,1,0:T(8,128)(2,1)S(1)} %shard_map.214.own), channel_id=1, source_target_pairs={{0,4},{4,0},{8,12},{12,8},{1,5},{5,1},{9,13},{13,9},{2,6},{6,2},{1... | collective-permute-start | bytes 983048 | tf_op jit(solution)/shard_map/ppermute | solution.py:377
  66.2 3.4 %collective-permute-start.22 = (bf16[4,80,512]{2,1,0:T(8,128)(2,1)S(1)}, bf16[4,80,512]{2,1,0:T(8,128)(2,1)S(1)}, u32[]{:S(2)}, u32[]{:S(2)}) collective-permute-start(bf16[4,80,512]{2,1,0:T(8,128)(2,1)S(1)} %collective-permute-done.20.over_x), channel_id=1, source_target_pairs={{0,4},{4,0},{8,12},{12,8},{1,5},{5,1},{9,13},{13,9},{2,6},{6,2},{1... | collective-permute-start | bytes 983048 | tf_op jit(solution)/shard_map/ppermute | solution.py:377
  66.2 1.9 %collective-permute-start.10 = (bf16[4,48,512]{2,1,0:T(8,128)(2,1)S(1)}, bf16[4,48,512]{2,1,0:T(8,128)(2,1)S(1)}, u32[]{:S(2)}, u32[]{:S(2)}) collective-permute-start(bf16[4,48,512]{2,1,0:T(8,128)(2,1)S(1)} %shard_map.209.own._), channel_id=1, source_target_pairs={{0,4},{4,0},{8,12},{12,8},{1,5},{5,1},{9,13},{13,9},{2,6},{6,2},{1... | collective-permute-start | bytes 589832 | tf_op jit(solution)/shard_map/ppermute | solution.py:377
  66.7 1.7 %collective-permute-start.11 = (bf16[4,48,512]{2,1,0:T(8,128)(2,1)S(1)}, bf16[4,48,512]{2,1,0:T(8,128)(2,1)S(1)}, u32[]{:S(2)}, u32[]{:S(2)}) collective-permute-start(bf16[4,48,512]{2,1,0:T(8,128)(2,1)S(1)} %collective-permute-done.9.over_x._), channel_id=1, source_target_pairs={{0,4},{4,0},{8,12},{12,8},{1,5},{5,1},{9,13},{13,9},{2,6},{6,2},{1... | collective-permute-start | bytes 589832 | tf_op jit(solution)/shard_map/ppermute | solution.py:377

commit v3 on v2

v3 whole, which is shorter than its diff:
```python
import functools

import jax
import jax.numpy as jnp
from jax import lax
from jax.experimental import pallas as pl
from jax.experimental.pallas import tpu as pltpu
from jax.sharding import PartitionSpec as P

BF16 = jnp.bfloat16
F32 = jnp.float32
VMEM = pl.BlockSpec(memory_space=pltpu.VMEM)
SMEM = pl.BlockSpec(memory_space=pltpu.SMEM)
ANY = pl.BlockSpec(memory_space=pl.ANY)
HBM = pl.BlockSpec(memory_space=pltpu.HBM)
GROUP = 4
LIMIT = 16 * 1024 * 1024


def nn(a, b):
    return jnp.dot(a, b, preferred_element_type=F32)


def tn(a, b):
    return lax.dot_general(a, b, (((0,), (0,)), ((), ())), preferred_element_type=F32)


def nt(a, b):
    return lax.dot_general(a, b, (((1,), (1,)), ((), ())), preferred_element_type=F32)


def gelu_pair(v):
    square = v * v
    t = jnp.tanh(0.7978845608028654 * v * (1.0 + 0.044715 * square))
    half = 0.5 * (1.0 + t)
    inner = 0.7978845608028654 * (1.0 + 0.134145 * square)
    return v * half, half + 0.5 * v * (1.0 - t * t) * inner


def col_sum(a):
    return jnp.sum(a.astype(F32), axis=0, keepdims=True)


def loop(count, body):
    if count == 1:
        body(0)
    else:
        lax.fori_loop(0, count, lambda i, c: (body(i), c)[1], 0)


def serve_kernel(me_ref, *refs):
    count = (len(refs) - 3) // 2
    requests, surface, blocks = refs[:count], refs[count], refs[count + 1 : 2 * count + 1]
    ids_ref, sems = refs[2 * count + 1], refs[2 * count + 2]
    rows = blocks[0].shape[0]
    me = me_ref[0]
    copies = []
    for m, request in enumerate(requests):
        wanted = jnp.int32(0)
        for k in range(count):
            wanted = wanted + jnp.where(request[0, k] == me, request[0, count + k], 0)
        ids_ref[m] = wanted
        copy = pltpu.make_async_copy(
            surface.at[pl.ds(pl.multiple_of(wanted * rows, rows), rows), :], blocks[m], sems.at[m]
        )
        copy.start()
        copies.append(copy)
    for copy in copies:
        copy.wait()


def fill(out, surf_ref, bias, m):
    rows = surf_ref.shape[1]
    out[m, 0:rows, :] = surf_ref[m]
    out[m, rows:, :] = bias


def early_kernel(block_rows, count_ref, _, *refs):
    far, outs, sems = refs[:11], refs[11:22], refs[25]
    hot_ref, scale_ref, base_ref = outs[8:]
    cell_ref, win_ref, b1_ref = refs[22:25]
    near = (cell_ref, win_ref, b1_ref) + tuple(outs[:8])
    loads = [pltpu.make_async_copy(a, b, sems.at[i]) for i, (a, b) in enumerate(zip(far, near))]
    for load in loads:
        load.start()
    groups, cells, entries = hot_ref.shape
    channels = scale_ref.shape[1]
    live_count = count_ref[0]
    scale_ref[...] = jnp.zeros_like(scale_ref)
    loads[0].wait()

    def group(g):
        lane = lax.broadcasted_iota(jnp.int32, (1, entries), 1) // block_rows + g * GROUP
        named = jnp.where(lane < live_count, cell_ref[g], -1)
        hot = (lax.broadcasted_iota(jnp.int32, (cells, entries), 0) == named).astype(BF16)
        hot_ref[g] = hot
        scale_ref[...] += nn(hot, jnp.ones((entries, channels), BF16))

    loop(groups, group)
    scale_ref[...] = 1.0 / jnp.maximum(scale_ref[...], 1.0)
    for load in loads[1:4]:
        load.wait()
    base_ref[...] = nn(outs[0][...], win_ref[...]) + b1_ref[...]
    for load in loads[4:]:
        load.wait()


def row_hot(row_ref, block_rows, g, k):
    rows = lax.broadcasted_iota(jnp.int32, (block_rows, block_rows), 0)
    named = row_ref[g][:, k * block_rows : (k + 1) * block_rows]
    return (rows == named).astype(BF16)


def half_grads(which, out, early, made):
    vol_ref = early[0]
    first_ref, second_ref, encoded_ref, grad_first_ref, gathered_ref, entry_ref = made
    width = first_ref.shape[1] // 2
    columns = pl.ds(pl.multiple_of(which * width, width), width)
    for at, a, b in ((0, first_ref, second_ref), (32, encoded_ref, grad_first_ref)):
        values = tn(a[:, columns], b[...]).astype(BF16)
        for i in range(8):
            out[i, at : at + 32, :] = values[i * 32 : (i + 1) * 32, :]

    def narrow(values):
        values = values.astype(BF16)
        for i in range(8):
            out[i, 64:80, :] = values[i * 16 : (i + 1) * 16, :]

    @pl.when(which == 0)
    def _():
        narrow(tn(vol_ref[...], grad_first_ref[...]))

    @pl.when(which != 0)
    def _():
        groups = gathered_ref.shape[0]
        if groups == 1:
            narrow(tn(gathered_ref[0], entry_ref[0]))
        else:
            zero = jnp.zeros((gathered_ref.shape[2], entry_ref.shape[2]), F32)
            narrow(
                lax.fori_loop(
                    0, groups, lambda g, total: total + tn(gathered_ref[g], entry_ref[g]), zero
                )
            )


def main_kernel(n_pieces, n_out, place_ref, owner_ref, *refs):
    pieces, early = refs[:n_pieces], refs[n_pieces : n_pieces + 11]
    vol_ref, wenc_ref, wmid_ref, wout_ref, cot_ref, row_ref, benc_ref, b2_ref = early[:8]
    hot_ref, scale_ref, base_ref = early[8:]
    keep_ref, send_ref = refs[n_pieces + 11 : n_pieces + 13]
    outs = refs[n_pieces + 13 : n_pieces + 13 + n_out]
    made = refs[n_pieces + 13 + n_out : n_pieces + 19 + n_out]
    first_ref, second_ref, encoded_ref, grad_first_ref, gathered_ref, entry_ref = made
    blocks, slope_ref, total_ref, surf_ref, sums_ref = refs[n_pieces + 19 + n_out :]
    mask = place_ref[1]
    groups = row_ref.shape[0]
    hidden = cot_ref.shape[1]
    block_rows, channels = blocks.shape[1:]
    base = 0
    for piece in pieces:
        if len(piece.shape) == 2:
            blocks[base] = piece[...]
            base += 1
        else:
            blocks[...] = piece[...]
    total_ref[...] = jnp.zeros_like(total_ref)

    def encode(g):
        for k in range(GROUP):
            block = blocks[owner_ref[g * GROUP + k] ^ mask]
            gathered_ref[g, k * block_rows : (k + 1) * block_rows, :] = tn(
                row_hot(row_ref, block_rows, g, k), block
            ).astype(BF16)
        act, slope = gelu_pair(nn(gathered_ref[g], wenc_ref[...]) + benc_ref[...])
        slope_ref[g] = slope
        total_ref[...] += nn(hot_ref[g], act.astype(BF16))

    loop(groups, encode)
    scale = jnp.concatenate([scale_ref[...]] * (hidden // channels), axis=1)
    encoded = (total_ref[...] * scale).astype(BF16)
    encoded_ref[...] = encoded
    first, first_slope = gelu_pair(base_ref[...] + nn(encoded, wmid_ref[...]))
    first = first.astype(BF16)
    first_ref[...] = first
    _, second_slope = gelu_pair(nn(first, wout_ref[...]) + b2_ref[...])
    grad_second = (cot_ref[...].astype(F32) * second_slope).astype(BF16)
    second_ref[...] = grad_second
    grad_first = (nt(grad_second, wout_ref[...]) * first_slope).astype(BF16)
    grad_first_ref[...] = grad_first
    grad_cell = (nt(grad_first, wmid_ref[...]) * scale).astype(BF16)

    sums_ref[...] = jnp.zeros_like(sums_ref)

    def reverse(g):
        entry = (tn(hot_ref[g], grad_cell) * slope_ref[g]).astype(BF16)
        entry_ref[g] = entry
        sums_ref[0:1, :] += col_sum(entry)
        grad_row = nt(entry, wenc_ref[...]).astype(BF16)
        for k in range(GROUP):
            grad_block = nn(
                row_hot(row_ref, block_rows, g, k),
                grad_row[k * block_rows : (k + 1) * block_rows, :],
            ).astype(BF16)
            slot = owner_ref[g * GROUP + k] ^ mask
            quarter = block_rows // 4
            for q in range(4):
                surf_ref[slot, :, q * channels : (q + 1) * channels] = grad_block[
                    q * quarter : (q + 1) * quarter, :
                ]

    loop(groups, reverse)
    sums_ref[1:2, :] = col_sum(grad_first)
    sums_ref[2:3, :] = col_sum(grad_second)
    sums = sums_ref[...]
    high = sums.astype(BF16).astype(F32)
    bias = jnp.concatenate([high, sums - high], axis=0).astype(BF16)
    rows = surf_ref.shape[1]
    for m, out in enumerate(outs):
        if len(out.shape) == 2:
            out[0:rows, :] = surf_ref[m]
            out[rows:, :] = bias
        else:
            loop(out.shape[0], functools.partial(fill, out, surf_ref, bias))
    half_grads(1 - place_ref[0], send_ref, early, made)
    half_grads(place_ref[0], keep_ref, early, made)


def halve_kernel(place_ref, keep_ref, got_ref, next_keep, next_send):
    mine = place_ref[0]
    quarter = next_keep.shape[0]
    for out, at in ((next_keep, mine), (next_send, 1 - mine)):
        rows = pl.ds(at * quarter, quarter)
        out[...] = (keep_ref[rows].astype(F32) + got_ref[rows].astype(F32)).astype(BF16)


def split_kernel(place_ref, keep_ref, got_ref, *refs):
    mine, outs = place_ref[0], refs[3:]
    for m, out in enumerate(outs):
        at = mine ^ m
        out[...] = (keep_ref[at].astype(F32) + got_ref[at].astype(F32)).astype(BF16)


def sum_kernel(_, *refs):
    total = refs[0][...].astype(F32)
    for ref in refs[1:-1]:
        total = total + ref[...].astype(F32)
    refs[-1][...] = total.astype(BF16)


def join_kernel(*refs):
    for m, ref in enumerate(refs[:-1]):
        refs[-1][m] = ref[...]


def label_kernel(ids_ref, *refs):
    out = refs[-1]
    for m, ref in enumerate(refs[:-1]):
        rows = ref.shape[0] - 16
        out[m, 0:rows, :] = ref[0:rows, :]
        place = lax.broadcasted_iota(jnp.int32, (16, ref.shape[1]), 0)
        tail = ref[rows:, :].astype(F32)
        out[m, rows:, :] = jnp.where(place == 3, ids_ref[m].astype(F32), tail).astype(BF16)


def add_surface(groups, surf, benc, b1, b2):
    surf[...] = jnp.zeros_like(surf)
    block_rows, channels = surf.shape[1:]
    quarter = block_rows // 4
    sources = [ref.at[m] for ref in groups for m in range(ref.shape[0])]
    bias = None
    for ref in sources:
        tail = ref[quarter:, :].astype(F32)
        block = jnp.max(tail[3:4, 0:channels]).astype(jnp.int32)
        for q in range(4):
            surf[block, q * quarter : (q + 1) * quarter, :] += ref[
                0:quarter, q * channels : (q + 1) * channels
            ].astype(F32)
        bias = tail if bias is None else bias + tail
    bias = bias[0:8, :] + bias[8:16, :]
    benc[...] = bias[0:1, :]
    b1[...] = bias[1:2, :]
    b2[...] = bias[2:3, :]


def final_kernel(place_ref, own, over_x, over_core, over_both, *refs):
    surf, wenc, benc, win, wmid, b1, wout, b2 = refs[4:]
    add_surface(refs[:4], surf, benc, b1, b2)
    c, x, z = place_ref[0], place_ref[1], place_ref[2]
    pieces = []
    for m in range(4):
        pieces.append((own.at[m], c, x, m))
        pieces.append((over_x.at[m], c, 1 - x, m))
        pieces.append((over_core.at[m], 1 - c, x, m))
        pieces.append((over_both.at[m], 1 - c, 1 - x, m))
    for ref, at_core, at_chip, m in pieces:
        spot = at_chip * 4 + (z ^ m)
        wide = pl.ds(pl.multiple_of((at_core * 8 + spot) * 32, 32), 32)
        narrow = pl.ds(pl.multiple_of(spot * 16, 16), 16)
        wout[wide, :] = ref[0:32, :]
        wmid[wide, :] = ref[32:64, :]

        @pl.when(at_core == 0)
        def _():
            win[narrow, :] = ref[64:80, :]

        @pl.when(at_core != 0)
        def _():
            wenc[narrow, :] = ref[64:80, :]


def call(kernel, out_shape, in_specs, *args, out_specs=None, scratch=(), flops=0, limit=LIMIT):
    many = isinstance(out_shape, (list, tuple))
    return pl.pallas_call(
        kernel,
        out_shape=out_shape,
        in_specs=in_specs,
        out_specs=out_specs or ([VMEM] * len(out_shape) if many else VMEM),
        scratch_shapes=scratch,
        compiler_params=pltpu.CompilerParams(vmem_limit_bytes=limit),
        cost_estimate=pl.CostEstimate(flops=flops, bytes_accessed=1 << 20, transcendentals=0),
    )(*args)


def shape(dims, kind=BF16):
    return jax.ShapeDtypeStruct(dims, kind)


def prepare(count, after, entry_row, entry_cell, n_sub, arrays):
    vol, cot, wenc, benc, win, wmid, b1, wout, b2 = arrays
    block_rows = entry_cell.shape[1] // n_sub
    cells, channels = vol.shape
    hidden = cot.shape[1]
    groups = n_sub // GROUP
    entries = GROUP * block_rows
    rows, named = (a.reshape(groups, 1, entries) for a in (entry_row, entry_cell))
    benc, b1, b2 = (a.reshape(1, hidden) for a in (benc, b1, b2))
    far = (named, win, b1, vol, wenc, wmid, wout, cot, rows, benc, b2)
    far = [pltpu.with_memory_space_constraint(a, pltpu.HBM) for a in far]
    return call(
        functools.partial(early_kernel, block_rows),
        [shape(a.shape, a.dtype) for a in far[3:]]
        + [
            shape((groups, cells, entries)),
            shape((cells, channels), F32),
            shape((cells, hidden), F32),
        ],
        [SMEM, SMEM] + [HBM] * 11,
        count,
        after,
        *far,
        scratch=[pltpu.VMEM(a.shape, a.dtype) for a in far[:3]] + [pltpu.SemaphoreType.DMA((11,))],
        flops=1 << 30,
    )


def compute(place, owner, pieces, early, n_sub):
    vol, wenc, wmid, wout, cot, rows = early[:6]
    cells, channels = vol.shape
    hidden = cot.shape[1]
    groups, _, entries = rows.shape
    block_rows = entries // GROUP
    message = (block_rows // 4 + 16, hidden)
    messages = [shape(message)] * n_sub if len(pieces) > 1 else [shape((n_sub,) + message)]
    keep, send, *messages = call(
        functools.partial(main_kernel, len(pieces), len(messages)),
        [shape((8, 80, hidden))] * 2 + messages,
        [SMEM] * 2 + [VMEM] * (len(pieces) + 11),
        place,
        owner,
        *pieces,
        *early,
        scratch=[pltpu.VMEM((cells, hidden), BF16)] * 4
        + [
            pltpu.VMEM((groups, entries, channels), BF16),
            pltpu.VMEM((groups, entries, hidden), BF16),
            pltpu.VMEM((n_sub, block_rows, channels), BF16),
            pltpu.VMEM((groups, entries, hidden), F32),
            pltpu.VMEM((cells, hidden), F32),
            pltpu.VMEM((n_sub, block_rows // 4, hidden), BF16),
            pltpu.VMEM((8, hidden), F32),
        ],
        flops=1 << 31,
        limit=32 * 1024 * 1024,
    )
    return keep, send, messages


def swap(value, axis, mask, size):
    return lax.ppermute(value, axis, [(i, i ^ mask) for i in range(size)])


def on_block(surface, owner, local, count, entry_row, entry_cell, arrays):
    region, me = lax.axis_index("region"), lax.axis_index("sub")
    core, chip = region % 2, region // 2
    n_sub = owner.shape[0]
    block_rows = entry_row.shape[1] // n_sub
    channels = surface.shape[1]
    hidden = arrays[1].shape[1]
    along_z = range(1, n_sub)

    request = jnp.concatenate([owner, local]).reshape(1, 2 * n_sub)
    requests = [request] + [swap(request, "sub", m, n_sub) for m in along_z]
    *blocks, ids = call(
        serve_kernel,
        [shape((block_rows, channels))] * n_sub + [shape((n_sub,), jnp.int32)],
        [SMEM] * (n_sub + 1) + [HBM],
        me.reshape(1),
        *requests,
        pltpu.with_memory_space_constraint(surface, pltpu.HBM),
        out_specs=[VMEM] * n_sub + [SMEM],
        scratch=[pltpu.SemaphoreType.DMA((n_sub,))],
    )
    blocks = [blocks[0]] + [swap(blocks[m], "sub", m, n_sub) for m in along_z]
    early = prepare(count, ids, entry_row, entry_cell, n_sub, arrays)
    keep, send, messages = compute(jnp.stack([core, me]), owner, blocks, early, n_sub)
    got = swap(send, "region", 1, 4)
    keep, send = call(
        halve_kernel, [shape((4, 80, hidden))] * 2, [SMEM, VMEM, VMEM], chip.reshape(1), keep, got
    )
    got = swap(send, "region", 2, 4)
    messages = [messages[0]] + [swap(messages[m], "sub", m, n_sub) for m in along_z]
    terms = call(
        label_kernel,
        shape((n_sub,) + messages[0].shape),
        [SMEM] + [VMEM] * n_sub,
        ids,
        *messages,
    )
    shards = call(
        split_kernel,
        [shape((80, hidden))] * n_sub,
        [SMEM, VMEM, VMEM] + [ANY] * 3,
        me.reshape(1),
        keep,
        got,
        *messages[1:],
    )
    shards = [shards[0]] + [swap(shards[m], "sub", m, n_sub) for m in along_z]
    terms_x = swap(terms, "region", 2, 4)
    total = call(sum_kernel, shape((80, hidden)), [ANY] + [VMEM] * n_sub, terms_x, *shards)
    totals = [total] + [swap(total, "sub", m, n_sub) for m in along_z]
    terms = [terms, terms_x, swap(terms, "region", 1, 4), swap(terms_x, "region", 1, 4)]
    own = call(join_kernel, shape((n_sub, 80, hidden)), [VMEM] * n_sub, *totals)
    over_x = swap(own, "region", 2, 4)
    over_core = swap(own, "region", 1, 4)
    over_both = swap(over_x, "region", 1, 4)
    surf, wenc, benc, win, wmid, b1, wout, b2 = call(
        final_kernel,
        [
            shape((surface.shape[0] // block_rows, block_rows, channels), F32),
            shape((128, hidden)),
            shape((1, hidden), F32),
            shape((128, hidden)),
            shape((512, hidden)),
            shape((1, hidden), F32),
            shape((512, hidden)),
            shape((1, hidden), F32),
        ],
        [SMEM] + [VMEM] * 8,
        jnp.stack([core, chip, me]),
        own,
        over_x,
        over_core,
        over_both,
        *terms,
    )
    return (
        surf.reshape(surface.shape),
        wenc,
        benc.reshape(hidden),
        win,
        wmid,
        b1.reshape(hidden),
        wout,
        b2.reshape(hidden),
    )


def on_any(surface, owner, local, count, entry_row, entry_cell, arrays):
    n_sub = owner.shape[0]
    block_rows = entry_row.shape[1] // n_sub
    channels = surface.shape[1]
    hidden = arrays[1].shape[1]
    to_all = functools.partial(lax.all_to_all, axis_name="sub", split_axis=0, concat_axis=0, tiled=True)
    wanted = jnp.zeros((n_sub,), jnp.int32).at[owner].set(local)
    asked = to_all(wanted)
    stored = surface.reshape(surface.shape[0] // block_rows, block_rows, channels)
    fetched = to_all(jnp.take(stored, asked, axis=0))
    keep, send, (messages,) = compute(
        jnp.zeros((2,), jnp.int32),
        owner,
        [fetched],
        prepare(count, asked, entry_row, entry_cell, n_sub, arrays),
        n_sub,
    )
    bias = messages[0, block_rows // 4 :].astype(F32)
    bias = bias[0:8] + bias[8:16]
    surf = to_all(messages[:, : block_rows // 4]).astype(F32).reshape(n_sub, block_rows // 4, 4, channels)
    surf = surf.transpose(0, 2, 1, 3).reshape(n_sub, block_rows, channels)
    surf = jnp.zeros(stored.shape, F32).at[asked].add(surf).reshape(surface.shape)
    shards, bias = lax.psum(
        (jnp.concatenate([keep, send]).astype(F32), bias), ("region", "sub")
    )
    shards = shards.astype(BF16)
    small = shards[:, 64:80].reshape(256, hidden)
    return (
        lax.psum(surf, "region"),
        small[128:],
        bias[0],
        small[:128],
        shards[:, 32:64].reshape(512, hidden),
        bias[1],
        shards[:, 0:32].reshape(512, hidden),
        bias[2],
    )


def per_device(
    vol_feat,
    cotangent,
    surface,
    enc_weight,
    enc_bias,
    in_weight,
    mid_weight,
    first_bias,
    out_weight,
    second_bias,
    block_owner,
    block_local,
    block_count,
    entry_row,
    entry_cell,
):
    arrays = (
        vol_feat,
        cotangent,
        enc_weight,
        enc_bias,
        in_weight,
        mid_weight,
        first_bias,
        out_weight,
        second_bias,
    )
    small = lax.axis_size("region") == 4 and lax.axis_size("sub") == 4
    run = on_block if small else on_any
    return run(
        surface, block_owner[0], block_local[0], block_count, entry_row, entry_cell, arrays
    )


def solution(mesh):
    by_cell = P(("case", "region", "sub"), None)
    in_specs = (
        (by_cell, by_cell, P(("case", "sub"), None))
        + (P(),) * 7
        + (by_cell, by_cell, P(("case", "region", "sub")), by_cell, by_cell)
    )
    rows, line = P("case", None), P("case")
    out_specs = (P(("case", "sub"), None), rows, line, rows, rows, line, rows, line)
    return jax.shard_map(
        per_device, mesh=mesh, in_specs=in_specs, out_specs=out_specs, check_vma=False
    )
```

time: 71.7 us -> 69.5 us (0.969)
  local copies, waits for them, and re-layouts: 2.02 us -> 0.66 us
    unnamed x14 -> x4, local copies, waits for them, and re-layouts: 2.02 us -> 0.66 us
    pallas_call x10 -> x9, Pallas kernels: 13.1 us -> 13.1 us  [call(): pl.pallas_call(kernel, out_shape=out_shape, in_specs=in_specs, out_specs=...]
  transfers between devices with their start and end apart: 23 -> 23, of which waited for: 14 -> 15; matrix products, arithmetic and copies ran while one was open for 0% -> 0% of each run, Pallas kernels for 5% -> 4%
where the time goes in v3:
time: 69.5 us; the launch traced here: 69.2 us
  starting transfers between devices  27.7 us (40%)
  waiting for transfers between devices  26.1 us (38%)
  Pallas kernels  13.1 us (19%)
  between operations  1.43 us (2%)
    ppermute x23, starting transfers between devices, swap(): return lax.ppermute(value, axis, [(i, i ^ mask) for i in range(size)])  27.7 us
    ppermute x23, waiting for transfers between devices, swap(): return lax.ppermute(value, axis, [(i, i ^ mask) for i in range(size)])  26.1 us
    pallas_call x9, Pallas kernels, call(): pl.pallas_call(kernel, out_shape=out_shape, in_specs=in_specs, out_specs=...  13.1 us
  transfers between devices with their start and end apart: 23, of which 15 were waited for; matrix products, arithmetic and copies ran while one was open for 0% of the time, Pallas kernels for 4%

profile of v3, /device:TPU:0, one launch (start us, length us, event | category | flops | bytes accessed | tf_op | source)
XLA Modules:
  0.0 69.2 jit_solution(12030734233579330890)
XLA Ops:
  0.6 0.0 copy-start
  0.6 0.0 copy-start.1
  0.7 0.6 copy-done
  1.3 0.0 copy-done.1
  1.3 0.1 add_bitcast_fusion.refs_0_
  1.4 5.0 %collective-permute-start.2 = (s32[1,8]{1,0:T(1,128)S(1)}, s32[1,8]{1,0:T(1,128)S(1)}, u32[]{:S(2)}, u32[]{:S(2)}) collective-permute-start(s32[1,8]{1,0:T(1,128)S(1)} %add_bitcast_fusion.refs_0_), channel_id=1, source_target_pairs={{0,3},{1,2},{2,1},{3,0},{4,7},{5,6},{6,5},{7,4},{8,11},{9,10},{10,... | collective-permute-start | bytes 104 | tf_op jit(solution)/shard_map/ppermute | solution.py:390
  6.4 0.0 collective-permute-start.1
  6.4 0.6 collective-permute-start
  7.7 0.1 pad_add_fusion.1.place_ref
  7.8 0.1 collective-permute-done.2.refs_3_
  7.9 2.9 %collective-permute-done.1.refs_2_ = s32[1,8]{1,0:T(1,128)S(1)} collective-permute-done((s32[1,8]{1,0:T(1,128)S(1)}, s32[1,8]{1,0:T(1,128)S(1)}, u32[]{:S(2)}, u32[]{:S(2)}) %collective-permute-start.1) | collective-permute-done | bytes 64 | tf_op jit(solution)/shard_map/ppermute | solution.py:390
  10.9 0.0 collective-permute-done.refs_1_
  10.9 2.0 %shard_map.206 = (bf16[128,128]{1,0:T(8,128)(2,1)S(1)}, bf16[128,128]{1,0:T(8,128)(2,1)S(1)}, bf16[128,128]{1,0:T(8,128)(2,1)S(1)}, bf16[128,128]{1,0:T(8,128)(2,1)S(1)}, s32[4]{0:T(128)S(1)}) custom-call(s32[1]{0:T(128)} %bitcast.2.me_ref.place_ref, s32[1,8]{1,0:T(1,128)S(1)} %add_bitcast_fusion.refs_0_, s32[1,8]{1,0:T(1,128)S(1)} %collective-permute-done.refs_1_, ...), custom_call_target="tpu_custom_call" | custom-call | bytes 1048576 | tf_op jit(solution)/shard_map/pallas_call | solution.py:314
  12.9 0.1 collective-permute-start.3
  13.0 2.1 %collective-permute-start.4 = (bf16[128,128]{1,0:T(8,128)(2,1)S(1)}, bf16[128,128]{1,0:T(8,128)(2,1)S(1)}, u32[]{:S(2)}, u32[]{:S(2)}) collective-permute-start(bf16[128,128]{1,0:T(8,128)(2,1)S(1)} %get-tuple-element.47), channel_id=1, source_target_pairs={{0,2},{1,3},{2,0},{3,1},{4,6},{5,7},{6,4},{7,5},{8,10},{9,11},{10,... | collective-permute-start | bytes 98312 | tf_op jit(solution)/shard_map/ppermute | solution.py:390
  15.1 2.3 %collective-permute-start.5 = (bf16[128,128]{1,0:T(8,128)(2,1)S(1)}, bf16[128,128]{1,0:T(8,128)(2,1)S(1)}, u32[]{:S(2)}, u32[]{:S(2)}) collective-permute-start(bf16[128,128]{1,0:T(8,128)(2,1)S(1)} %get-tuple-element.48), channel_id=1, source_target_pairs={{0,3},{1,2},{2,1},{3,0},{4,7},{5,6},{6,5},{7,4},{8,11},{9,10},{10,... | collective-permute-start | bytes 98312 | tf_op jit(solution)/shard_map/ppermute | solution.py:390
  17.3 2.2 %shard_map.207 = (bf16[512,128]{1,0:T(8,128)(2,1)S(1)}, bf16[128,512]{1,0:T(8,128)(2,1)S(1)}, bf16[512,512]{1,0:T(8,128)(2,1)S(1)}, bf16[512,512]{1,0:T(8,128)(2...) custom-call(s32[1]{0:T(128)S(6)} %copy.23.count_ref, ...), custom_call_target="tpu_custom_call" | custom-call | flops 1073741824 | bytes 1048576 | tf_op jit(solution)/shard_map/pallas_call | solution.py:314
  19.6 0.0 collective-permute-done.3.refs_1_
  19.6 0.0 collective-permute-done.4.refs_2_
  19.6 1.2 %collective-permute-done.5.refs_3_ = bf16[128,128]{1,0:T(8,128)(2,1)S(1)} collective-permute-done((bf16[128,128]{1,0:T(8,128)(2,1)S(1)}, bf16[128,128]{1,0:T(8,128)(2,1)S(1)}, u32[]{:S(2)}, u32[]{:S(2)}) %collective-permute-start.5) | collective-permute-done | bytes 32800 | tf_op jit(solution)/shard_map/ppermute | solution.py:390
  20.8 5.6 %shard_map.208 = (bf16[8,80,512]{2,1,0:T(8,128)(2,1)S(1)}, bf16[8,80,512]{2,1,0:T(8,128)(2,1)S(1)}, bf16[48,512]{1,0:T(8,128)(2,1)S(1)}, bf16[48,512]{1,0:T(8,12...) custom-call(s32[2]{0:T(128)S(1)} %pad_add_fusion.1.place_ref, s32[4]{0:T(128)S(1)} %bitcast.17, ...), custom_call_target="tpu_custom_call" | custom-call | flops 2147483648 | bytes 1048576 | tf_op jit(solution)/shard_map/pallas_call | solution.py:314
  26.5 0.1 collective-permute-start.10
  26.5 2.1 %collective-permute-done.10.got_ref = bf16[8,80,512]{2,1,0:T(8,128)(2,1)S(1)} collective-permute-done((bf16[8,80,512]{2,1,0:T(8,128)(2,1)S(1)}, bf16[8,80,512]{2,1,0:T(8,128)(2,1)S(1)}, u32[]{:S(2)}, u32[]{:S(2)}) %collective-permute-start.10) | collective-permute-done | bytes 655392 | tf_op jit(solution)/shard_map/ppermute | solution.py:390
  28.6 0.2 shard_map.210
  28.8 1.5 %collective-permute-start.11 = (bf16[4,80,512]{2,1,0:T(8,128)(2,1)S(1)}, bf16[4,80,512]{2,1,0:T(8,128)(2,1)S(1)}, u32[]{:S(2)}, u32[]{:S(2)}) collective-permute-start(bf16[4,80,512]{2,1,0:T(8,128)(2,1)S(1)} %get-tuple-element.67), channel_id=1, source_target_pairs={{0,8},{4,12},{8,0},{12,4},{1,9},{5,13},{9,1},{13,5},{2,10},{6,14},... | collective-permute-start | bytes 983048 | tf_op jit(solution)/shard_map/ppermute | solution.py:390
  30.3 0.2 collective-permute-start.6
  30.4 2.7 %collective-permute-start.7 = (bf16[48,512]{1,0:T(8,128)(2,1)S(1)}, bf16[48,512]{1,0:T(8,128)(2,1)S(1)}, u32[]{:S(2)}, u32[]{:S(2)}) collective-permute-start(bf16[48,512]{1,0:T(8,128)(2,1)S(1)} %get-tuple-element.62), channel_id=1, source_target_pairs={{0,2},{1,3},{2,0},{3,1},{4,6},{5,7},{6,4},{7,5},{8,10},{9,11},{10,... | collective-permute-start | bytes 147464 | tf_op jit(solution)/shard_map/ppermute | solution.py:390
  33.2 1.5 %collective-permute-start.8 = (bf16[48,512]{1,0:T(8,128)(2,1)S(1)}, bf16[48,512]{1,0:T(8,128)(2,1)S(1)}, u32[]{:S(2)}, u32[]{:S(2)}) collective-permute-start(bf16[48,512]{1,0:T(8,128)(2,1)S(1)} %get-tuple-element.63), channel_id=1, source_target_pairs={{0,3},{1,2},{2,1},{3,0},{4,7},{5,6},{6,5},{7,4},{8,11},{9,10},{10,... | collective-permute-start | bytes 147464 | tf_op jit(solution)/shard_map/ppermute | solution.py:390
  34.7 0.0 collective-permute-done.6.refs_1_.refs_0_
  34.7 2.7 %collective-permute-done.7.refs_2_.refs_1_ = bf16[48,512]{1,0:T(8,128)(2,1)S(1)} collective-permute-done((bf16[48,512]{1,0:T(8,128)(2,1)S(1)}, bf16[48,512]{1,0:T(8,128)(2,1)S(1)}, u32[]{:S(2)}, u32[]{:S(2)}) %collective-permute-start.7) | collective-permute-done | bytes 49184 | tf_op jit(solution)/shard_map/ppermute | solution.py:390
  37.4 1.6 %collective-permute-done.8.refs_3_.refs_2_ = bf16[48,512]{1,0:T(8,128)(2,1)S(1)} collective-permute-done((bf16[48,512]{1,0:T(8,128)(2,1)S(1)}, bf16[48,512]{1,0:T(8,128)(2,1)S(1)}, u32[]{:S(2)}, u32[]{:S(2)}) %collective-permute-start.8) | collective-permute-done | bytes 49184 | tf_op jit(solution)/shard_map/ppermute | solution.py:390
  39.1 0.6 shard_map.209.refs_0_
  39.6 0.6 collective-permute-start.9
  40.2 0.0 collective-permute-done.11.got_ref
  40.2 0.1 shard_map.211
  40.3 0.1 collective-permute-start.12
  40.4 2.1 %collective-permute-start.13 = (bf16[80,512]{1,0:T(8,128)(2,1)S(1)}, bf16[80,512]{1,0:T(8,128)(2,1)S(1)}, u32[]{:S(2)}, u32[]{:S(2)}) collective-permute-start(bf16[80,512]{1,0:T(8,128)(2,1)S(1)} %get-tuple-element.70), channel_id=1, source_target_pairs={{0,2},{1,3},{2,0},{3,1},{4,6},{5,7},{6,4},{7,5},{8,10},{9,11},{10,... | collective-permute-start | bytes 245768 | tf_op jit(solution)/shard_map/ppermute | solution.py:390
  42.5 2.3 %collective-permute-start.14 = (bf16[80,512]{1,0:T(8,128)(2,1)S(1)}, bf16[80,512]{1,0:T(8,128)(2,1)S(1)}, u32[]{:S(2)}, u32[]{:S(2)}) collective-permute-start(bf16[80,512]{1,0:T(8,128)(2,1)S(1)} %get-tuple-element.71), channel_id=1, source_target_pairs={{0,3},{1,2},{2,1},{3,0},{4,7},{5,6},{6,5},{7,4},{8,11},{9,10},{10,... | collective-permute-start | bytes 245768 | tf_op jit(solution)/shard_map/ppermute | solution.py:390
  44.7 0.6 collective-permute-done.9._.refs_1_
  45.4 0.0 collective-permute-done.12.refs_1_
  45.4 2.0 %collective-permute-done.13.refs_2_ = bf16[80,512]{1,0:T(8,128)(2,1)S(1)} collective-permute-done((bf16[80,512]{1,0:T(8,128)(2,1)S(1)}, bf16[80,512]{1,0:T(8,128)(2,1)S(1)}, u32[]{:S(2)}, u32[]{:S(2)}) %collective-permute-start.13) | collective-permute-done | bytes 81952 | tf_op jit(solution)/shard_map/ppermute | solution.py:390
  47.4 1.5 %collective-permute-done.14.refs_3_ = bf16[80,512]{1,0:T(8,128)(2,1)S(1)} collective-permute-done((bf16[80,512]{1,0:T(8,128)(2,1)S(1)}, bf16[80,512]{1,0:T(8,128)(2,1)S(1)}, u32[]{:S(2)}, u32[]{:S(2)}) %collective-permute-start.14) | collective-permute-done | bytes 81952 | tf_op jit(solution)/shard_map/ppermute | solution.py:390
  48.9 2.3 %collective-permute-start.17 = (bf16[80,512]{1,0:T(8,128)(2,1)S(1)}, bf16[80,512]{1,0:T(8,128)(2,1)S(1)}, u32[]{:S(2)}, u32[]{:S(2)}) collective-permute-start(bf16[80,512]{1,0:T(8,128)(2,1)S(1)} %shard_map.212.refs_0_), channel_id=1, source_target_pairs={{0,3},{1,2},{2,1},{3,0},{4,7},{5,6},{6,5},{7,4},{8,11},{9,10},{10,... | collective-permute-start | bytes 245768 | tf_op jit(solution)/shard_map/ppermute | solution.py:390
  51.2 1.0 %collective-permute-start.16 = (bf16[80,512]{1,0:T(8,128)(2,1)S(1)}, bf16[80,512]{1,0:T(8,128)(2,1)S(1)}, u32[]{:S(2)}, u32[]{:S(2)}) collective-permute-start(bf16[80,512]{1,0:T(8,128)(2,1)S(1)} %shard_map.212.refs_0_), channel_id=1, source_target_pairs={{0,2},{1,3},{2,0},{3,1},{4,6},{5,7},{6,4},{7,5},{8,10},{9,11},{10,... | collective-permute-start | bytes 245768 | tf_op jit(solution)/shard_map/ppermute | solution.py:390
  52.2 1.2 %collective-permute-start.15 = (bf16[80,512]{1,0:T(8,128)(2,1)S(1)}, bf16[80,512]{1,0:T(8,128)(2,1)S(1)}, u32[]{:S(2)}, u32[]{:S(2)}) collective-permute-start(bf16[80,512]{1,0:T(8,128)(2,1)S(1)} %shard_map.212.refs_0_), channel_id=1, source_target_pairs={{0,1},{1,0},{2,3},{3,2},{4,5},{5,4},{6,7},{7,6},{8,9},{9,8},{10,11... | collective-permute-start | bytes 245768 | tf_op jit(solution)/shard_map/ppermute | solution.py:390
  53.3 2.0 %collective-permute-done.17.refs_3_ = bf16[80,512]{1,0:T(8,128)(2,1)S(1)} collective-permute-done((bf16[80,512]{1,0:T(8,128)(2,1)S(1)}, bf16[80,512]{1,0:T(8,128)(2,1)S(1)}, u32[]{:S(2)}, u32[]{:S(2)}) %collective-permute-start.17) | collective-permute-done | bytes 81952 | tf_op jit(solution)/shard_map/ppermute | solution.py:390
  55.3 2.0 %collective-permute-done.16.refs_2_ = bf16[80,512]{1,0:T(8,128)(2,1)S(1)} collective-permute-done((bf16[80,512]{1,0:T(8,128)(2,1)S(1)}, bf16[80,512]{1,0:T(8,128)(2,1)S(1)}, u32[]{:S(2)}, u32[]{:S(2)}) %collective-permute-start.16) | collective-permute-done | bytes 81952 | tf_op jit(solution)/shard_map/ppermute | solution.py:390
  57.3 0.2 collective-permute-done.15.refs_1_
  57.5 1.6 %collective-permute-start.18 = (bf16[4,80,512]{2,1,0:T(8,128)(2,1)S(1)}, bf16[4,80,512]{2,1,0:T(8,128)(2,1)S(1)}, u32[]{:S(2)}, u32[]{:S(2)}) collective-permute-start(bf16[4,80,512]{2,1,0:T(8,128)(2,1)S(1)} %shard_map.213.own), channel_id=1, source_target_pairs={{0,8},{4,12},{8,0},{12,4},{1,9},{5,13},{9,1},{13,5},{2,10},{6,14},... | collective-permute-start | bytes 983048 | tf_op jit(solution)/shard_map/ppermute | solution.py:390
  59.1 0.0 collective-permute-start.19
  59.1 5.5 %collective-permute-done.18.over_x = bf16[4,80,512]{2,1,0:T(8,128)(2,1)S(1)} collective-permute-done((bf16[4,80,512]{2,1,0:T(8,128)(2,1)S(1)}, bf16[4,80,512]{2,1,0:T(8,128)(2,1)S(1)}, u32[]{:S(2)}, u32[]{:S(2)}) %collective-permute-start.18) | collective-permute-done | bytes 327712 | tf_op jit(solution)/shard_map/ppermute | solution.py:390
  64.6 0.0 collective-permute-start.20
  64.6 0.5 collective-permute-start.21
  65.2 0.0 collective-permute-start.22
  65.2 0.1 pad_add_fusion.place_ref
  65.2 1.3 %collective-permute-done.21.refs_2_ = bf16[4,48,512]{2,1,0:T(8,128)(2,1)S(1)} collective-permute-done((bf16[4,48,512]{2,1,0:T(8,128)(2,1)S(1)}, bf16[4,48,512]{2,1,0:T(8,128)(2,1)S(1)}, u32[]{:S(2)}, u32[]{:S(2)}) %collective-permute-start.21) | collective-permute-done | bytes 196640 | tf_op jit(solution)/shard_map/ppermute | solution.py:390
  66.6 0.3 collective-permute-done.22.refs_3_
  66.8 0.0 collective-permute-done.19.over_core
  66.8 0.0 collective-permute-done.20.over_both
  66.8 2.4 %shard_map.214 = (f32[16,128,128]{2,1,0:T(8,128)}, bf16[128,512]{1,0:T(8,128)(2,1)}, f32[1,512]{1,0:T(1,128)}, bf16[128,512]{1,0:T(8,128)(2,1)}, bf16[512,512]{1...) custom-call(s32[3]{0:T(128)S(1)} %pad_add_fusion.place_ref, ...), custom_call_target="tpu_custom_call" | custom-call | bytes 1048576 | tf_op jit(solution)/shard_map/pallas_call | solution.py:314
  (2 shorter events, 0.1 us)
Async XLA Ops:
  0.6 0.7 copy-start
  0.6 0.7 copy-start.1
  1.4 6.6 %collective-permute-start.2 = (s32[1,8]{1,0:T(1,128)S(1)}, s32[1,8]{1,0:T(1,128)S(1)}, u32[]{:S(2)}, u32[]{:S(2)}) collective-permute-start(s32[1,8]{1,0:T(1,128)S(1)} %add_bitcast_fusion.refs_0_), channel_id=1, source_target_pairs={{0,3},{1,2},{2,1},{3,0},{4,7},{5,6},{6,5},{7,4},{8,11},{9,10},{10,... | collective-permute-start | bytes 104 | tf_op jit(solution)/shard_map/ppermute | solution.py:390
  6.4 4.4 %collective-permute-start.1 = (s32[1,8]{1,0:T(1,128)S(1)}, s32[1,8]{1,0:T(1,128)S(1)}, u32[]{:S(2)}, u32[]{:S(2)}) collective-permute-start(s32[1,8]{1,0:T(1,128)S(1)} %add_bitcast_fusion.refs_0_), channel_id=1, source_target_pairs={{0,2},{1,3},{2,0},{3,1},{4,6},{5,7},{6,4},{7,5},{8,10},{9,11},{10,... | collective-permute-start | bytes 104 | tf_op jit(solution)/shard_map/ppermute | solution.py:390
  6.4 4.4 %collective-permute-start = (s32[1,8]{1,0:T(1,128)S(1)}, s32[1,8]{1,0:T(1,128)S(1)}, u32[]{:S(2)}, u32[]{:S(2)}) collective-permute-start(s32[1,8]{1,0:T(1,128)S(1)} %add_bitcast_fusion.refs_0_), channel_id=1, source_target_pairs={{0,1},{1,0},{2,3},{3,2},{4,5},{5,4},{6,7},{7,6},{8,9},{9,8},{10,11... | collective-permute-start | bytes 104 | tf_op jit(solution)/shard_map/ppermute | solution.py:390
  12.9 6.7 %collective-permute-start.3 = (bf16[128,128]{1,0:T(8,128)(2,1)S(1)}, bf16[128,128]{1,0:T(8,128)(2,1)S(1)}, u32[]{:S(2)}, u32[]{:S(2)}) collective-permute-start(bf16[128,128]{1,0:T(8,128)(2,1)S(1)} %get-tuple-element.46), channel_id=1, source_target_pairs={{0,1},{1,0},{2,3},{3,2},{4,5},{5,4},{6,7},{7,6},{8,9},{9,8},{10,11... | collective-permute-start | bytes 98312 | tf_op jit(solution)/shard_map/ppermute | solution.py:390
  13.0 6.6 %collective-permute-start.4 = (bf16[128,128]{1,0:T(8,128)(2,1)S(1)}, bf16[128,128]{1,0:T(8,128)(2,1)S(1)}, u32[]{:S(2)}, u32[]{:S(2)}) collective-permute-start(bf16[128,128]{1,0:T(8,128)(2,1)S(1)} %get-tuple-element.47), channel_id=1, source_target_pairs={{0,2},{1,3},{2,0},{3,1},{4,6},{5,7},{6,4},{7,5},{8,10},{9,11},{10,... | collective-permute-start | bytes 98312 | tf_op jit(solution)/shard_map/ppermute | solution.py:390
  15.1 5.7 %collective-permute-start.5 = (bf16[128,128]{1,0:T(8,128)(2,1)S(1)}, bf16[128,128]{1,0:T(8,128)(2,1)S(1)}, u32[]{:S(2)}, u32[]{:S(2)}) collective-permute-start(bf16[128,128]{1,0:T(8,128)(2,1)S(1)} %get-tuple-element.48), channel_id=1, source_target_pairs={{0,3},{1,2},{2,1},{3,0},{4,7},{5,6},{6,5},{7,4},{8,11},{9,10},{10,... | collective-permute-start | bytes 98312 | tf_op jit(solution)/shard_map/ppermute | solution.py:390
  26.5 2.2 %collective-permute-start.10 = (bf16[8,80,512]{2,1,0:T(8,128)(2,1)S(1)}, bf16[8,80,512]{2,1,0:T(8,128)(2,1)S(1)}, u32[]{:S(2)}, u32[]{:S(2)}) collective-permute-start(bf16[8,80,512]{2,1,0:T(8,128)(2,1)S(1)} %get-tuple-element.65), channel_id=1, source_target_pairs={{0,4},{4,0},{8,12},{12,8},{1,5},{5,1},{9,13},{13,9},{2,6},{6,2},{1... | collective-permute-start | bytes 1966088 | tf_op jit(solution)/shard_map/ppermute | solution.py:390
  28.8 11.4 %collective-permute-start.11 = (bf16[4,80,512]{2,1,0:T(8,128)(2,1)S(1)}, bf16[4,80,512]{2,1,0:T(8,128)(2,1)S(1)}, u32[]{:S(2)}, u32[]{:S(2)}) collective-permute-start(bf16[4,80,512]{2,1,0:T(8,128)(2,1)S(1)} %get-tuple-element.67), channel_id=1, source_target_pairs={{0,8},{4,12},{8,0},{12,4},{1,9},{5,13},{9,1},{13,5},{2,10},{6,14},... | collective-permute-start | bytes 983048 | tf_op jit(solution)/shard_map/ppermute | solution.py:390
  30.3 4.4 %collective-permute-start.6 = (bf16[48,512]{1,0:T(8,128)(2,1)S(1)}, bf16[48,512]{1,0:T(8,128)(2,1)S(1)}, u32[]{:S(2)}, u32[]{:S(2)}) collective-permute-start(bf16[48,512]{1,0:T(8,128)(2,1)S(1)} %get-tuple-element.61), channel_id=1, source_target_pairs={{0,1},{1,0},{2,3},{3,2},{4,5},{5,4},{6,7},{7,6},{8,9},{9,8},{10,11... | collective-permute-start | bytes 147464 | tf_op jit(solution)/shard_map/ppermute | solution.py:390
  30.4 7.0 %collective-permute-start.7 = (bf16[48,512]{1,0:T(8,128)(2,1)S(1)}, bf16[48,512]{1,0:T(8,128)(2,1)S(1)}, u32[]{:S(2)}, u32[]{:S(2)}) collective-permute-start(bf16[48,512]{1,0:T(8,128)(2,1)S(1)} %get-tuple-element.62), channel_id=1, source_target_pairs={{0,2},{1,3},{2,0},{3,1},{4,6},{5,7},{6,4},{7,5},{8,10},{9,11},{10,... | collective-permute-start | bytes 147464 | tf_op jit(solution)/shard_map/ppermute | solution.py:390
  33.2 5.9 %collective-permute-start.8 = (bf16[48,512]{1,0:T(8,128)(2,1)S(1)}, bf16[48,512]{1,0:T(8,128)(2,1)S(1)}, u32[]{:S(2)}, u32[]{:S(2)}) collective-permute-start(bf16[48,512]{1,0:T(8,128)(2,1)S(1)} %get-tuple-element.63), channel_id=1, source_target_pairs={{0,3},{1,2},{2,1},{3,0},{4,7},{5,6},{6,5},{7,4},{8,11},{9,10},{10,... | collective-permute-start | bytes 147464 | tf_op jit(solution)/shard_map/ppermute | solution.py:390
  39.6 5.7 %collective-permute-start.9 = (bf16[4,48,512]{2,1,0:T(8,128)(2,1)S(1)}, bf16[4,48,512]{2,1,0:T(8,128)(2,1)S(1)}, u32[]{:S(2)}, u32[]{:S(2)}) collective-permute-start(bf16[4,48,512]{2,1,0:T(8,128)(2,1)S(1)} %shard_map.209.refs_0_), channel_id=1, source_target_pairs={{0,8},{4,12},{8,0},{12,4},{1,9},{5,13},{9,1},{13,5},{2,10},{6,14},... | collective-permute-start | bytes 589832 | tf_op jit(solution)/shard_map/ppermute | solution.py:390
  40.3 5.1 %collective-permute-start.12 = (bf16[80,512]{1,0:T(8,128)(2,1)S(1)}, bf16[80,512]{1,0:T(8,128)(2,1)S(1)}, u32[]{:S(2)}, u32[]{:S(2)}) collective-permute-start(bf16[80,512]{1,0:T(8,128)(2,1)S(1)} %get-tuple-element.69), channel_id=1, source_target_pairs={{0,1},{1,0},{2,3},{3,2},{4,5},{5,4},{6,7},{7,6},{8,9},{9,8},{10,11... | collective-permute-start | bytes 245768 | tf_op jit(solution)/shard_map/ppermute | solution.py:390
  40.4 7.0 %collective-permute-start.13 = (bf16[80,512]{1,0:T(8,128)(2,1)S(1)}, bf16[80,512]{1,0:T(8,128)(2,1)S(1)}, u32[]{:S(2)}, u32[]{:S(2)}) collective-permute-start(bf16[80,512]{1,0:T(8,128)(2,1)S(1)} %get-tuple-element.70), channel_id=1, source_target_pairs={{0,2},{1,3},{2,0},{3,1},{4,6},{5,7},{6,4},{7,5},{8,10},{9,11},{10,... | collective-permute-start | bytes 245768 | tf_op jit(solution)/shard_map/ppermute | solution.py:390
  42.5 6.3 %collective-permute-start.14 = (bf16[80,512]{1,0:T(8,128)(2,1)S(1)}, bf16[80,512]{1,0:T(8,128)(2,1)S(1)}, u32[]{:S(2)}, u32[]{:S(2)}) collective-permute-start(bf16[80,512]{1,0:T(8,128)(2,1)S(1)} %get-tuple-element.71), channel_id=1, source_target_pairs={{0,3},{1,2},{2,1},{3,0},{4,7},{5,6},{6,5},{7,4},{8,11},{9,10},{10,... | collective-permute-start | bytes 245768 | tf_op jit(solution)/shard_map/ppermute | solution.py:390
  48.9 6.4 %collective-permute-start.17 = (bf16[80,512]{1,0:T(8,128)(2,1)S(1)}, bf16[80,512]{1,0:T(8,128)(2,1)S(1)}, u32[]{:S(2)}, u32[]{:S(2)}) collective-permute-start(bf16[80,512]{1,0:T(8,128)(2,1)S(1)} %shard_map.212.refs_0_), channel_id=1, source_target_pairs={{0,3},{1,2},{2,1},{3,0},{4,7},{5,6},{6,5},{7,4},{8,11},{9,10},{10,... | collective-permute-start | bytes 245768 | tf_op jit(solution)/shard_map/ppermute | solution.py:390
  51.2 6.1 %collective-permute-start.16 = (bf16[80,512]{1,0:T(8,128)(2,1)S(1)}, bf16[80,512]{1,0:T(8,128)(2,1)S(1)}, u32[]{:S(2)}, u32[]{:S(2)}) collective-permute-start(bf16[80,512]{1,0:T(8,128)(2,1)S(1)} %shard_map.212.refs_0_), channel_id=1, source_target_pairs={{0,2},{1,3},{2,0},{3,1},{4,6},{5,7},{6,4},{7,5},{8,10},{9,11},{10,... | collective-permute-start | bytes 245768 | tf_op jit(solution)/shard_map/ppermute | solution.py:390
  52.2 5.3 %collective-permute-start.15 = (bf16[80,512]{1,0:T(8,128)(2,1)S(1)}, bf16[80,512]{1,0:T(8,128)(2,1)S(1)}, u32[]{:S(2)}, u32[]{:S(2)}) collective-permute-start(bf16[80,512]{1,0:T(8,128)(2,1)S(1)} %shard_map.212.refs_0_), channel_id=1, source_target_pairs={{0,1},{1,0},{2,3},{3,2},{4,5},{5,4},{6,7},{7,6},{8,9},{9,8},{10,11... | collective-permute-start | bytes 245768 | tf_op jit(solution)/shard_map/ppermute | solution.py:390
  57.5 7.1 %collective-permute-start.18 = (bf16[4,80,512]{2,1,0:T(8,128)(2,1)S(1)}, bf16[4,80,512]{2,1,0:T(8,128)(2,1)S(1)}, u32[]{:S(2)}, u32[]{:S(2)}) collective-permute-start(bf16[4,80,512]{2,1,0:T(8,128)(2,1)S(1)} %shard_map.213.own), channel_id=1, source_target_pairs={{0,8},{4,12},{8,0},{12,4},{1,9},{5,13},{9,1},{13,5},{2,10},{6,14},... | collective-permute-start | bytes 983048 | tf_op jit(solution)/shard_map/ppermute | solution.py:390
  59.1 7.7 %collective-permute-start.19 = (bf16[4,80,512]{2,1,0:T(8,128)(2,1)S(1)}, bf16[4,80,512]{2,1,0:T(8,128)(2,1)S(1)}, u32[]{:S(2)}, u32[]{:S(2)}) collective-permute-start(bf16[4,80,512]{2,1,0:T(8,128)(2,1)S(1)} %shard_map.213.own), channel_id=1, source_target_pairs={{0,4},{4,0},{8,12},{12,8},{1,5},{5,1},{9,13},{13,9},{2,6},{6,2},{1... | collective-permute-start | bytes 983048 | tf_op jit(solution)/shard_map/ppermute | solution.py:390
  64.6 2.2 %collective-permute-start.20 = (bf16[4,80,512]{2,1,0:T(8,128)(2,1)S(1)}, bf16[4,80,512]{2,1,0:T(8,128)(2,1)S(1)}, u32[]{:S(2)}, u32[]{:S(2)}) collective-permute-start(bf16[4,80,512]{2,1,0:T(8,128)(2,1)S(1)} %collective-permute-done.18.over_x), channel_id=1, source_target_pairs={{0,4},{4,0},{8,12},{12,8},{1,5},{5,1},{9,13},{13,9},{2,6},{6,2},{1... | collective-permute-start | bytes 983048 | tf_op jit(solution)/shard_map/ppermute | solution.py:390
  64.6 1.9 %collective-permute-start.21 = (bf16[4,48,512]{2,1,0:T(8,128)(2,1)S(1)}, bf16[4,48,512]{2,1,0:T(8,128)(2,1)S(1)}, u32[]{:S(2)}, u32[]{:S(2)}) collective-permute-start(bf16[4,48,512]{2,1,0:T(8,128)(2,1)S(1)} %shard_map.209.refs_0_), channel_id=1, source_target_pairs={{0,4},{4,0},{8,12},{12,8},{1,5},{5,1},{9,13},{13,9},{2,6},{6,2},{1... | collective-permute-start | bytes 589832 | tf_op jit(solution)/shard_map/ppermute | solution.py:390
  65.2 1.7 %collective-permute-start.22 = (bf16[4,48,512]{2,1,0:T(8,128)(2,1)S(1)}, bf16[4,48,512]{2,1,0:T(8,128)(2,1)S(1)}, u32[]{:S(2)}, u32[]{:S(2)}) collective-permute-start(bf16[4,48,512]{2,1,0:T(8,128)(2,1)S(1)} %collective-permute-done.9._.refs_1_), channel_id=1, source_target_pairs={{0,4},{4,0},{8,12},{12,8},{1,5},{5,1},{9,13},{13,9},{2,6},{6,2},{1... | collective-permute-start | bytes 589832 | tf_op jit(solution)/shard_map/ppermute | solution.py:390

commit v4 on v3

--- a/solution.py
+++ b/solution.py
@@ -49,24 +49,17 @@
 
 
 def serve_kernel(me_ref, *refs):
-    count = (len(refs) - 3) // 2
+    count = (len(refs) - 2) // 2
     requests, surface, blocks = refs[:count], refs[count], refs[count + 1 : 2 * count + 1]
-    ids_ref, sems = refs[2 * count + 1], refs[2 * count + 2]
+    ids_ref = refs[2 * count + 1]
     rows = blocks[0].shape[0]
     me = me_ref[0]
-    copies = []
     for m, request in enumerate(requests):
         wanted = jnp.int32(0)
         for k in range(count):
             wanted = wanted + jnp.where(request[0, k] == me, request[0, count + k], 0)
         ids_ref[m] = wanted
-        copy = pltpu.make_async_copy(
-            surface.at[pl.ds(pl.multiple_of(wanted * rows, rows), rows), :], blocks[m], sems.at[m]
-        )
-        copy.start()
-        copies.append(copy)
-    for copy in copies:
-        copy.wait()
+        blocks[m][...] = surface[pl.ds(pl.multiple_of(wanted * rows, rows), rows), :]
 
 
 def fill(out, surf_ref, bias, m):
@@ -401,15 +394,15 @@
 
     request = jnp.concatenate([owner, local]).reshape(1, 2 * n_sub)
     requests = [request] + [swap(request, "sub", m, n_sub) for m in along_z]
+    near = swap(surface, "region", 1, 4)
     *blocks, ids = call(
         serve_kernel,
         [shape((block_rows, channels))] * n_sub + [shape((n_sub,), jnp.int32)],
-        [SMEM] * (n_sub + 1) + [HBM],
+        [SMEM] * (n_sub + 1) + [VMEM],
         me.reshape(1),
         *requests,
-        pltpu.with_memory_space_constraint(surface, pltpu.HBM),
+        near,
         out_specs=[VMEM] * n_sub + [SMEM],
-        scratch=[pltpu.SemaphoreType.DMA((n_sub,))],
     )
     blocks = [blocks[0]] + [swap(blocks[m], "sub", m, n_sub) for m in along_z]
     early = prepare(count, ids, entry_row, entry_cell, n_sub, arrays)

time: 69.5 us -> 68.7 us (0.988)
  Pallas kernels: 13.1 us -> 12.3 us
    pallas_call x9, Pallas kernels: 13.1 us -> 12.3 us  [call(): pl.pallas_call(kernel, out_shape=out_shape, in_specs=in_specs, out_specs=...]
    ppermute x23 -> x24, starting transfers between devices: 27.7 us -> 27.8 us  [swap(): return lax.ppermute(value, axis, [(i, i ^ mask) for i in range(size)])]
    ppermute x23 -> x24, waiting for transfers between devices: 26.1 us -> 26.1 us  [swap(): return lax.ppermute(value, axis, [(i, i ^ mask) for i in range(size)])]
  transfers between devices with their start and end apart: 23 -> 24, of which waited for: 15 -> 15; matrix products, arithmetic and copies ran while one was open for 0% -> 0% of each run, Pallas kernels for 4% -> 4%
where the time goes in v4:
time: 68.7 us; the launch traced here: 68.5 us
  starting transfers between devices  27.8 us (40%)
  waiting for transfers between devices  26.1 us (38%)
  Pallas kernels  12.3 us (18%)
  between operations  1.41 us (2%)
    ppermute x24, starting transfers between devices, swap(): return lax.ppermute(value, axis, [(i, i ^ mask) for i in range(size)])  27.8 us
    ppermute x24, waiting for transfers between devices, swap(): return lax.ppermute(value, axis, [(i, i ^ mask) for i in range(size)])  26.1 us
    pallas_call x9, Pallas kernels, call(): pl.pallas_call(kernel, out_shape=out_shape, in_specs=in_specs, out_specs=...  12.3 us
  transfers between devices with their start and end apart: 24, of which 15 were waited for; matrix products, arithmetic and copies ran while one was open for 0% of the time, Pallas kernels for 4%

profile of v4, /device:TPU:0, one launch (start us, length us, event | category | flops | bytes accessed | tf_op | source)
XLA Modules:
  0.0 68.5 jit_solution(8565794078219695944)
XLA Ops:
  0.6 0.5 collective-permute-start.3
  1.2 0.0 copy-start
  1.2 0.0 copy-start.1
  1.2 0.7 copy-done
  1.8 0.0 copy-done.1
  1.8 0.1 add_bitcast_fusion.refs_0_
  1.9 4.6 %collective-permute-start.2 = (s32[1,8]{1,0:T(1,128)S(1)}, s32[1,8]{1,0:T(1,128)S(1)}, u32[]{:S(2)}, u32[]{:S(2)}) collective-permute-start(s32[1,8]{1,0:T(1,128)S(1)} %add_bitcast_fusion.refs_0_), channel_id=1, source_target_pairs={{0,3},{1,2},{2,1},{3,0},{4,7},{5,6},{6,5},{7,4},{8,11},{9,10},{10,... | collective-permute-start | bytes 104 | tf_op jit(solution)/shard_map/ppermute | solution.py:383
  6.5 0.0 collective-permute-start.1
  6.5 0.6 collective-permute-start
  7.8 0.1 pad_add_fusion.1.place_ref
  7.9 0.1 collective-permute-done.2.refs_3_
  8.0 2.9 %collective-permute-done.1.refs_2_ = s32[1,8]{1,0:T(1,128)S(1)} collective-permute-done((s32[1,8]{1,0:T(1,128)S(1)}, s32[1,8]{1,0:T(1,128)S(1)}, u32[]{:S(2)}, u32[]{:S(2)}) %collective-permute-start.1) | collective-permute-done | bytes 64 | tf_op jit(solution)/shard_map/ppermute | solution.py:383
  10.9 0.0 collective-permute-done.refs_1_
  11.0 0.0 collective-permute-done.3.refs_4_
  11.0 1.2 %shard_map.206 = (bf16[128,128]{1,0:T(8,128)(2,1)S(1)}, bf16[128,128]{1,0:T(8,128)(2,1)S(1)}, bf16[128,128]{1,0:T(8,128)(2,1)S(1)}, bf16[128,128]{1,0:T(8,128)(2,1)S(1)}, s32[4]{0:T(128)S(1)}) custom-call(s32[1]{0:T(128)} %bitcast.2.me_ref.place_ref, s32[1,8]{1,0:T(1,128)S(1)} %add_bitcast_fusion.refs_0_, s32[1,8]{1,0:T(1,128)S(1)} %collective-permute-done.refs_1_, ...), custom_call_target="tpu_custom_call" | custom-call | bytes 1048576 | tf_op jit(solution)/shard_map/pallas_call | solution.py:307
  12.1 0.1 collective-permute-start.4
  12.2 2.1 %collective-permute-start.5 = (bf16[128,128]{1,0:T(8,128)(2,1)S(1)}, bf16[128,128]{1,0:T(8,128)(2,1)S(1)}, u32[]{:S(2)}, u32[]{:S(2)}) collective-permute-start(bf16[128,128]{1,0:T(8,128)(2,1)S(1)} %get-tuple-element.47), channel_id=1, source_target_pairs={{0,2},{1,3},{2,0},{3,1},{4,6},{5,7},{6,4},{7,5},{8,10},{9,11},{10,... | collective-permute-start | bytes 98312 | tf_op jit(solution)/shard_map/ppermute | solution.py:383
  14.3 2.3 %collective-permute-start.6 = (bf16[128,128]{1,0:T(8,128)(2,1)S(1)}, bf16[128,128]{1,0:T(8,128)(2,1)S(1)}, u32[]{:S(2)}, u32[]{:S(2)}) collective-permute-start(bf16[128,128]{1,0:T(8,128)(2,1)S(1)} %get-tuple-element.48), channel_id=1, source_target_pairs={{0,3},{1,2},{2,1},{3,0},{4,7},{5,6},{6,5},{7,4},{8,11},{9,10},{10,... | collective-permute-start | bytes 98312 | tf_op jit(solution)/shard_map/ppermute | solution.py:383
  16.6 2.2 %shard_map.207 = (bf16[512,128]{1,0:T(8,128)(2,1)S(1)}, bf16[128,512]{1,0:T(8,128)(2,1)S(1)}, bf16[512,512]{1,0:T(8,128)(2,1)S(1)}, bf16[512,512]{1,0:T(8,128)(2...) custom-call(s32[1]{0:T(128)S(6)} %copy.23.count_ref, ...), custom_call_target="tpu_custom_call" | custom-call | flops 1073741824 | bytes 1048576 | tf_op jit(solution)/shard_map/pallas_call | solution.py:307
  18.8 0.0 collective-permute-done.4.refs_1_
  18.8 0.0 collective-permute-done.5.refs_2_
  18.9 1.2 %collective-permute-done.6.refs_3_ = bf16[128,128]{1,0:T(8,128)(2,1)S(1)} collective-permute-done((bf16[128,128]{1,0:T(8,128)(2,1)S(1)}, bf16[128,128]{1,0:T(8,128)(2,1)S(1)}, u32[]{:S(2)}, u32[]{:S(2)}) %collective-permute-start.6) | collective-permute-done | bytes 32800 | tf_op jit(solution)/shard_map/ppermute | solution.py:383
  20.0 5.6 %shard_map.208 = (bf16[8,80,512]{2,1,0:T(8,128)(2,1)S(1)}, bf16[8,80,512]{2,1,0:T(8,128)(2,1)S(1)}, bf16[48,512]{1,0:T(8,128)(2,1)S(1)}, bf16[48,512]{1,0:T(8,12...) custom-call(s32[2]{0:T(128)S(1)} %pad_add_fusion.1.place_ref, s32[4]{0:T(128)S(1)} %bitcast.17, ...), custom_call_target="tpu_custom_call" | custom-call | flops 2147483648 | bytes 1048576 | tf_op jit(solution)/shard_map/pallas_call | solution.py:307
  25.7 0.1 collective-permute-start.11
  25.8 2.1 %collective-permute-done.11.got_ref = bf16[8,80,512]{2,1,0:T(8,128)(2,1)S(1)} collective-permute-done((bf16[8,80,512]{2,1,0:T(8,128)(2,1)S(1)}, bf16[8,80,512]{2,1,0:T(8,128)(2,1)S(1)}, u32[]{:S(2)}, u32[]{:S(2)}) %collective-permute-start.11) | collective-permute-done | bytes 655392 | tf_op jit(solution)/shard_map/ppermute | solution.py:383
  27.8 0.2 shard_map.210
  28.0 1.6 %collective-permute-start.12 = (bf16[4,80,512]{2,1,0:T(8,128)(2,1)S(1)}, bf16[4,80,512]{2,1,0:T(8,128)(2,1)S(1)}, u32[]{:S(2)}, u32[]{:S(2)}) collective-permute-start(bf16[4,80,512]{2,1,0:T(8,128)(2,1)S(1)} %get-tuple-element.67), channel_id=1, source_target_pairs={{0,8},{4,12},{8,0},{12,4},{1,9},{5,13},{9,1},{13,5},{2,10},{6,14},... | collective-permute-start | bytes 983048 | tf_op jit(solution)/shard_map/ppermute | solution.py:383
  29.6 0.2 collective-permute-start.7
  29.7 2.7 %collective-permute-start.8 = (bf16[48,512]{1,0:T(8,128)(2,1)S(1)}, bf16[48,512]{1,0:T(8,128)(2,1)S(1)}, u32[]{:S(2)}, u32[]{:S(2)}) collective-permute-start(bf16[48,512]{1,0:T(8,128)(2,1)S(1)} %get-tuple-element.62), channel_id=1, source_target_pairs={{0,2},{1,3},{2,0},{3,1},{4,6},{5,7},{6,4},{7,5},{8,10},{9,11},{10,... | collective-permute-start | bytes 147464 | tf_op jit(solution)/shard_map/ppermute | solution.py:383
  32.4 1.5 %collective-permute-start.9 = (bf16[48,512]{1,0:T(8,128)(2,1)S(1)}, bf16[48,512]{1,0:T(8,128)(2,1)S(1)}, u32[]{:S(2)}, u32[]{:S(2)}) collective-permute-start(bf16[48,512]{1,0:T(8,128)(2,1)S(1)} %get-tuple-element.63), channel_id=1, source_target_pairs={{0,3},{1,2},{2,1},{3,0},{4,7},{5,6},{6,5},{7,4},{8,11},{9,10},{10,... | collective-permute-start | bytes 147464 | tf_op jit(solution)/shard_map/ppermute | solution.py:383
  33.9 0.0 collective-permute-done.7.refs_1_.refs_0_
  34.0 2.7 %collective-permute-done.8.refs_2_.refs_1_ = bf16[48,512]{1,0:T(8,128)(2,1)S(1)} collective-permute-done((bf16[48,512]{1,0:T(8,128)(2,1)S(1)}, bf16[48,512]{1,0:T(8,128)(2,1)S(1)}, u32[]{:S(2)}, u32[]{:S(2)}) %collective-permute-start.8) | collective-permute-done | bytes 49184 | tf_op jit(solution)/shard_map/ppermute | solution.py:383
  36.6 1.6 %collective-permute-done.9.refs_3_.refs_2_ = bf16[48,512]{1,0:T(8,128)(2,1)S(1)} collective-permute-done((bf16[48,512]{1,0:T(8,128)(2,1)S(1)}, bf16[48,512]{1,0:T(8,128)(2,1)S(1)}, u32[]{:S(2)}, u32[]{:S(2)}) %collective-permute-start.9) | collective-permute-done | bytes 49184 | tf_op jit(solution)/shard_map/ppermute | solution.py:383
  38.3 0.6 shard_map.209.refs_0_
  38.9 0.6 collective-permute-start.10
  39.5 0.0 collective-permute-done.12.got_ref
  39.5 0.1 shard_map.211
  39.5 0.1 collective-permute-start.13
  39.6 2.1 %collective-permute-start.14 = (bf16[80,512]{1,0:T(8,128)(2,1)S(1)}, bf16[80,512]{1,0:T(8,128)(2,1)S(1)}, u32[]{:S(2)}, u32[]{:S(2)}) collective-permute-start(bf16[80,512]{1,0:T(8,128)(2,1)S(1)} %get-tuple-element.70), channel_id=1, source_target_pairs={{0,2},{1,3},{2,0},{3,1},{4,6},{5,7},{6,4},{7,5},{8,10},{9,11},{10,... | collective-permute-start | bytes 245768 | tf_op jit(solution)/shard_map/ppermute | solution.py:383
  41.7 2.3 %collective-permute-start.15 = (bf16[80,512]{1,0:T(8,128)(2,1)S(1)}, bf16[80,512]{1,0:T(8,128)(2,1)S(1)}, u32[]{:S(2)}, u32[]{:S(2)}) collective-permute-start(bf16[80,512]{1,0:T(8,128)(2,1)S(1)} %get-tuple-element.71), channel_id=1, source_target_pairs={{0,3},{1,2},{2,1},{3,0},{4,7},{5,6},{6,5},{7,4},{8,11},{9,10},{10,... | collective-permute-start | bytes 245768 | tf_op jit(solution)/shard_map/ppermute | solution.py:383
  44.0 0.6 collective-permute-done.10._.refs_1_
  44.6 0.0 collective-permute-done.13.refs_1_
  44.6 2.1 %collective-permute-done.14.refs_2_ = bf16[80,512]{1,0:T(8,128)(2,1)S(1)} collective-permute-done((bf16[80,512]{1,0:T(8,128)(2,1)S(1)}, bf16[80,512]{1,0:T(8,128)(2,1)S(1)}, u32[]{:S(2)}, u32[]{:S(2)}) %collective-permute-start.14) | collective-permute-done | bytes 81952 | tf_op jit(solution)/shard_map/ppermute | solution.py:383
  46.7 1.4 %collective-permute-done.15.refs_3_ = bf16[80,512]{1,0:T(8,128)(2,1)S(1)} collective-permute-done((bf16[80,512]{1,0:T(8,128)(2,1)S(1)}, bf16[80,512]{1,0:T(8,128)(2,1)S(1)}, u32[]{:S(2)}, u32[]{:S(2)}) %collective-permute-start.15) | collective-permute-done | bytes 81952 | tf_op jit(solution)/shard_map/ppermute | solution.py:383
  48.1 2.3 %collective-permute-start.18 = (bf16[80,512]{1,0:T(8,128)(2,1)S(1)}, bf16[80,512]{1,0:T(8,128)(2,1)S(1)}, u32[]{:S(2)}, u32[]{:S(2)}) collective-permute-start(bf16[80,512]{1,0:T(8,128)(2,1)S(1)} %shard_map.212.refs_0_), channel_id=1, source_target_pairs={{0,3},{1,2},{2,1},{3,0},{4,7},{5,6},{6,5},{7,4},{8,11},{9,10},{10,... | collective-permute-start | bytes 245768 | tf_op jit(solution)/shard_map/ppermute | solution.py:383
  50.5 0.9 %collective-permute-start.17 = (bf16[80,512]{1,0:T(8,128)(2,1)S(1)}, bf16[80,512]{1,0:T(8,128)(2,1)S(1)}, u32[]{:S(2)}, u32[]{:S(2)}) collective-permute-start(bf16[80,512]{1,0:T(8,128)(2,1)S(1)} %shard_map.212.refs_0_), channel_id=1, source_target_pairs={{0,2},{1,3},{2,0},{3,1},{4,6},{5,7},{6,4},{7,5},{8,10},{9,11},{10,... | collective-permute-start | bytes 245768 | tf_op jit(solution)/shard_map/ppermute | solution.py:383
  51.4 1.2 %collective-permute-start.16 = (bf16[80,512]{1,0:T(8,128)(2,1)S(1)}, bf16[80,512]{1,0:T(8,128)(2,1)S(1)}, u32[]{:S(2)}, u32[]{:S(2)}) collective-permute-start(bf16[80,512]{1,0:T(8,128)(2,1)S(1)} %shard_map.212.refs_0_), channel_id=1, source_target_pairs={{0,1},{1,0},{2,3},{3,2},{4,5},{5,4},{6,7},{7,6},{8,9},{9,8},{10,11... | collective-permute-start | bytes 245768 | tf_op jit(solution)/shard_map/ppermute | solution.py:383
  52.6 2.0 %collective-permute-done.18.refs_3_ = bf16[80,512]{1,0:T(8,128)(2,1)S(1)} collective-permute-done((bf16[80,512]{1,0:T(8,128)(2,1)S(1)}, bf16[80,512]{1,0:T(8,128)(2,1)S(1)}, u32[]{:S(2)}, u32[]{:S(2)}) %collective-permute-start.18) | collective-permute-done | bytes 81952 | tf_op jit(solution)/shard_map/ppermute | solution.py:383
  54.5 2.0 %collective-permute-done.17.refs_2_ = bf16[80,512]{1,0:T(8,128)(2,1)S(1)} collective-permute-done((bf16[80,512]{1,0:T(8,128)(2,1)S(1)}, bf16[80,512]{1,0:T(8,128)(2,1)S(1)}, u32[]{:S(2)}, u32[]{:S(2)}) %collective-permute-start.17) | collective-permute-done | bytes 81952 | tf_op jit(solution)/shard_map/ppermute | solution.py:383
  56.5 0.2 collective-permute-done.16.refs_1_
  56.7 1.6 %collective-permute-start.19 = (bf16[4,80,512]{2,1,0:T(8,128)(2,1)S(1)}, bf16[4,80,512]{2,1,0:T(8,128)(2,1)S(1)}, u32[]{:S(2)}, u32[]{:S(2)}) collective-permute-start(bf16[4,80,512]{2,1,0:T(8,128)(2,1)S(1)} %shard_map.213.own), channel_id=1, source_target_pairs={{0,8},{4,12},{8,0},{12,4},{1,9},{5,13},{9,1},{13,5},{2,10},{6,14},... | collective-permute-start | bytes 983048 | tf_op jit(solution)/shard_map/ppermute | solution.py:383
  58.3 0.0 collective-permute-start.20
  58.3 5.6 %collective-permute-done.19.over_x = bf16[4,80,512]{2,1,0:T(8,128)(2,1)S(1)} collective-permute-done((bf16[4,80,512]{2,1,0:T(8,128)(2,1)S(1)}, bf16[4,80,512]{2,1,0:T(8,128)(2,1)S(1)}, u32[]{:S(2)}, u32[]{:S(2)}) %collective-permute-start.19) | collective-permute-done | bytes 327712 | tf_op jit(solution)/shard_map/ppermute | solution.py:383
  63.9 0.0 collective-permute-start.21
  63.9 0.5 collective-permute-start.22
  64.4 0.0 collective-permute-start.23
  64.4 0.1 pad_add_fusion.place_ref
  64.5 1.3 %collective-permute-done.22.refs_2_ = bf16[4,48,512]{2,1,0:T(8,128)(2,1)S(1)} collective-permute-done((bf16[4,48,512]{2,1,0:T(8,128)(2,1)S(1)}, bf16[4,48,512]{2,1,0:T(8,128)(2,1)S(1)}, u32[]{:S(2)}, u32[]{:S(2)}) %collective-permute-start.22) | collective-permute-done | bytes 196640 | tf_op jit(solution)/shard_map/ppermute | solution.py:383
  65.8 0.3 collective-permute-done.23.refs_3_
  66.1 0.0 collective-permute-done.20.over_core
  66.1 0.0 collective-permute-done.21.over_both
  66.1 2.4 %shard_map.214 = (f32[16,128,128]{2,1,0:T(8,128)}, bf16[128,512]{1,0:T(8,128)(2,1)}, f32[1,512]{1,0:T(1,128)}, bf16[128,512]{1,0:T(8,128)(2,1)}, bf16[512,512]{1...) custom-call(s32[3]{0:T(128)S(1)} %pad_add_fusion.place_ref, ...), custom_call_target="tpu_custom_call" | custom-call | bytes 1048576 | tf_op jit(solution)/shard_map/pallas_call | solution.py:307
  (2 shorter events, 0.1 us)
Async XLA Ops:
  0.6 10.3 %collective-permute-start.3 = (bf16[2048,128]{1,0:T(8,128)(2,1)}, bf16[2048,128]{1,0:T(8,128)(2,1)S(1)}, u32[]{:S(2)}, u32[]{:S(2)}) collective-permute-start(bf16[2048,128]{1,0:T(8,128)(2,1)} %param.17), channel_id=1, source_target_pairs={{0,4},{4,0},{8,12},{12,8},{1,5},{5,1},{9,13},{13,9},{2,6},{6,2},{1... | collective-permute-start | bytes 1572872 | tf_op jit(solution)/shard_map/ppermute | solution.py:383
  1.2 0.7 copy-start
  1.2 0.7 copy-start.1
  1.9 6.1 %collective-permute-start.2 = (s32[1,8]{1,0:T(1,128)S(1)}, s32[1,8]{1,0:T(1,128)S(1)}, u32[]{:S(2)}, u32[]{:S(2)}) collective-permute-start(s32[1,8]{1,0:T(1,128)S(1)} %add_bitcast_fusion.refs_0_), channel_id=1, source_target_pairs={{0,3},{1,2},{2,1},{3,0},{4,7},{5,6},{6,5},{7,4},{8,11},{9,10},{10,... | collective-permute-start | bytes 104 | tf_op jit(solution)/shard_map/ppermute | solution.py:383
  6.5 4.4 %collective-permute-start.1 = (s32[1,8]{1,0:T(1,128)S(1)}, s32[1,8]{1,0:T(1,128)S(1)}, u32[]{:S(2)}, u32[]{:S(2)}) collective-permute-start(s32[1,8]{1,0:T(1,128)S(1)} %add_bitcast_fusion.refs_0_), channel_id=1, source_target_pairs={{0,2},{1,3},{2,0},{3,1},{4,6},{5,7},{6,4},{7,5},{8,10},{9,11},{10,... | collective-permute-start | bytes 104 | tf_op jit(solution)/shard_map/ppermute | solution.py:383
  6.5 4.4 %collective-permute-start = (s32[1,8]{1,0:T(1,128)S(1)}, s32[1,8]{1,0:T(1,128)S(1)}, u32[]{:S(2)}, u32[]{:S(2)}) collective-permute-start(s32[1,8]{1,0:T(1,128)S(1)} %add_bitcast_fusion.refs_0_), channel_id=1, source_target_pairs={{0,1},{1,0},{2,3},{3,2},{4,5},{5,4},{6,7},{7,6},{8,9},{9,8},{10,11... | collective-permute-start | bytes 104 | tf_op jit(solution)/shard_map/ppermute | solution.py:383
  12.1 6.7 %collective-permute-start.4 = (bf16[128,128]{1,0:T(8,128)(2,1)S(1)}, bf16[128,128]{1,0:T(8,128)(2,1)S(1)}, u32[]{:S(2)}, u32[]{:S(2)}) collective-permute-start(bf16[128,128]{1,0:T(8,128)(2,1)S(1)} %get-tuple-element.46), channel_id=1, source_target_pairs={{0,1},{1,0},{2,3},{3,2},{4,5},{5,4},{6,7},{7,6},{8,9},{9,8},{10,11... | collective-permute-start | bytes 98312 | tf_op jit(solution)/shard_map/ppermute | solution.py:383
  12.2 6.6 %collective-permute-start.5 = (bf16[128,128]{1,0:T(8,128)(2,1)S(1)}, bf16[128,128]{1,0:T(8,128)(2,1)S(1)}, u32[]{:S(2)}, u32[]{:S(2)}) collective-permute-start(bf16[128,128]{1,0:T(8,128)(2,1)S(1)} %get-tuple-element.47), channel_id=1, source_target_pairs={{0,2},{1,3},{2,0},{3,1},{4,6},{5,7},{6,4},{7,5},{8,10},{9,11},{10,... | collective-permute-start | bytes 98312 | tf_op jit(solution)/shard_map/ppermute | solution.py:383
  14.3 5.7 %collective-permute-start.6 = (bf16[128,128]{1,0:T(8,128)(2,1)S(1)}, bf16[128,128]{1,0:T(8,128)(2,1)S(1)}, u32[]{:S(2)}, u32[]{:S(2)}) collective-permute-start(bf16[128,128]{1,0:T(8,128)(2,1)S(1)} %get-tuple-element.48), channel_id=1, source_target_pairs={{0,3},{1,2},{2,1},{3,0},{4,7},{5,6},{6,5},{7,4},{8,11},{9,10},{10,... | collective-permute-start | bytes 98312 | tf_op jit(solution)/shard_map/ppermute | solution.py:383
  25.7 2.2 %collective-permute-start.11 = (bf16[8,80,512]{2,1,0:T(8,128)(2,1)S(1)}, bf16[8,80,512]{2,1,0:T(8,128)(2,1)S(1)}, u32[]{:S(2)}, u32[]{:S(2)}) collective-permute-start(bf16[8,80,512]{2,1,0:T(8,128)(2,1)S(1)} %get-tuple-element.65), channel_id=1, source_target_pairs={{0,4},{4,0},{8,12},{12,8},{1,5},{5,1},{9,13},{13,9},{2,6},{6,2},{1... | collective-permute-start | bytes 1966088 | tf_op jit(solution)/shard_map/ppermute | solution.py:383
  28.0 11.5 %collective-permute-start.12 = (bf16[4,80,512]{2,1,0:T(8,128)(2,1)S(1)}, bf16[4,80,512]{2,1,0:T(8,128)(2,1)S(1)}, u32[]{:S(2)}, u32[]{:S(2)}) collective-permute-start(bf16[4,80,512]{2,1,0:T(8,128)(2,1)S(1)} %get-tuple-element.67), channel_id=1, source_target_pairs={{0,8},{4,12},{8,0},{12,4},{1,9},{5,13},{9,1},{13,5},{2,10},{6,14},... | collective-permute-start | bytes 983048 | tf_op jit(solution)/shard_map/ppermute | solution.py:383
  29.6 4.4 %collective-permute-start.7 = (bf16[48,512]{1,0:T(8,128)(2,1)S(1)}, bf16[48,512]{1,0:T(8,128)(2,1)S(1)}, u32[]{:S(2)}, u32[]{:S(2)}) collective-permute-start(bf16[48,512]{1,0:T(8,128)(2,1)S(1)} %get-tuple-element.61), channel_id=1, source_target_pairs={{0,1},{1,0},{2,3},{3,2},{4,5},{5,4},{6,7},{7,6},{8,9},{9,8},{10,11... | collective-permute-start | bytes 147464 | tf_op jit(solution)/shard_map/ppermute | solution.py:383
  29.7 6.9 %collective-permute-start.8 = (bf16[48,512]{1,0:T(8,128)(2,1)S(1)}, bf16[48,512]{1,0:T(8,128)(2,1)S(1)}, u32[]{:S(2)}, u32[]{:S(2)}) collective-permute-start(bf16[48,512]{1,0:T(8,128)(2,1)S(1)} %get-tuple-element.62), channel_id=1, source_target_pairs={{0,2},{1,3},{2,0},{3,1},{4,6},{5,7},{6,4},{7,5},{8,10},{9,11},{10,... | collective-permute-start | bytes 147464 | tf_op jit(solution)/shard_map/ppermute | solution.py:383
  32.4 5.9 %collective-permute-start.9 = (bf16[48,512]{1,0:T(8,128)(2,1)S(1)}, bf16[48,512]{1,0:T(8,128)(2,1)S(1)}, u32[]{:S(2)}, u32[]{:S(2)}) collective-permute-start(bf16[48,512]{1,0:T(8,128)(2,1)S(1)} %get-tuple-element.63), channel_id=1, source_target_pairs={{0,3},{1,2},{2,1},{3,0},{4,7},{5,6},{6,5},{7,4},{8,11},{9,10},{10,... | collective-permute-start | bytes 147464 | tf_op jit(solution)/shard_map/ppermute | solution.py:383
  38.9 5.7 %collective-permute-start.10 = (bf16[4,48,512]{2,1,0:T(8,128)(2,1)S(1)}, bf16[4,48,512]{2,1,0:T(8,128)(2,1)S(1)}, u32[]{:S(2)}, u32[]{:S(2)}) collective-permute-start(bf16[4,48,512]{2,1,0:T(8,128)(2,1)S(1)} %shard_map.209.refs_0_), channel_id=1, source_target_pairs={{0,8},{4,12},{8,0},{12,4},{1,9},{5,13},{9,1},{13,5},{2,10},{6,14},... | collective-permute-start | bytes 589832 | tf_op jit(solution)/shard_map/ppermute | solution.py:383
  39.5 5.1 %collective-permute-start.13 = (bf16[80,512]{1,0:T(8,128)(2,1)S(1)}, bf16[80,512]{1,0:T(8,128)(2,1)S(1)}, u32[]{:S(2)}, u32[]{:S(2)}) collective-permute-start(bf16[80,512]{1,0:T(8,128)(2,1)S(1)} %get-tuple-element.69), channel_id=1, source_target_pairs={{0,1},{1,0},{2,3},{3,2},{4,5},{5,4},{6,7},{7,6},{8,9},{9,8},{10,11... | collective-permute-start | bytes 245768 | tf_op jit(solution)/shard_map/ppermute | solution.py:383
  39.6 7.0 %collective-permute-start.14 = (bf16[80,512]{1,0:T(8,128)(2,1)S(1)}, bf16[80,512]{1,0:T(8,128)(2,1)S(1)}, u32[]{:S(2)}, u32[]{:S(2)}) collective-permute-start(bf16[80,512]{1,0:T(8,128)(2,1)S(1)} %get-tuple-element.70), channel_id=1, source_target_pairs={{0,2},{1,3},{2,0},{3,1},{4,6},{5,7},{6,4},{7,5},{8,10},{9,11},{10,... | collective-permute-start | bytes 245768 | tf_op jit(solution)/shard_map/ppermute | solution.py:383
  41.7 6.3 %collective-permute-start.15 = (bf16[80,512]{1,0:T(8,128)(2,1)S(1)}, bf16[80,512]{1,0:T(8,128)(2,1)S(1)}, u32[]{:S(2)}, u32[]{:S(2)}) collective-permute-start(bf16[80,512]{1,0:T(8,128)(2,1)S(1)} %get-tuple-element.71), channel_id=1, source_target_pairs={{0,3},{1,2},{2,1},{3,0},{4,7},{5,6},{6,5},{7,4},{8,11},{9,10},{10,... | collective-permute-start | bytes 245768 | tf_op jit(solution)/shard_map/ppermute | solution.py:383
  48.1 6.4 %collective-permute-start.18 = (bf16[80,512]{1,0:T(8,128)(2,1)S(1)}, bf16[80,512]{1,0:T(8,128)(2,1)S(1)}, u32[]{:S(2)}, u32[]{:S(2)}) collective-permute-start(bf16[80,512]{1,0:T(8,128)(2,1)S(1)} %shard_map.212.refs_0_), channel_id=1, source_target_pairs={{0,3},{1,2},{2,1},{3,0},{4,7},{5,6},{6,5},{7,4},{8,11},{9,10},{10,... | collective-permute-start | bytes 245768 | tf_op jit(solution)/shard_map/ppermute | solution.py:383
  50.5 6.1 %collective-permute-start.17 = (bf16[80,512]{1,0:T(8,128)(2,1)S(1)}, bf16[80,512]{1,0:T(8,128)(2,1)S(1)}, u32[]{:S(2)}, u32[]{:S(2)}) collective-permute-start(bf16[80,512]{1,0:T(8,128)(2,1)S(1)} %shard_map.212.refs_0_), channel_id=1, source_target_pairs={{0,2},{1,3},{2,0},{3,1},{4,6},{5,7},{6,4},{7,5},{8,10},{9,11},{10,... | collective-permute-start | bytes 245768 | tf_op jit(solution)/shard_map/ppermute | solution.py:383
  51.4 5.3 %collective-permute-start.16 = (bf16[80,512]{1,0:T(8,128)(2,1)S(1)}, bf16[80,512]{1,0:T(8,128)(2,1)S(1)}, u32[]{:S(2)}, u32[]{:S(2)}) collective-permute-start(bf16[80,512]{1,0:T(8,128)(2,1)S(1)} %shard_map.212.refs_0_), channel_id=1, source_target_pairs={{0,1},{1,0},{2,3},{3,2},{4,5},{5,4},{6,7},{7,6},{8,9},{9,8},{10,11... | collective-permute-start | bytes 245768 | tf_op jit(solution)/shard_map/ppermute | solution.py:383
  56.7 7.1 %collective-permute-start.19 = (bf16[4,80,512]{2,1,0:T(8,128)(2,1)S(1)}, bf16[4,80,512]{2,1,0:T(8,128)(2,1)S(1)}, u32[]{:S(2)}, u32[]{:S(2)}) collective-permute-start(bf16[4,80,512]{2,1,0:T(8,128)(2,1)S(1)} %shard_map.213.own), channel_id=1, source_target_pairs={{0,8},{4,12},{8,0},{12,4},{1,9},{5,13},{9,1},{13,5},{2,10},{6,14},... | collective-permute-start | bytes 983048 | tf_op jit(solution)/shard_map/ppermute | solution.py:383
  58.3 7.8 %collective-permute-start.20 = (bf16[4,80,512]{2,1,0:T(8,128)(2,1)S(1)}, bf16[4,80,512]{2,1,0:T(8,128)(2,1)S(1)}, u32[]{:S(2)}, u32[]{:S(2)}) collective-permute-start(bf16[4,80,512]{2,1,0:T(8,128)(2,1)S(1)} %shard_map.213.own), channel_id=1, source_target_pairs={{0,4},{4,0},{8,12},{12,8},{1,5},{5,1},{9,13},{13,9},{2,6},{6,2},{1... | collective-permute-start | bytes 983048 | tf_op jit(solution)/shard_map/ppermute | solution.py:383
  63.9 2.2 %collective-permute-start.21 = (bf16[4,80,512]{2,1,0:T(8,128)(2,1)S(1)}, bf16[4,80,512]{2,1,0:T(8,128)(2,1)S(1)}, u32[]{:S(2)}, u32[]{:S(2)}) collective-permute-start(bf16[4,80,512]{2,1,0:T(8,128)(2,1)S(1)} %collective-permute-done.19.over_x), channel_id=1, source_target_pairs={{0,4},{4,0},{8,12},{12,8},{1,5},{5,1},{9,13},{13,9},{2,6},{6,2},{1... | collective-permute-start | bytes 983048 | tf_op jit(solution)/shard_map/ppermute | solution.py:383
  63.9 1.9 %collective-permute-start.22 = (bf16[4,48,512]{2,1,0:T(8,128)(2,1)S(1)}, bf16[4,48,512]{2,1,0:T(8,128)(2,1)S(1)}, u32[]{:S(2)}, u32[]{:S(2)}) collective-permute-start(bf16[4,48,512]{2,1,0:T(8,128)(2,1)S(1)} %shard_map.209.refs_0_), channel_id=1, source_target_pairs={{0,4},{4,0},{8,12},{12,8},{1,5},{5,1},{9,13},{13,9},{2,6},{6,2},{1... | collective-permute-start | bytes 589832 | tf_op jit(solution)/shard_map/ppermute | solution.py:383
  64.4 1.7 %collective-permute-start.23 = (bf16[4,48,512]{2,1,0:T(8,128)(2,1)S(1)}, bf16[4,48,512]{2,1,0:T(8,128)(2,1)S(1)}, u32[]{:S(2)}, u32[]{:S(2)}) collective-permute-start(bf16[4,48,512]{2,1,0:T(8,128)(2,1)S(1)} %collective-permute-done.10._.refs_1_), channel_id=1, source_target_pairs={{0,4},{4,0},{8,12},{12,8},{1,5},{5,1},{9,13},{13,9},{2,6},{6,2},{1... | collective-permute-start | bytes 589832 | tf_op jit(solution)/shard_map/ppermute | solution.py:383

commit v5 on v4

--- a/solution.py
+++ b/solution.py
@@ -256,7 +256,9 @@
         out[m, rows:, :] = jnp.where(place == 3, ids_ref[m].astype(F32), tail).astype(BF16)
 
 
-def add_surface(groups, surf, benc, b1, b2):
+def surface_kernel(*refs):
+    groups, own, surf, benc, b1, b2, passed = refs[:4], *refs[4:]
+    passed[...] = own[...]
     surf[...] = jnp.zeros_like(surf)
     block_rows, channels = surf.shape[1:]
     quarter = block_rows // 4
@@ -276,9 +278,7 @@
     b2[...] = bias[2:3, :]
 
 
-def final_kernel(place_ref, own, over_x, over_core, over_both, *refs):
-    surf, wenc, benc, win, wmid, b1, wout, b2 = refs[4:]
-    add_surface(refs[:4], surf, benc, b1, b2)
+def weights_kernel(place_ref, own, over_x, over_core, over_both, wenc, win, wmid, wout):
     c, x, z = place_ref[0], place_ref[1], place_ref[2]
     pieces = []
     for m in range(4):
@@ -436,27 +436,26 @@
     terms = [terms, terms_x, swap(terms, "region", 1, 4), swap(terms_x, "region", 1, 4)]
     own = call(join_kernel, shape((n_sub, 80, hidden)), [VMEM] * n_sub, *totals)
     over_x = swap(own, "region", 2, 4)
-    over_core = swap(own, "region", 1, 4)
+    surf, benc, b1, b2, passed = call(
+        surface_kernel,
+        [shape((surface.shape[0] // block_rows, block_rows, channels), F32)]
+        + [shape((1, hidden), F32)] * 3
+        + [shape(own.shape)],
+        [VMEM] * 5,
+        *terms,
+        own,
+    )
+    over_core = swap(passed, "region", 1, 4)
     over_both = swap(over_x, "region", 1, 4)
-    surf, wenc, benc, win, wmid, b1, wout, b2 = call(
-        final_kernel,
-        [
-            shape((surface.shape[0] // block_rows, block_rows, channels), F32),
-            shape((128, hidden)),
-            shape((1, hidden), F32),
-            shape((128, hidden)),
-            shape((512, hidden)),
-            shape((1, hidden), F32),
-            shape((512, hidden)),
-            shape((1, hidden), F32),
-        ],
-        [SMEM] + [VMEM] * 8,
+    wenc, win, wmid, wout = call(
+        weights_kernel,
+        [shape((128, hidden)), shape((128, hidden)), shape((512, hidden)), shape((512, hidden))],
+        [SMEM] + [VMEM] * 4,
         jnp.stack([core, chip, me]),
         own,
         over_x,
         over_core,
         over_both,
-        *terms,
     )
     return (
         surf.reshape(surface.shape),

time: 68.7 us -> 67.5 us (0.983)
  waiting for transfers between devices: 26.1 us -> 24.1 us
    ppermute x24, waiting for transfers between devices: 26.1 us -> 24.1 us  [swap(): return lax.ppermute(value, axis, [(i, i ^ mask) for i in range(size)])]
    pallas_call x9 -> x10, Pallas kernels: 12.3 us -> 12.9 us  [call(): pl.pallas_call(kernel, out_shape=out_shape, in_specs=in_specs, out_specs=...]
  transfers between devices with their start and end apart: 24 -> 24, of which waited for: 15 -> 16; matrix products, arithmetic and copies ran while one was open for 0% -> 0% of each run, Pallas kernels for 4% -> 6%
where the time goes in v5:
time: 67.5 us; the launch traced here: 67.3 us
  starting transfers between devices  28 us (41%)
  waiting for transfers between devices  24.1 us (36%)
  Pallas kernels  12.9 us (19%)
  between operations  1.42 us (2%)
    ppermute x24, starting transfers between devices, swap(): return lax.ppermute(value, axis, [(i, i ^ mask) for i in range(size)])  28 us
    ppermute x24, waiting for transfers between devices, swap(): return lax.ppermute(value, axis, [(i, i ^ mask) for i in range(size)])  24.1 us
    pallas_call x10, Pallas kernels, call(): pl.pallas_call(kernel, out_shape=out_shape, in_specs=in_specs, out_specs=...  12.9 us
  transfers between devices with their start and end apart: 24, of which 16 were waited for; matrix products, arithmetic and copies ran while one was open for 0% of the time, Pallas kernels for 6%

profile of v5, /device:TPU:0, one launch (start us, length us, event | category | flops | bytes accessed | tf_op | source)
XLA Modules:
  0.0 67.3 jit_solution(11758459238910697091)
XLA Ops:
  0.6 0.5 collective-permute-start.3
  1.2 0.0 copy-start
  1.2 0.0 copy-start.1
  1.2 0.7 copy-done
  1.8 0.0 copy-done.1
  1.8 0.1 add_bitcast_fusion.refs_0_
  1.9 4.6 %collective-permute-start.2 = (s32[1,8]{1,0:T(1,128)S(1)}, s32[1,8]{1,0:T(1,128)S(1)}, u32[]{:S(2)}, u32[]{:S(2)}) collective-permute-start(s32[1,8]{1,0:T(1,128)S(1)} %add_bitcast_fusion.refs_0_), channel_id=1, source_target_pairs={{0,3},{1,2},{2,1},{3,0},{4,7},{5,6},{6,5},{7,4},{8,11},{9,10},{10,... | collective-permute-start | bytes 104 | tf_op jit(solution)/shard_map/ppermute | solution.py:383
  6.5 0.0 collective-permute-start.1
  6.5 0.6 collective-permute-start
  7.8 0.1 pad_add_fusion.place_ref
  7.9 0.1 collective-permute-done.2.refs_3_
  8.0 2.9 %collective-permute-done.1.refs_2_ = s32[1,8]{1,0:T(1,128)S(1)} collective-permute-done((s32[1,8]{1,0:T(1,128)S(1)}, s32[1,8]{1,0:T(1,128)S(1)}, u32[]{:S(2)}, u32[]{:S(2)}) %collective-permute-start.1) | collective-permute-done | bytes 64 | tf_op jit(solution)/shard_map/ppermute | solution.py:383
  10.9 0.0 collective-permute-done.refs_1_
  11.0 0.0 collective-permute-done.3.refs_4_
  11.0 1.2 %shard_map.206 = (bf16[128,128]{1,0:T(8,128)(2,1)S(1)}, bf16[128,128]{1,0:T(8,128)(2,1)S(1)}, bf16[128,128]{1,0:T(8,128)(2,1)S(1)}, bf16[128,128]{1,0:T(8,128)(2,1)S(1)}, s32[4]{0:T(128)S(1)}) custom-call(s32[1]{0:T(128)} %bitcast.me_ref.place_ref, s32[1,8]{1,0:T(1,128)S(1)} %add_bitcast_fusion.refs_0_, s32[1,8]{1,0:T(1,128)S(1)} %collective-permute-done.refs_1_, ...), custom_call_target="tpu_custom_call" | custom-call | bytes 1048576 | tf_op jit(solution)/shard_map/pallas_call | solution.py:307
  12.1 0.1 collective-permute-start.4
  12.2 2.1 %collective-permute-start.5 = (bf16[128,128]{1,0:T(8,128)(2,1)S(1)}, bf16[128,128]{1,0:T(8,128)(2,1)S(1)}, u32[]{:S(2)}, u32[]{:S(2)}) collective-permute-start(bf16[128,128]{1,0:T(8,128)(2,1)S(1)} %get-tuple-element.48), channel_id=1, source_target_pairs={{0,2},{1,3},{2,0},{3,1},{4,6},{5,7},{6,4},{7,5},{8,10},{9,11},{10,... | collective-permute-start | bytes 98312 | tf_op jit(solution)/shard_map/ppermute | solution.py:383
  14.3 2.3 %collective-permute-start.6 = (bf16[128,128]{1,0:T(8,128)(2,1)S(1)}, bf16[128,128]{1,0:T(8,128)(2,1)S(1)}, u32[]{:S(2)}, u32[]{:S(2)}) collective-permute-start(bf16[128,128]{1,0:T(8,128)(2,1)S(1)} %get-tuple-element.49), channel_id=1, source_target_pairs={{0,3},{1,2},{2,1},{3,0},{4,7},{5,6},{6,5},{7,4},{8,11},{9,10},{10,... | collective-permute-start | bytes 98312 | tf_op jit(solution)/shard_map/ppermute | solution.py:383
  16.6 2.2 %shard_map.207 = (bf16[512,128]{1,0:T(8,128)(2,1)S(1)}, bf16[128,512]{1,0:T(8,128)(2,1)S(1)}, bf16[512,512]{1,0:T(8,128)(2,1)S(1)}, bf16[512,512]{1,0:T(8,128)(2...) custom-call(s32[1]{0:T(128)S(6)} %copy.23.count_ref, ...), custom_call_target="tpu_custom_call" | custom-call | flops 1073741824 | bytes 1048576 | tf_op jit(solution)/shard_map/pallas_call | solution.py:307
  18.8 0.0 collective-permute-done.4.refs_1_
  18.8 0.0 collective-permute-done.5.refs_2_
  18.9 1.2 %collective-permute-done.6.refs_3_ = bf16[128,128]{1,0:T(8,128)(2,1)S(1)} collective-permute-done((bf16[128,128]{1,0:T(8,128)(2,1)S(1)}, bf16[128,128]{1,0:T(8,128)(2,1)S(1)}, u32[]{:S(2)}, u32[]{:S(2)}) %collective-permute-start.6) | collective-permute-done | bytes 32800 | tf_op jit(solution)/shard_map/ppermute | solution.py:383
  20.0 5.6 %shard_map.208 = (bf16[8,80,512]{2,1,0:T(8,128)(2,1)S(1)}, bf16[8,80,512]{2,1,0:T(8,128)(2,1)S(1)}, bf16[48,512]{1,0:T(8,128)(2,1)S(1)}, bf16[48,512]{1,0:T(8,12...) custom-call(s32[2]{0:T(128)S(1)} %pad_add_fusion.place_ref, s32[4]{0:T(128)S(1)} %bitcast.17, ...), custom_call_target="tpu_custom_call" | custom-call | flops 2147483648 | bytes 1048576 | tf_op jit(solution)/shard_map/pallas_call | solution.py:307
  25.7 0.1 collective-permute-start.13
  25.8 2.1 %collective-permute-done.13.got_ref = bf16[8,80,512]{2,1,0:T(8,128)(2,1)S(1)} collective-permute-done((bf16[8,80,512]{2,1,0:T(8,128)(2,1)S(1)}, bf16[8,80,512]{2,1,0:T(8,128)(2,1)S(1)}, u32[]{:S(2)}, u32[]{:S(2)}) %collective-permute-start.13) | collective-permute-done | bytes 655392 | tf_op jit(solution)/shard_map/ppermute | solution.py:383
  27.8 0.2 shard_map.210
  28.0 1.6 %collective-permute-start.14 = (bf16[4,80,512]{2,1,0:T(8,128)(2,1)S(1)}, bf16[4,80,512]{2,1,0:T(8,128)(2,1)S(1)}, u32[]{:S(2)}, u32[]{:S(2)}) collective-permute-start(bf16[4,80,512]{2,1,0:T(8,128)(2,1)S(1)} %get-tuple-element.68), channel_id=1, source_target_pairs={{0,8},{4,12},{8,0},{12,4},{1,9},{5,13},{9,1},{13,5},{2,10},{6,14},... | collective-permute-start | bytes 983048 | tf_op jit(solution)/shard_map/ppermute | solution.py:383
  29.6 0.2 collective-permute-start.7
  29.7 2.7 %collective-permute-start.8 = (bf16[48,512]{1,0:T(8,128)(2,1)S(1)}, bf16[48,512]{1,0:T(8,128)(2,1)S(1)}, u32[]{:S(2)}, u32[]{:S(2)}) collective-permute-start(bf16[48,512]{1,0:T(8,128)(2,1)S(1)} %get-tuple-element.63), channel_id=1, source_target_pairs={{0,2},{1,3},{2,0},{3,1},{4,6},{5,7},{6,4},{7,5},{8,10},{9,11},{10,... | collective-permute-start | bytes 147464 | tf_op jit(solution)/shard_map/ppermute | solution.py:383
  32.4 1.5 %collective-permute-start.9 = (bf16[48,512]{1,0:T(8,128)(2,1)S(1)}, bf16[48,512]{1,0:T(8,128)(2,1)S(1)}, u32[]{:S(2)}, u32[]{:S(2)}) collective-permute-start(bf16[48,512]{1,0:T(8,128)(2,1)S(1)} %get-tuple-element.64), channel_id=1, source_target_pairs={{0,3},{1,2},{2,1},{3,0},{4,7},{5,6},{6,5},{7,4},{8,11},{9,10},{10,... | collective-permute-start | bytes 147464 | tf_op jit(solution)/shard_map/ppermute | solution.py:383
  33.9 0.0 collective-permute-done.7.refs_1_.refs_0_
  34.0 2.7 %collective-permute-done.8.refs_2_.refs_1_ = bf16[48,512]{1,0:T(8,128)(2,1)S(1)} collective-permute-done((bf16[48,512]{1,0:T(8,128)(2,1)S(1)}, bf16[48,512]{1,0:T(8,128)(2,1)S(1)}, u32[]{:S(2)}, u32[]{:S(2)}) %collective-permute-start.8) | collective-permute-done | bytes 49184 | tf_op jit(solution)/shard_map/ppermute | solution.py:383
  36.6 1.6 %collective-permute-done.9.refs_3_.refs_2_ = bf16[48,512]{1,0:T(8,128)(2,1)S(1)} collective-permute-done((bf16[48,512]{1,0:T(8,128)(2,1)S(1)}, bf16[48,512]{1,0:T(8,128)(2,1)S(1)}, u32[]{:S(2)}, u32[]{:S(2)}) %collective-permute-start.9) | collective-permute-done | bytes 49184 | tf_op jit(solution)/shard_map/ppermute | solution.py:383
  38.3 0.6 shard_map.209.refs_0_
  38.9 0.6 collective-permute-start.10
  39.5 0.0 collective-permute-done.14.got_ref
  39.5 0.1 shard_map.211
  39.5 0.1 collective-permute-start.15
  39.6 2.1 %collective-permute-start.16 = (bf16[80,512]{1,0:T(8,128)(2,1)S(1)}, bf16[80,512]{1,0:T(8,128)(2,1)S(1)}, u32[]{:S(2)}, u32[]{:S(2)}) collective-permute-start(bf16[80,512]{1,0:T(8,128)(2,1)S(1)} %get-tuple-element.71), channel_id=1, source_target_pairs={{0,2},{1,3},{2,0},{3,1},{4,6},{5,7},{6,4},{7,5},{8,10},{9,11},{10,... | collective-permute-start | bytes 245768 | tf_op jit(solution)/shard_map/ppermute | solution.py:383
  41.7 2.3 %collective-permute-start.17 = (bf16[80,512]{1,0:T(8,128)(2,1)S(1)}, bf16[80,512]{1,0:T(8,128)(2,1)S(1)}, u32[]{:S(2)}, u32[]{:S(2)}) collective-permute-start(bf16[80,512]{1,0:T(8,128)(2,1)S(1)} %get-tuple-element.72), channel_id=1, source_target_pairs={{0,3},{1,2},{2,1},{3,0},{4,7},{5,6},{6,5},{7,4},{8,11},{9,10},{10,... | collective-permute-start | bytes 245768 | tf_op jit(solution)/shard_map/ppermute | solution.py:383
  44.0 0.6 collective-permute-done.10._.refs_1_
  44.6 0.0 collective-permute-done.15.refs_1_
  44.6 2.1 %collective-permute-done.16.refs_2_ = bf16[80,512]{1,0:T(8,128)(2,1)S(1)} collective-permute-done((bf16[80,512]{1,0:T(8,128)(2,1)S(1)}, bf16[80,512]{1,0:T(8,128)(2,1)S(1)}, u32[]{:S(2)}, u32[]{:S(2)}) %collective-permute-start.16) | collective-permute-done | bytes 81952 | tf_op jit(solution)/shard_map/ppermute | solution.py:383
  46.7 1.4 %collective-permute-done.17.refs_3_ = bf16[80,512]{1,0:T(8,128)(2,1)S(1)} collective-permute-done((bf16[80,512]{1,0:T(8,128)(2,1)S(1)}, bf16[80,512]{1,0:T(8,128)(2,1)S(1)}, u32[]{:S(2)}, u32[]{:S(2)}) %collective-permute-start.17) | collective-permute-done | bytes 81952 | tf_op jit(solution)/shard_map/ppermute | solution.py:383
  48.1 2.3 %collective-permute-start.20 = (bf16[80,512]{1,0:T(8,128)(2,1)S(1)}, bf16[80,512]{1,0:T(8,128)(2,1)S(1)}, u32[]{:S(2)}, u32[]{:S(2)}) collective-permute-start(bf16[80,512]{1,0:T(8,128)(2,1)S(1)} %shard_map.212.refs_0_), channel_id=1, source_target_pairs={{0,3},{1,2},{2,1},{3,0},{4,7},{5,6},{6,5},{7,4},{8,11},{9,10},{10,... | collective-permute-start | bytes 245768 | tf_op jit(solution)/shard_map/ppermute | solution.py:383
  50.5 0.9 %collective-permute-start.19 = (bf16[80,512]{1,0:T(8,128)(2,1)S(1)}, bf16[80,512]{1,0:T(8,128)(2,1)S(1)}, u32[]{:S(2)}, u32[]{:S(2)}) collective-permute-start(bf16[80,512]{1,0:T(8,128)(2,1)S(1)} %shard_map.212.refs_0_), channel_id=1, source_target_pairs={{0,2},{1,3},{2,0},{3,1},{4,6},{5,7},{6,4},{7,5},{8,10},{9,11},{10,... | collective-permute-start | bytes 245768 | tf_op jit(solution)/shard_map/ppermute | solution.py:383
  51.4 1.2 %collective-permute-start.18 = (bf16[80,512]{1,0:T(8,128)(2,1)S(1)}, bf16[80,512]{1,0:T(8,128)(2,1)S(1)}, u32[]{:S(2)}, u32[]{:S(2)}) collective-permute-start(bf16[80,512]{1,0:T(8,128)(2,1)S(1)} %shard_map.212.refs_0_), channel_id=1, source_target_pairs={{0,1},{1,0},{2,3},{3,2},{4,5},{5,4},{6,7},{7,6},{8,9},{9,8},{10,11... | collective-permute-start | bytes 245768 | tf_op jit(solution)/shard_map/ppermute | solution.py:383
  52.6 2.0 %collective-permute-done.20.refs_3_ = bf16[80,512]{1,0:T(8,128)(2,1)S(1)} collective-permute-done((bf16[80,512]{1,0:T(8,128)(2,1)S(1)}, bf16[80,512]{1,0:T(8,128)(2,1)S(1)}, u32[]{:S(2)}, u32[]{:S(2)}) %collective-permute-start.20) | collective-permute-done | bytes 81952 | tf_op jit(solution)/shard_map/ppermute | solution.py:383
  54.5 2.0 %collective-permute-done.19.refs_2_ = bf16[80,512]{1,0:T(8,128)(2,1)S(1)} collective-permute-done((bf16[80,512]{1,0:T(8,128)(2,1)S(1)}, bf16[80,512]{1,0:T(8,128)(2,1)S(1)}, u32[]{:S(2)}, u32[]{:S(2)}) %collective-permute-start.19) | collective-permute-done | bytes 81952 | tf_op jit(solution)/shard_map/ppermute | solution.py:383
  56.5 0.2 collective-permute-done.18.refs_1_
  56.7 1.6 %collective-permute-start.21 = (bf16[4,80,512]{2,1,0:T(8,128)(2,1)S(1)}, bf16[4,80,512]{2,1,0:T(8,128)(2,1)S(1)}, u32[]{:S(2)}, u32[]{:S(2)}) collective-permute-start(bf16[4,80,512]{2,1,0:T(8,128)(2,1)S(1)} %shard_map.213.refs_4_.own), channel_id=1, source_target_pairs={{0,8},{4,12},{8,0},{12,4},{1,9},{5,13},{9,1},{13,5},{2,10},{6,14},... | collective-permute-start | bytes 983048 | tf_op jit(solution)/shard_map/ppermute | solution.py:383
  58.3 0.0 collective-permute-start.11
  58.3 0.5 collective-permute-start.12
  58.8 0.9 %collective-permute-done.11.refs_2_ = bf16[4,48,512]{2,1,0:T(8,128)(2,1)S(1)} collective-permute-done((bf16[4,48,512]{2,1,0:T(8,128)(2,1)S(1)}, bf16[4,48,512]{2,1,0:T(8,128)(2,1)S(1)}, u32[]{:S(2)}, u32[]{:S(2)}) %collective-permute-start.11) | collective-permute-done | bytes 196640 | tf_op jit(solution)/shard_map/ppermute | solution.py:383
  59.7 0.3 collective-permute-done.12.refs_3_
  60.0 1.2 %shard_map.214 = (f32[16,128,128]{2,1,0:T(8,128)}, f32[1,512]{1,0:T(1,128)}, f32[1,512]{1,0:T(1,128)}, f32[1,512]{1,0:T(1,128)}, bf16[4,80,512]{2,1,0:T(8,128)(2,1)S(1)}) custom-call(bf16[4,48,512]{2,1,0:T(8,128)(2,1)S(1)} %shard_map.209.refs_0_, bf16[4,48,512]{2,1,0:T(8,128)(2,1)S(1)} %collective-permute-done.10._.refs_1_, ...), custom_call_target="tpu_custom_call" | custom-call | bytes 1048576 | tf_op jit(solution)/shard_map/pallas_call | solution.py:307
  61.2 0.2 collective-permute-start.22
  61.5 2.4 %collective-permute-done.21.over_x = bf16[4,80,512]{2,1,0:T(8,128)(2,1)S(1)} collective-permute-done((bf16[4,80,512]{2,1,0:T(8,128)(2,1)S(1)}, bf16[4,80,512]{2,1,0:T(8,128)(2,1)S(1)}, u32[]{:S(2)}, u32[]{:S(2)}) %collective-permute-start.21) | collective-permute-done | bytes 327712 | tf_op jit(solution)/shard_map/ppermute | solution.py:383
  63.9 0.0 collective-permute-start.23
  63.9 0.1 pad_add_fusion.1.place_ref
  64.0 0.0 collective-permute-done.22.over_core
  64.0 1.5 %collective-permute-done.23.over_both = bf16[4,80,512]{2,1,0:T(8,128)(2,1)S(1)} collective-permute-done((bf16[4,80,512]{2,1,0:T(8,128)(2,1)S(1)}, bf16[4,80,512]{2,1,0:T(8,128)(2,1)S(1)}, u32[]{:S(2)}, u32[]{:S(2)}) %collective-permute-start.23) | collective-permute-done | bytes 327712 | tf_op jit(solution)/shard_map/ppermute | solution.py:383
  65.5 1.8 %shard_map.215 = (bf16[128,512]{1,0:T(8,128)(2,1)}, bf16[128,512]{1,0:T(8,128)(2,1)}, bf16[512,512]{1,0:T(8,128)(2,1)}, bf16[512,512]{1,0:T(8,128)(2,1)}) custom-call(s32[3]{0:T(128)S(1)} %pad_add_fusion.1.place_ref, bf16[4,80,512]{2,1,0:T(8,128)(2,1)S(1)} %shard_map.213.refs_4_.own, bf16[4,80,512]{2,1,0:T(8,128)(2,1)S(1)} %collective-permute-done.21.over_x, ...), custom_call_target="tpu_custom_call" | custom-call | bytes 1048576 | tf_op jit(solution)/shard_map/pallas_call | solution.py:307
  (2 shorter events, 0.1 us)
Async XLA Ops:
  0.6 10.3 %collective-permute-start.3 = (bf16[2048,128]{1,0:T(8,128)(2,1)}, bf16[2048,128]{1,0:T(8,128)(2,1)S(1)}, u32[]{:S(2)}, u32[]{:S(2)}) collective-permute-start(bf16[2048,128]{1,0:T(8,128)(2,1)} %param.17), channel_id=1, source_target_pairs={{0,4},{4,0},{8,12},{12,8},{1,5},{5,1},{9,13},{13,9},{2,6},{6,2},{1... | collective-permute-start | bytes 1572872 | tf_op jit(solution)/shard_map/ppermute | solution.py:383
  1.2 0.7 copy-start
  1.2 0.7 copy-start.1
  1.9 6.1 %collective-permute-start.2 = (s32[1,8]{1,0:T(1,128)S(1)}, s32[1,8]{1,0:T(1,128)S(1)}, u32[]{:S(2)}, u32[]{:S(2)}) collective-permute-start(s32[1,8]{1,0:T(1,128)S(1)} %add_bitcast_fusion.refs_0_), channel_id=1, source_target_pairs={{0,3},{1,2},{2,1},{3,0},{4,7},{5,6},{6,5},{7,4},{8,11},{9,10},{10,... | collective-permute-start | bytes 104 | tf_op jit(solution)/shard_map/ppermute | solution.py:383
  6.5 4.4 %collective-permute-start.1 = (s32[1,8]{1,0:T(1,128)S(1)}, s32[1,8]{1,0:T(1,128)S(1)}, u32[]{:S(2)}, u32[]{:S(2)}) collective-permute-start(s32[1,8]{1,0:T(1,128)S(1)} %add_bitcast_fusion.refs_0_), channel_id=1, source_target_pairs={{0,2},{1,3},{2,0},{3,1},{4,6},{5,7},{6,4},{7,5},{8,10},{9,11},{10,... | collective-permute-start | bytes 104 | tf_op jit(solution)/shard_map/ppermute | solution.py:383
  6.5 4.4 %collective-permute-start = (s32[1,8]{1,0:T(1,128)S(1)}, s32[1,8]{1,0:T(1,128)S(1)}, u32[]{:S(2)}, u32[]{:S(2)}) collective-permute-start(s32[1,8]{1,0:T(1,128)S(1)} %add_bitcast_fusion.refs_0_), channel_id=1, source_target_pairs={{0,1},{1,0},{2,3},{3,2},{4,5},{5,4},{6,7},{7,6},{8,9},{9,8},{10,11... | collective-permute-start | bytes 104 | tf_op jit(solution)/shard_map/ppermute | solution.py:383
  12.1 6.7 %collective-permute-start.4 = (bf16[128,128]{1,0:T(8,128)(2,1)S(1)}, bf16[128,128]{1,0:T(8,128)(2,1)S(1)}, u32[]{:S(2)}, u32[]{:S(2)}) collective-permute-start(bf16[128,128]{1,0:T(8,128)(2,1)S(1)} %get-tuple-element.47), channel_id=1, source_target_pairs={{0,1},{1,0},{2,3},{3,2},{4,5},{5,4},{6,7},{7,6},{8,9},{9,8},{10,11... | collective-permute-start | bytes 98312 | tf_op jit(solution)/shard_map/ppermute | solution.py:383
  12.2 6.6 %collective-permute-start.5 = (bf16[128,128]{1,0:T(8,128)(2,1)S(1)}, bf16[128,128]{1,0:T(8,128)(2,1)S(1)}, u32[]{:S(2)}, u32[]{:S(2)}) collective-permute-start(bf16[128,128]{1,0:T(8,128)(2,1)S(1)} %get-tuple-element.48), channel_id=1, source_target_pairs={{0,2},{1,3},{2,0},{3,1},{4,6},{5,7},{6,4},{7,5},{8,10},{9,11},{10,... | collective-permute-start | bytes 98312 | tf_op jit(solution)/shard_map/ppermute | solution.py:383
  14.3 5.7 %collective-permute-start.6 = (bf16[128,128]{1,0:T(8,128)(2,1)S(1)}, bf16[128,128]{1,0:T(8,128)(2,1)S(1)}, u32[]{:S(2)}, u32[]{:S(2)}) collective-permute-start(bf16[128,128]{1,0:T(8,128)(2,1)S(1)} %get-tuple-element.49), channel_id=1, source_target_pairs={{0,3},{1,2},{2,1},{3,0},{4,7},{5,6},{6,5},{7,4},{8,11},{9,10},{10,... | collective-permute-start | bytes 98312 | tf_op jit(solution)/shard_map/ppermute | solution.py:383
  25.7 2.2 %collective-permute-start.13 = (bf16[8,80,512]{2,1,0:T(8,128)(2,1)S(1)}, bf16[8,80,512]{2,1,0:T(8,128)(2,1)S(1)}, u32[]{:S(2)}, u32[]{:S(2)}) collective-permute-start(bf16[8,80,512]{2,1,0:T(8,128)(2,1)S(1)} %get-tuple-element.66), channel_id=1, source_target_pairs={{0,4},{4,0},{8,12},{12,8},{1,5},{5,1},{9,13},{13,9},{2,6},{6,2},{1... | collective-permute-start | bytes 1966088 | tf_op jit(solution)/shard_map/ppermute | solution.py:383
  28.0 11.5 %collective-permute-start.14 = (bf16[4,80,512]{2,1,0:T(8,128)(2,1)S(1)}, bf16[4,80,512]{2,1,0:T(8,128)(2,1)S(1)}, u32[]{:S(2)}, u32[]{:S(2)}) collective-permute-start(bf16[4,80,512]{2,1,0:T(8,128)(2,1)S(1)} %get-tuple-element.68), channel_id=1, source_target_pairs={{0,8},{4,12},{8,0},{12,4},{1,9},{5,13},{9,1},{13,5},{2,10},{6,14},... | collective-permute-start | bytes 983048 | tf_op jit(solution)/shard_map/ppermute | solution.py:383
  29.6 4.4 %collective-permute-start.7 = (bf16[48,512]{1,0:T(8,128)(2,1)S(1)}, bf16[48,512]{1,0:T(8,128)(2,1)S(1)}, u32[]{:S(2)}, u32[]{:S(2)}) collective-permute-start(bf16[48,512]{1,0:T(8,128)(2,1)S(1)} %get-tuple-element.62), channel_id=1, source_target_pairs={{0,1},{1,0},{2,3},{3,2},{4,5},{5,4},{6,7},{7,6},{8,9},{9,8},{10,11... | collective-permute-start | bytes 147464 | tf_op jit(solution)/shard_map/ppermute | solution.py:383
  29.7 6.9 %collective-permute-start.8 = (bf16[48,512]{1,0:T(8,128)(2,1)S(1)}, bf16[48,512]{1,0:T(8,128)(2,1)S(1)}, u32[]{:S(2)}, u32[]{:S(2)}) collective-permute-start(bf16[48,512]{1,0:T(8,128)(2,1)S(1)} %get-tuple-element.63), channel_id=1, source_target_pairs={{0,2},{1,3},{2,0},{3,1},{4,6},{5,7},{6,4},{7,5},{8,10},{9,11},{10,... | collective-permute-start | bytes 147464 | tf_op jit(solution)/shard_map/ppermute | solution.py:383
  32.4 5.9 %collective-permute-start.9 = (bf16[48,512]{1,0:T(8,128)(2,1)S(1)}, bf16[48,512]{1,0:T(8,128)(2,1)S(1)}, u32[]{:S(2)}, u32[]{:S(2)}) collective-permute-start(bf16[48,512]{1,0:T(8,128)(2,1)S(1)} %get-tuple-element.64), channel_id=1, source_target_pairs={{0,3},{1,2},{2,1},{3,0},{4,7},{5,6},{6,5},{7,4},{8,11},{9,10},{10,... | collective-permute-start | bytes 147464 | tf_op jit(solution)/shard_map/ppermute | solution.py:383
  38.9 5.7 %collective-permute-start.10 = (bf16[4,48,512]{2,1,0:T(8,128)(2,1)S(1)}, bf16[4,48,512]{2,1,0:T(8,128)(2,1)S(1)}, u32[]{:S(2)}, u32[]{:S(2)}) collective-permute-start(bf16[4,48,512]{2,1,0:T(8,128)(2,1)S(1)} %shard_map.209.refs_0_), channel_id=1, source_target_pairs={{0,8},{4,12},{8,0},{12,4},{1,9},{5,13},{9,1},{13,5},{2,10},{6,14},... | collective-permute-start | bytes 589832 | tf_op jit(solution)/shard_map/ppermute | solution.py:383
  39.5 5.1 %collective-permute-start.15 = (bf16[80,512]{1,0:T(8,128)(2,1)S(1)}, bf16[80,512]{1,0:T(8,128)(2,1)S(1)}, u32[]{:S(2)}, u32[]{:S(2)}) collective-permute-start(bf16[80,512]{1,0:T(8,128)(2,1)S(1)} %get-tuple-element.70), channel_id=1, source_target_pairs={{0,1},{1,0},{2,3},{3,2},{4,5},{5,4},{6,7},{7,6},{8,9},{9,8},{10,11... | collective-permute-start | bytes 245768 | tf_op jit(solution)/shard_map/ppermute | solution.py:383
  39.6 7.0 %collective-permute-start.16 = (bf16[80,512]{1,0:T(8,128)(2,1)S(1)}, bf16[80,512]{1,0:T(8,128)(2,1)S(1)}, u32[]{:S(2)}, u32[]{:S(2)}) collective-permute-start(bf16[80,512]{1,0:T(8,128)(2,1)S(1)} %get-tuple-element.71), channel_id=1, source_target_pairs={{0,2},{1,3},{2,0},{3,1},{4,6},{5,7},{6,4},{7,5},{8,10},{9,11},{10,... | collective-permute-start | bytes 245768 | tf_op jit(solution)/shard_map/ppermute | solution.py:383
  41.7 6.3 %collective-permute-start.17 = (bf16[80,512]{1,0:T(8,128)(2,1)S(1)}, bf16[80,512]{1,0:T(8,128)(2,1)S(1)}, u32[]{:S(2)}, u32[]{:S(2)}) collective-permute-start(bf16[80,512]{1,0:T(8,128)(2,1)S(1)} %get-tuple-element.72), channel_id=1, source_target_pairs={{0,3},{1,2},{2,1},{3,0},{4,7},{5,6},{6,5},{7,4},{8,11},{9,10},{10,... | collective-permute-start | bytes 245768 | tf_op jit(solution)/shard_map/ppermute | solution.py:383
  48.1 6.4 %collective-permute-start.20 = (bf16[80,512]{1,0:T(8,128)(2,1)S(1)}, bf16[80,512]{1,0:T(8,128)(2,1)S(1)}, u32[]{:S(2)}, u32[]{:S(2)}) collective-permute-start(bf16[80,512]{1,0:T(8,128)(2,1)S(1)} %shard_map.212.refs_0_), channel_id=1, source_target_pairs={{0,3},{1,2},{2,1},{3,0},{4,7},{5,6},{6,5},{7,4},{8,11},{9,10},{10,... | collective-permute-start | bytes 245768 | tf_op jit(solution)/shard_map/ppermute | solution.py:383
  50.5 6.1 %collective-permute-start.19 = (bf16[80,512]{1,0:T(8,128)(2,1)S(1)}, bf16[80,512]{1,0:T(8,128)(2,1)S(1)}, u32[]{:S(2)}, u32[]{:S(2)}) collective-permute-start(bf16[80,512]{1,0:T(8,128)(2,1)S(1)} %shard_map.212.refs_0_), channel_id=1, source_target_pairs={{0,2},{1,3},{2,0},{3,1},{4,6},{5,7},{6,4},{7,5},{8,10},{9,11},{10,... | collective-permute-start | bytes 245768 | tf_op jit(solution)/shard_map/ppermute | solution.py:383
  51.4 5.3 %collective-permute-start.18 = (bf16[80,512]{1,0:T(8,128)(2,1)S(1)}, bf16[80,512]{1,0:T(8,128)(2,1)S(1)}, u32[]{:S(2)}, u32[]{:S(2)}) collective-permute-start(bf16[80,512]{1,0:T(8,128)(2,1)S(1)} %shard_map.212.refs_0_), channel_id=1, source_target_pairs={{0,1},{1,0},{2,3},{3,2},{4,5},{5,4},{6,7},{7,6},{8,9},{9,8},{10,11... | collective-permute-start | bytes 245768 | tf_op jit(solution)/shard_map/ppermute | solution.py:383
  56.7 7.1 %collective-permute-start.21 = (bf16[4,80,512]{2,1,0:T(8,128)(2,1)S(1)}, bf16[4,80,512]{2,1,0:T(8,128)(2,1)S(1)}, u32[]{:S(2)}, u32[]{:S(2)}) collective-permute-start(bf16[4,80,512]{2,1,0:T(8,128)(2,1)S(1)} %shard_map.213.refs_4_.own), channel_id=1, source_target_pairs={{0,8},{4,12},{8,0},{12,4},{1,9},{5,13},{9,1},{13,5},{2,10},{6,14},... | collective-permute-start | bytes 983048 | tf_op jit(solution)/shard_map/ppermute | solution.py:383
  58.3 1.4 %collective-permute-start.11 = (bf16[4,48,512]{2,1,0:T(8,128)(2,1)S(1)}, bf16[4,48,512]{2,1,0:T(8,128)(2,1)S(1)}, u32[]{:S(2)}, u32[]{:S(2)}) collective-permute-start(bf16[4,48,512]{2,1,0:T(8,128)(2,1)S(1)} %shard_map.209.refs_0_), channel_id=1, source_target_pairs={{0,4},{4,0},{8,12},{12,8},{1,5},{5,1},{9,13},{13,9},{2,6},{6,2},{1... | collective-permute-start | bytes 589832 | tf_op jit(solution)/shard_map/ppermute | solution.py:383
  58.3 1.7 %collective-permute-start.12 = (bf16[4,48,512]{2,1,0:T(8,128)(2,1)S(1)}, bf16[4,48,512]{2,1,0:T(8,128)(2,1)S(1)}, u32[]{:S(2)}, u32[]{:S(2)}) collective-permute-start(bf16[4,48,512]{2,1,0:T(8,128)(2,1)S(1)} %collective-permute-done.10._.refs_1_), channel_id=1, source_target_pairs={{0,4},{4,0},{8,12},{12,8},{1,5},{5,1},{9,13},{13,9},{2,6},{6,2},{1... | collective-permute-start | bytes 589832 | tf_op jit(solution)/shard_map/ppermute | solution.py:383
  61.2 2.7 %collective-permute-start.22 = (bf16[4,80,512]{2,1,0:T(8,128)(2,1)S(1)}, bf16[4,80,512]{2,1,0:T(8,128)(2,1)S(1)}, u32[]{:S(2)}, u32[]{:S(2)}) collective-permute-start(bf16[4,80,512]{2,1,0:T(8,128)(2,1)S(1)} %get-tuple-element.74), channel_id=1, source_target_pairs={{0,4},{4,0},{8,12},{12,8},{1,5},{5,1},{9,13},{13,9},{2,6},{6,2},{1... | collective-permute-start | bytes 983048 | tf_op jit(solution)/shard_map/ppermute | solution.py:383
  63.9 1.6 %collective-permute-start.23 = (bf16[4,80,512]{2,1,0:T(8,128)(2,1)S(1)}, bf16[4,80,512]{2,1,0:T(8,128)(2,1)S(1)}, u32[]{:S(2)}, u32[]{:S(2)}) collective-permute-start(bf16[4,80,512]{2,1,0:T(8,128)(2,1)S(1)} %collective-permute-done.21.over_x), channel_id=1, source_target_pairs={{0,4},{4,0},{8,12},{12,8},{1,5},{5,1},{9,13},{13,9},{2,6},{6,2},{1... | collective-permute-start | bytes 983048 | tf_op jit(solution)/shard_map/ppermute | solution.py:383

commit v6 on v5

--- a/solution.py
+++ b/solution.py
@@ -241,9 +241,9 @@
     refs[-1][...] = total.astype(BF16)
 
 
-def join_kernel(*refs):
+def join_kernel(place_ref, *refs):
     for m, ref in enumerate(refs[:-1]):
-        refs[-1][m] = ref[...]
+        refs[-1][place_ref[0] ^ m] = ref[...]
 
 
 def label_kernel(ids_ref, *refs):
@@ -278,31 +278,48 @@
     b2[...] = bias[2:3, :]
 
 
-def weights_kernel(place_ref, own, over_x, over_core, over_both, wenc, win, wmid, wout):
-    c, x, z = place_ref[0], place_ref[1], place_ref[2]
-    pieces = []
-    for m in range(4):
-        pieces.append((own.at[m], c, x, m))
-        pieces.append((over_x.at[m], c, 1 - x, m))
-        pieces.append((over_core.at[m], 1 - c, x, m))
-        pieces.append((over_both.at[m], 1 - c, 1 - x, m))
-    for ref, at_core, at_chip, m in pieces:
-        spot = at_chip * 4 + (z ^ m)
-        wide = pl.ds(pl.multiple_of((at_core * 8 + spot) * 32, 32), 32)
-        narrow = pl.ds(pl.multiple_of(spot * 16, 16), 16)
-        wout[wide, :] = ref[0:32, :]
-        wmid[wide, :] = ref[32:64, :]
-
-        @pl.when(at_core == 0)
-        def _():
-            win[narrow, :] = ref[64:80, :]
-
-        @pl.when(at_core != 0)
-        def _():
-            wenc[narrow, :] = ref[64:80, :]
-
-
-def call(kernel, out_shape, in_specs, *args, out_specs=None, scratch=(), flops=0, limit=LIMIT):
+def place_shards(sources, outs, sems):
+    wenc, win, wmid, wout = outs
+    copies = []
+    for i, (ref, at_core, at_chip) in enumerate(sources):
+        count = ref.shape[0]
+        wide = pl.ds((at_core * 2 + at_chip) * count, count)
+        narrow = pl.ds(at_chip * count, count)
+        for k, (rows, out, where, on) in enumerate(
+            (
+                (pl.ds(0, 32), wout, wide, None),
+                (pl.ds(32, 32), wmid, wide, None),
+                (pl.ds(64, 16), win, narrow, at_core == 0),
+                (pl.ds(64, 16), wenc, narrow, at_core != 0),
+            )
+        ):
+            copy = pltpu.make_async_copy(
+                ref.at[:, rows, :], out.at[where], sems.at[i * 3 + min(k, 2)]
+            )
+            copies.append((copy, on))
+    for copy, on in copies:
+        if on is None:
+            copy.start()
+        else:
+            pl.when(on)(copy.start)
+    for copy, on in copies:
+        if on is None:
+            copy.wait()
+        else:
+            pl.when(on)(copy.wait)
+
+
+def weights_kernel(place_ref, own, over_x, over_core, *refs):
+    c, x = place_ref[0], place_ref[1]
+    place_shards(((own, c, x), (over_x, c, 1 - x), (over_core, 1 - c, x)), refs[:4], refs[4])
+
+
+def last_weights_kernel(place_ref, over_both, *refs):
+    c, x = place_ref[0], place_ref[1]
+    place_shards(((over_both, 1 - c, 1 - x),), refs[4:8], refs[8])
+
+
+def call(kernel, out_shape, in_specs, *args, out_specs=None, scratch=(), flops=0, limit=LIMIT, aliases=None):
     many = isinstance(out_shape, (list, tuple))
     return pl.pallas_call(
         kernel,
@@ -310,6 +327,7 @@
         in_specs=in_specs,
         out_specs=out_specs or ([VMEM] * len(out_shape) if many else VMEM),
         scratch_shapes=scratch,
+        input_output_aliases=aliases or {},
         compiler_params=pltpu.CompilerParams(vmem_limit_bytes=limit),
         cost_estimate=pl.CostEstimate(flops=flops, bytes_accessed=1 << 20, transcendentals=0),
     )(*args)
@@ -434,7 +452,7 @@
     total = call(sum_kernel, shape((80, hidden)), [ANY] + [VMEM] * n_sub, terms_x, *shards)
     totals = [total] + [swap(total, "sub", m, n_sub) for m in along_z]
     terms = [terms, terms_x, swap(terms, "region", 1, 4), swap(terms_x, "region", 1, 4)]
-    own = call(join_kernel, shape((n_sub, 80, hidden)), [VMEM] * n_sub, *totals)
+    own = call(join_kernel, shape((n_sub, 80, hidden)), [SMEM] + [VMEM] * n_sub, me.reshape(1), *totals)
     over_x = swap(own, "region", 2, 4)
     surf, benc, b1, b2, passed = call(
         surface_kernel,
@@ -447,24 +465,39 @@
     )
     over_core = swap(passed, "region", 1, 4)
     over_both = swap(over_x, "region", 1, 4)
-    wenc, win, wmid, wout = call(
+    place = jnp.stack([core, chip])
+    grads = [shape((8, 16, hidden))] * 2 + [shape((16, 32, hidden))] * 2
+    some = call(
         weights_kernel,
-        [shape((128, hidden)), shape((128, hidden)), shape((512, hidden)), shape((512, hidden))],
-        [SMEM] + [VMEM] * 4,
-        jnp.stack([core, chip, me]),
+        grads,
+        [SMEM] + [VMEM] * 3,
+        place,
         own,
         over_x,
         over_core,
+        out_specs=[HBM] * 4,
+        scratch=[pltpu.SemaphoreType.DMA((9,))],
+        flops=1 << 30,
+    )
+    wenc, win, wmid, wout = call(
+        last_weights_kernel,
+        grads,
+        [SMEM, VMEM] + [HBM] * 4,
+        place,
         over_both,
+        *some,
+        out_specs=[HBM] * 4,
+        scratch=[pltpu.SemaphoreType.DMA((3,))],
+        aliases={2 + i: i for i in range(4)},
     )
     return (
         surf.reshape(surface.shape),
-        wenc,
+        wenc.reshape(128, hidden),
         benc.reshape(hidden),
-        win,
-        wmid,
+        win.reshape(128, hidden),
+        wmid.reshape(512, hidden),
         b1.reshape(hidden),
-        wout,
+        wout.reshape(512, hidden),
         b2.reshape(hidden),
     )
 

time: 67.5 us -> 67.1 us (level)
  waiting for transfers between devices: 24.1 us -> 22.5 us
  Pallas kernels: 12.9 us -> 14 us
    ppermute x24, waiting for transfers between devices: 24.1 us -> 22.5 us  [swap(): return lax.ppermute(value, axis, [(i, i ^ mask) for i in range(size)])]
    pallas_call x10 -> x11, Pallas kernels: 12.9 us -> 14 us  [call(): pl.pallas_call(kernel, out_shape=out_shape, in_specs=in_specs, out_specs=...]
  transfers between devices with their start and end apart: 24 -> 24, of which waited for: 16 -> 15; matrix products, arithmetic and copies ran while one was open for 0% -> 0% of each run, Pallas kernels for 6% -> 8%
where the time goes in v6:
time: 67.1 us; the launch traced here: 66.8 us
  starting transfers between devices  28 us (42%)
  waiting for transfers between devices  22.5 us (34%)
  Pallas kernels  14 us (21%)
  between operations  1.43 us (2%)
    ppermute x24, starting transfers between devices, swap(): return lax.ppermute(value, axis, [(i, i ^ mask) for i in range(size)])  28 us
    ppermute x24, waiting for transfers between devices, swap(): return lax.ppermute(value, axis, [(i, i ^ mask) for i in range(size)])  22.5 us
    pallas_call x11, Pallas kernels, call(): pl.pallas_call(kernel, out_shape=out_shape, in_specs=in_specs, out_specs=...  14 us
  transfers between devices with their start and end apart: 24, of which 15 were waited for; matrix products, arithmetic and copies ran while one was open for 0% of the time, Pallas kernels for 8%

profile of v6, /device:TPU:0, one launch (start us, length us, event | category | flops | bytes accessed | tf_op | source)
XLA Modules:
  0.0 66.8 jit_solution(235770536926993016)
XLA Ops:
  0.6 0.5 collective-permute-start.3
  1.2 0.0 copy-start
  1.2 0.0 copy-start.1
  1.2 0.7 copy-done
  1.8 0.0 copy-done.1
  1.8 0.1 add_bitcast_fusion.refs_0_
  1.9 4.6 %collective-permute-start.2 = (s32[1,8]{1,0:T(1,128)S(1)}, s32[1,8]{1,0:T(1,128)S(1)}, u32[]{:S(2)}, u32[]{:S(2)}) collective-permute-start(s32[1,8]{1,0:T(1,128)S(1)} %add_bitcast_fusion.refs_0_), channel_id=1, source_target_pairs={{0,3},{1,2},{2,1},{3,0},{4,7},{5,6},{6,5},{7,4},{8,11},{9,10},{10,... | collective-permute-start | bytes 104 | tf_op jit(solution)/shard_map/ppermute | solution.py:401
  6.5 0.0 collective-permute-start.1
  6.5 0.6 collective-permute-start
  7.8 0.1 pad_add_fusion.place_ref
  7.9 0.1 collective-permute-done.2.refs_3_
  8.0 2.9 %collective-permute-done.1.refs_2_ = s32[1,8]{1,0:T(1,128)S(1)} collective-permute-done((s32[1,8]{1,0:T(1,128)S(1)}, s32[1,8]{1,0:T(1,128)S(1)}, u32[]{:S(2)}, u32[]{:S(2)}) %collective-permute-start.1) | collective-permute-done | bytes 64 | tf_op jit(solution)/shard_map/ppermute | solution.py:401
  10.9 0.0 collective-permute-done.refs_1_
  11.0 0.0 collective-permute-done.3.refs_4_
  11.0 1.2 %shard_map.206 = (bf16[128,128]{1,0:T(8,128)(2,1)S(1)}, bf16[128,128]{1,0:T(8,128)(2,1)S(1)}, bf16[128,128]{1,0:T(8,128)(2,1)S(1)}, bf16[128,128]{1,0:T(8,128)(2,1)S(1)}, s32[4]{0:T(128)S(1)}) custom-call(s32[1]{0:T(128)} %bitcast.me_ref.place_ref, s32[1,8]{1,0:T(1,128)S(1)} %add_bitcast_fusion.refs_0_, s32[1,8]{1,0:T(1,128)S(1)} %collective-permute-done.refs_1_, ...), custom_call_target="tpu_custom_call" | custom-call | bytes 1048576 | tf_op jit(solution)/shard_map/pallas_call | solution.py:324
  12.1 0.1 collective-permute-start.4
  12.2 2.1 %collective-permute-start.5 = (bf16[128,128]{1,0:T(8,128)(2,1)S(1)}, bf16[128,128]{1,0:T(8,128)(2,1)S(1)}, u32[]{:S(2)}, u32[]{:S(2)}) collective-permute-start(bf16[128,128]{1,0:T(8,128)(2,1)S(1)} %get-tuple-element.52), channel_id=1, source_target_pairs={{0,2},{1,3},{2,0},{3,1},{4,6},{5,7},{6,4},{7,5},{8,10},{9,11},{10,... | collective-permute-start | bytes 98312 | tf_op jit(solution)/shard_map/ppermute | solution.py:401
  14.3 2.3 %collective-permute-start.6 = (bf16[128,128]{1,0:T(8,128)(2,1)S(1)}, bf16[128,128]{1,0:T(8,128)(2,1)S(1)}, u32[]{:S(2)}, u32[]{:S(2)}) collective-permute-start(bf16[128,128]{1,0:T(8,128)(2,1)S(1)} %get-tuple-element.53), channel_id=1, source_target_pairs={{0,3},{1,2},{2,1},{3,0},{4,7},{5,6},{6,5},{7,4},{8,11},{9,10},{10,... | collective-permute-start | bytes 98312 | tf_op jit(solution)/shard_map/ppermute | solution.py:401
  16.6 2.2 %shard_map.207 = (bf16[512,128]{1,0:T(8,128)(2,1)S(1)}, bf16[128,512]{1,0:T(8,128)(2,1)S(1)}, bf16[512,512]{1,0:T(8,128)(2,1)S(1)}, bf16[512,512]{1,0:T(8,128)(2...) custom-call(s32[1]{0:T(128)S(6)} %copy.31.count_ref, ...), custom_call_target="tpu_custom_call" | custom-call | flops 1073741824 | bytes 1048576 | tf_op jit(solution)/shard_map/pallas_call | solution.py:324
  18.8 0.0 collective-permute-done.4.refs_1_
  18.8 0.0 collective-permute-done.5.refs_2_
  18.9 1.2 %collective-permute-done.6.refs_3_ = bf16[128,128]{1,0:T(8,128)(2,1)S(1)} collective-permute-done((bf16[128,128]{1,0:T(8,128)(2,1)S(1)}, bf16[128,128]{1,0:T(8,128)(2,1)S(1)}, u32[]{:S(2)}, u32[]{:S(2)}) %collective-permute-start.6) | collective-permute-done | bytes 32800 | tf_op jit(solution)/shard_map/ppermute | solution.py:401
  20.0 5.6 %shard_map.208 = (bf16[8,80,512]{2,1,0:T(8,128)(2,1)S(1)}, bf16[8,80,512]{2,1,0:T(8,128)(2,1)S(1)}, bf16[48,512]{1,0:T(8,128)(2,1)S(1)}, bf16[48,512]{1,0:T(8,12...) custom-call(s32[2]{0:T(128)S(1)} %pad_add_fusion.place_ref, s32[4]{0:T(128)S(1)} %bitcast.21, ...), custom_call_target="tpu_custom_call" | custom-call | flops 2147483648 | bytes 1048576 | tf_op jit(solution)/shard_map/pallas_call | solution.py:324
  25.7 0.1 collective-permute-start.13
  25.8 2.1 %collective-permute-done.13.got_ref = bf16[8,80,512]{2,1,0:T(8,128)(2,1)S(1)} collective-permute-done((bf16[8,80,512]{2,1,0:T(8,128)(2,1)S(1)}, bf16[8,80,512]{2,1,0:T(8,128)(2,1)S(1)}, u32[]{:S(2)}, u32[]{:S(2)}) %collective-permute-start.13) | collective-permute-done | bytes 655392 | tf_op jit(solution)/shard_map/ppermute | solution.py:401
  27.8 0.2 shard_map.210
  28.0 1.6 %collective-permute-start.14 = (bf16[4,80,512]{2,1,0:T(8,128)(2,1)S(1)}, bf16[4,80,512]{2,1,0:T(8,128)(2,1)S(1)}, u32[]{:S(2)}, u32[]{:S(2)}) collective-permute-start(bf16[4,80,512]{2,1,0:T(8,128)(2,1)S(1)} %get-tuple-element.72), channel_id=1, source_target_pairs={{0,8},{4,12},{8,0},{12,4},{1,9},{5,13},{9,1},{13,5},{2,10},{6,14},... | collective-permute-start | bytes 983048 | tf_op jit(solution)/shard_map/ppermute | solution.py:401
  29.6 0.2 collective-permute-start.7
  29.7 2.7 %collective-permute-start.8 = (bf16[48,512]{1,0:T(8,128)(2,1)S(1)}, bf16[48,512]{1,0:T(8,128)(2,1)S(1)}, u32[]{:S(2)}, u32[]{:S(2)}) collective-permute-start(bf16[48,512]{1,0:T(8,128)(2,1)S(1)} %get-tuple-element.67), channel_id=1, source_target_pairs={{0,2},{1,3},{2,0},{3,1},{4,6},{5,7},{6,4},{7,5},{8,10},{9,11},{10,... | collective-permute-start | bytes 147464 | tf_op jit(solution)/shard_map/ppermute | solution.py:401
  32.4 1.5 %collective-permute-start.9 = (bf16[48,512]{1,0:T(8,128)(2,1)S(1)}, bf16[48,512]{1,0:T(8,128)(2,1)S(1)}, u32[]{:S(2)}, u32[]{:S(2)}) collective-permute-start(bf16[48,512]{1,0:T(8,128)(2,1)S(1)} %get-tuple-element.68), channel_id=1, source_target_pairs={{0,3},{1,2},{2,1},{3,0},{4,7},{5,6},{6,5},{7,4},{8,11},{9,10},{10,... | collective-permute-start | bytes 147464 | tf_op jit(solution)/shard_map/ppermute | solution.py:401
  33.9 0.0 collective-permute-done.7.refs_1_.refs_0_
  34.0 2.7 %collective-permute-done.8.refs_2_.refs_1_ = bf16[48,512]{1,0:T(8,128)(2,1)S(1)} collective-permute-done((bf16[48,512]{1,0:T(8,128)(2,1)S(1)}, bf16[48,512]{1,0:T(8,128)(2,1)S(1)}, u32[]{:S(2)}, u32[]{:S(2)}) %collective-permute-start.8) | collective-permute-done | bytes 49184 | tf_op jit(solution)/shard_map/ppermute | solution.py:401
  36.6 1.6 %collective-permute-done.9.refs_3_.refs_2_ = bf16[48,512]{1,0:T(8,128)(2,1)S(1)} collective-permute-done((bf16[48,512]{1,0:T(8,128)(2,1)S(1)}, bf16[48,512]{1,0:T(8,128)(2,1)S(1)}, u32[]{:S(2)}, u32[]{:S(2)}) %collective-permute-start.9) | collective-permute-done | bytes 49184 | tf_op jit(solution)/shard_map/ppermute | solution.py:401
  38.3 0.6 shard_map.209.refs_0_
  38.9 0.6 collective-permute-start.10
  39.5 0.0 collective-permute-done.14.got_ref
  39.5 0.1 shard_map.211
  39.5 0.1 collective-permute-start.15
  39.6 2.1 %collective-permute-start.16 = (bf16[80,512]{1,0:T(8,128)(2,1)S(1)}, bf16[80,512]{1,0:T(8,128)(2,1)S(1)}, u32[]{:S(2)}, u32[]{:S(2)}) collective-permute-start(bf16[80,512]{1,0:T(8,128)(2,1)S(1)} %get-tuple-element.75), channel_id=1, source_target_pairs={{0,2},{1,3},{2,0},{3,1},{4,6},{5,7},{6,4},{7,5},{8,10},{9,11},{10,... | collective-permute-start | bytes 245768 | tf_op jit(solution)/shard_map/ppermute | solution.py:401
  41.7 2.3 %collective-permute-start.17 = (bf16[80,512]{1,0:T(8,128)(2,1)S(1)}, bf16[80,512]{1,0:T(8,128)(2,1)S(1)}, u32[]{:S(2)}, u32[]{:S(2)}) collective-permute-start(bf16[80,512]{1,0:T(8,128)(2,1)S(1)} %get-tuple-element.76), channel_id=1, source_target_pairs={{0,3},{1,2},{2,1},{3,0},{4,7},{5,6},{6,5},{7,4},{8,11},{9,10},{10,... | collective-permute-start | bytes 245768 | tf_op jit(solution)/shard_map/ppermute | solution.py:401
  44.0 0.6 collective-permute-done.10._.refs_1_
  44.6 0.0 collective-permute-done.15.refs_1_
  44.6 2.1 %collective-permute-done.16.refs_2_ = bf16[80,512]{1,0:T(8,128)(2,1)S(1)} collective-permute-done((bf16[80,512]{1,0:T(8,128)(2,1)S(1)}, bf16[80,512]{1,0:T(8,128)(2,1)S(1)}, u32[]{:S(2)}, u32[]{:S(2)}) %collective-permute-start.16) | collective-permute-done | bytes 81952 | tf_op jit(solution)/shard_map/ppermute | solution.py:401
  46.7 1.4 %collective-permute-done.17.refs_3_ = bf16[80,512]{1,0:T(8,128)(2,1)S(1)} collective-permute-done((bf16[80,512]{1,0:T(8,128)(2,1)S(1)}, bf16[80,512]{1,0:T(8,128)(2,1)S(1)}, u32[]{:S(2)}, u32[]{:S(2)}) %collective-permute-start.17) | collective-permute-done | bytes 81952 | tf_op jit(solution)/shard_map/ppermute | solution.py:401
  48.1 2.3 %collective-permute-start.20 = (bf16[80,512]{1,0:T(8,128)(2,1)S(1)}, bf16[80,512]{1,0:T(8,128)(2,1)S(1)}, u32[]{:S(2)}, u32[]{:S(2)}) collective-permute-start(bf16[80,512]{1,0:T(8,128)(2,1)S(1)} %shard_map.212.refs_0_), channel_id=1, source_target_pairs={{0,3},{1,2},{2,1},{3,0},{4,7},{5,6},{6,5},{7,4},{8,11},{9,10},{10,... | collective-permute-start | bytes 245768 | tf_op jit(solution)/shard_map/ppermute | solution.py:401
  50.5 0.9 %collective-permute-start.19 = (bf16[80,512]{1,0:T(8,128)(2,1)S(1)}, bf16[80,512]{1,0:T(8,128)(2,1)S(1)}, u32[]{:S(2)}, u32[]{:S(2)}) collective-permute-start(bf16[80,512]{1,0:T(8,128)(2,1)S(1)} %shard_map.212.refs_0_), channel_id=1, source_target_pairs={{0,2},{1,3},{2,0},{3,1},{4,6},{5,7},{6,4},{7,5},{8,10},{9,11},{10,... | collective-permute-start | bytes 245768 | tf_op jit(solution)/shard_map/ppermute | solution.py:401
  51.4 1.2 %collective-permute-start.18 = (bf16[80,512]{1,0:T(8,128)(2,1)S(1)}, bf16[80,512]{1,0:T(8,128)(2,1)S(1)}, u32[]{:S(2)}, u32[]{:S(2)}) collective-permute-start(bf16[80,512]{1,0:T(8,128)(2,1)S(1)} %shard_map.212.refs_0_), channel_id=1, source_target_pairs={{0,1},{1,0},{2,3},{3,2},{4,5},{5,4},{6,7},{7,6},{8,9},{9,8},{10,11... | collective-permute-start | bytes 245768 | tf_op jit(solution)/shard_map/ppermute | solution.py:401
  52.6 2.0 %collective-permute-done.20.refs_3_ = bf16[80,512]{1,0:T(8,128)(2,1)S(1)} collective-permute-done((bf16[80,512]{1,0:T(8,128)(2,1)S(1)}, bf16[80,512]{1,0:T(8,128)(2,1)S(1)}, u32[]{:S(2)}, u32[]{:S(2)}) %collective-permute-start.20) | collective-permute-done | bytes 81952 | tf_op jit(solution)/shard_map/ppermute | solution.py:401
  54.5 2.0 %collective-permute-done.19.refs_2_ = bf16[80,512]{1,0:T(8,128)(2,1)S(1)} collective-permute-done((bf16[80,512]{1,0:T(8,128)(2,1)S(1)}, bf16[80,512]{1,0:T(8,128)(2,1)S(1)}, u32[]{:S(2)}, u32[]{:S(2)}) %collective-permute-start.19) | collective-permute-done | bytes 81952 | tf_op jit(solution)/shard_map/ppermute | solution.py:401
  56.6 0.2 collective-permute-done.18.refs_1_
  56.7 1.6 %collective-permute-start.21 = (bf16[4,80,512]{2,1,0:T(8,128)(2,1)S(1)}, bf16[4,80,512]{2,1,0:T(8,128)(2,1)S(1)}, u32[]{:S(2)}, u32[]{:S(2)}) collective-permute-start(bf16[4,80,512]{2,1,0:T(8,128)(2,1)S(1)} %shard_map.213.refs_4_.own), channel_id=1, source_target_pairs={{0,8},{4,12},{8,0},{12,4},{1,9},{5,13},{9,1},{13,5},{2,10},{6,14},... | collective-permute-start | bytes 983048 | tf_op jit(solution)/shard_map/ppermute | solution.py:401
  58.3 0.0 collective-permute-start.11
  58.3 0.5 collective-permute-start.12
  58.8 0.9 %collective-permute-done.11.refs_2_ = bf16[4,48,512]{2,1,0:T(8,128)(2,1)S(1)} collective-permute-done((bf16[4,48,512]{2,1,0:T(8,128)(2,1)S(1)}, bf16[4,48,512]{2,1,0:T(8,128)(2,1)S(1)}, u32[]{:S(2)}, u32[]{:S(2)}) %collective-permute-start.11) | collective-permute-done | bytes 196640 | tf_op jit(solution)/shard_map/ppermute | solution.py:401
  59.7 0.3 collective-permute-done.12.refs_3_
  60.0 1.2 %shard_map.214 = (f32[16,128,128]{2,1,0:T(8,128)}, f32[1,512]{1,0:T(1,128)}, f32[1,512]{1,0:T(1,128)}, f32[1,512]{1,0:T(1,128)}, bf16[4,80,512]{2,1,0:T(8,128)(2,1)S(1)}) custom-call(bf16[4,48,512]{2,1,0:T(8,128)(2,1)S(1)} %shard_map.209.refs_0_, bf16[4,48,512]{2,1,0:T(8,128)(2,1)S(1)} %collective-permute-done.10._.refs_1_, ...), custom_call_target="tpu_custom_call" | custom-call | bytes 1048576 | tf_op jit(solution)/shard_map/pallas_call | solution.py:324
  61.2 0.2 collective-permute-start.23
  61.5 2.4 %collective-permute-done.21.over_x = bf16[4,80,512]{2,1,0:T(8,128)(2,1)S(1)} collective-permute-done((bf16[4,80,512]{2,1,0:T(8,128)(2,1)S(1)}, bf16[4,80,512]{2,1,0:T(8,128)(2,1)S(1)}, u32[]{:S(2)}, u32[]{:S(2)}) %collective-permute-start.21) | collective-permute-done | bytes 327712 | tf_op jit(solution)/shard_map/ppermute | solution.py:401
  63.9 0.0 collective-permute-start.22
  63.9 0.1 pad_add_fusion.1.place_ref
  64.0 0.0 collective-permute-done.23.over_core
  64.0 1.6 %shard_map.215 = (bf16[8,16,512]{2,1,0:T(8,128)(2,1)}, bf16[8,16,512]{2,1,0:T(8,128)(2,1)}, bf16[16,32,512]{2,1,0:T(8,128)(2,1)}, bf16[16,32,512]{2,1,0:T(8,128)(2,1)}) custom-call(s32[2]{0:T(128)S(1)} %pad_add_fusion.1.place_ref, bf16[4,80,512]{2,1,0:T(8,128)(2,1)S(1)} %shard_map.213.refs_4_.own, bf16[4,80,512]{2,1,0:T(8,128)(2,1)S(1)} %collective-permute-done.21.over_x, ...), custom_call_target="tpu_custom_call" | custom-call | flops 1073741824 | bytes 1048576 | tf_op jit(solution)/shard_map/pallas_call | solution.py:324
  65.5 0.0 collective-permute-done.22.over_both
  65.5 1.3 %shard_map.216 = (bf16[8,16,512]{2,1,0:T(8,128)(2,1)}, bf16[8,16,512]{2,1,0:T(8,128)(2,1)}, bf16[16,32,512]{2,1,0:T(8,128)(2,1)}, bf16[16,32,512]{2,1,0:T(8,128)(2,1)}) custom-call(s32[2]{0:T(128)S(1)} %pad_add_fusion.1.place_ref, ...), custom_call_target="tpu_custom_call", output_to_operand_aliasing={{0}: (2, {}), {1}: (3, {}), {2}: (4, {}), {3}: (5, {})} | custom-call | bytes 1048576 | tf_op jit(solution)/shard_map/pallas_call | solution.py:324
  (2 shorter events, 0.1 us)
Async XLA Ops:
  0.6 10.3 %collective-permute-start.3 = (bf16[2048,128]{1,0:T(8,128)(2,1)}, bf16[2048,128]{1,0:T(8,128)(2,1)S(1)}, u32[]{:S(2)}, u32[]{:S(2)}) collective-permute-start(bf16[2048,128]{1,0:T(8,128)(2,1)} %param.17), channel_id=1, source_target_pairs={{0,4},{4,0},{8,12},{12,8},{1,5},{5,1},{9,13},{13,9},{2,6},{6,2},{1... | collective-permute-start | bytes 1572872 | tf_op jit(solution)/shard_map/ppermute | solution.py:401
  1.2 0.7 copy-start
  1.2 0.7 %copy-start.1 = (s32[1,4]{1,0:T(1,128)S(1)}, s32[1,4]{1,0:T(1,128)}, u32[]{:S(2)}) copy-start(s32[1,4]{1,0:T(1,128)} %param.26) | copy-start | bytes 52
  1.9 6.1 %collective-permute-start.2 = (s32[1,8]{1,0:T(1,128)S(1)}, s32[1,8]{1,0:T(1,128)S(1)}, u32[]{:S(2)}, u32[]{:S(2)}) collective-permute-start(s32[1,8]{1,0:T(1,128)S(1)} %add_bitcast_fusion.refs_0_), channel_id=1, source_target_pairs={{0,3},{1,2},{2,1},{3,0},{4,7},{5,6},{6,5},{7,4},{8,11},{9,10},{10,... | collective-permute-start | bytes 104 | tf_op jit(solution)/shard_map/ppermute | solution.py:401
  6.5 4.4 %collective-permute-start.1 = (s32[1,8]{1,0:T(1,128)S(1)}, s32[1,8]{1,0:T(1,128)S(1)}, u32[]{:S(2)}, u32[]{:S(2)}) collective-permute-start(s32[1,8]{1,0:T(1,128)S(1)} %add_bitcast_fusion.refs_0_), channel_id=1, source_target_pairs={{0,2},{1,3},{2,0},{3,1},{4,6},{5,7},{6,4},{7,5},{8,10},{9,11},{10,... | collective-permute-start | bytes 104 | tf_op jit(solution)/shard_map/ppermute | solution.py:401
  6.5 4.4 %collective-permute-start = (s32[1,8]{1,0:T(1,128)S(1)}, s32[1,8]{1,0:T(1,128)S(1)}, u32[]{:S(2)}, u32[]{:S(2)}) collective-permute-start(s32[1,8]{1,0:T(1,128)S(1)} %add_bitcast_fusion.refs_0_), channel_id=1, source_target_pairs={{0,1},{1,0},{2,3},{3,2},{4,5},{5,4},{6,7},{7,6},{8,9},{9,8},{10,11... | collective-permute-start | bytes 104 | tf_op jit(solution)/shard_map/ppermute | solution.py:401
  12.1 6.7 %collective-permute-start.4 = (bf16[128,128]{1,0:T(8,128)(2,1)S(1)}, bf16[128,128]{1,0:T(8,128)(2,1)S(1)}, u32[]{:S(2)}, u32[]{:S(2)}) collective-permute-start(bf16[128,128]{1,0:T(8,128)(2,1)S(1)} %get-tuple-element.51), channel_id=1, source_target_pairs={{0,1},{1,0},{2,3},{3,2},{4,5},{5,4},{6,7},{7,6},{8,9},{9,8},{10,11... | collective-permute-start | bytes 98312 | tf_op jit(solution)/shard_map/ppermute | solution.py:401
  12.2 6.6 %collective-permute-start.5 = (bf16[128,128]{1,0:T(8,128)(2,1)S(1)}, bf16[128,128]{1,0:T(8,128)(2,1)S(1)}, u32[]{:S(2)}, u32[]{:S(2)}) collective-permute-start(bf16[128,128]{1,0:T(8,128)(2,1)S(1)} %get-tuple-element.52), channel_id=1, source_target_pairs={{0,2},{1,3},{2,0},{3,1},{4,6},{5,7},{6,4},{7,5},{8,10},{9,11},{10,... | collective-permute-start | bytes 98312 | tf_op jit(solution)/shard_map/ppermute | solution.py:401
  14.3 5.7 %collective-permute-start.6 = (bf16[128,128]{1,0:T(8,128)(2,1)S(1)}, bf16[128,128]{1,0:T(8,128)(2,1)S(1)}, u32[]{:S(2)}, u32[]{:S(2)}) collective-permute-start(bf16[128,128]{1,0:T(8,128)(2,1)S(1)} %get-tuple-element.53), channel_id=1, source_target_pairs={{0,3},{1,2},{2,1},{3,0},{4,7},{5,6},{6,5},{7,4},{8,11},{9,10},{10,... | collective-permute-start | bytes 98312 | tf_op jit(solution)/shard_map/ppermute | solution.py:401
  25.7 2.2 %collective-permute-start.13 = (bf16[8,80,512]{2,1,0:T(8,128)(2,1)S(1)}, bf16[8,80,512]{2,1,0:T(8,128)(2,1)S(1)}, u32[]{:S(2)}, u32[]{:S(2)}) collective-permute-start(bf16[8,80,512]{2,1,0:T(8,128)(2,1)S(1)} %get-tuple-element.70), channel_id=1, source_target_pairs={{0,4},{4,0},{8,12},{12,8},{1,5},{5,1},{9,13},{13,9},{2,6},{6,2},{1... | collective-permute-start | bytes 1966088 | tf_op jit(solution)/shard_map/ppermute | solution.py:401
  28.0 11.5 %collective-permute-start.14 = (bf16[4,80,512]{2,1,0:T(8,128)(2,1)S(1)}, bf16[4,80,512]{2,1,0:T(8,128)(2,1)S(1)}, u32[]{:S(2)}, u32[]{:S(2)}) collective-permute-start(bf16[4,80,512]{2,1,0:T(8,128)(2,1)S(1)} %get-tuple-element.72), channel_id=1, source_target_pairs={{0,8},{4,12},{8,0},{12,4},{1,9},{5,13},{9,1},{13,5},{2,10},{6,14},... | collective-permute-start | bytes 983048 | tf_op jit(solution)/shard_map/ppermute | solution.py:401
  29.6 4.4 %collective-permute-start.7 = (bf16[48,512]{1,0:T(8,128)(2,1)S(1)}, bf16[48,512]{1,0:T(8,128)(2,1)S(1)}, u32[]{:S(2)}, u32[]{:S(2)}) collective-permute-start(bf16[48,512]{1,0:T(8,128)(2,1)S(1)} %get-tuple-element.66), channel_id=1, source_target_pairs={{0,1},{1,0},{2,3},{3,2},{4,5},{5,4},{6,7},{7,6},{8,9},{9,8},{10,11... | collective-permute-start | bytes 147464 | tf_op jit(solution)/shard_map/ppermute | solution.py:401
  29.7 6.9 %collective-permute-start.8 = (bf16[48,512]{1,0:T(8,128)(2,1)S(1)}, bf16[48,512]{1,0:T(8,128)(2,1)S(1)}, u32[]{:S(2)}, u32[]{:S(2)}) collective-permute-start(bf16[48,512]{1,0:T(8,128)(2,1)S(1)} %get-tuple-element.67), channel_id=1, source_target_pairs={{0,2},{1,3},{2,0},{3,1},{4,6},{5,7},{6,4},{7,5},{8,10},{9,11},{10,... | collective-permute-start | bytes 147464 | tf_op jit(solution)/shard_map/ppermute | solution.py:401
  32.4 5.9 %collective-permute-start.9 = (bf16[48,512]{1,0:T(8,128)(2,1)S(1)}, bf16[48,512]{1,0:T(8,128)(2,1)S(1)}, u32[]{:S(2)}, u32[]{:S(2)}) collective-permute-start(bf16[48,512]{1,0:T(8,128)(2,1)S(1)} %get-tuple-element.68), channel_id=1, source_target_pairs={{0,3},{1,2},{2,1},{3,0},{4,7},{5,6},{6,5},{7,4},{8,11},{9,10},{10,... | collective-permute-start | bytes 147464 | tf_op jit(solution)/shard_map/ppermute | solution.py:401
  38.9 5.7 %collective-permute-start.10 = (bf16[4,48,512]{2,1,0:T(8,128)(2,1)S(1)}, bf16[4,48,512]{2,1,0:T(8,128)(2,1)S(1)}, u32[]{:S(2)}, u32[]{:S(2)}) collective-permute-start(bf16[4,48,512]{2,1,0:T(8,128)(2,1)S(1)} %shard_map.209.refs_0_), channel_id=1, source_target_pairs={{0,8},{4,12},{8,0},{12,4},{1,9},{5,13},{9,1},{13,5},{2,10},{6,14},... | collective-permute-start | bytes 589832 | tf_op jit(solution)/shard_map/ppermute | solution.py:401
  39.5 5.1 %collective-permute-start.15 = (bf16[80,512]{1,0:T(8,128)(2,1)S(1)}, bf16[80,512]{1,0:T(8,128)(2,1)S(1)}, u32[]{:S(2)}, u32[]{:S(2)}) collective-permute-start(bf16[80,512]{1,0:T(8,128)(2,1)S(1)} %get-tuple-element.74), channel_id=1, source_target_pairs={{0,1},{1,0},{2,3},{3,2},{4,5},{5,4},{6,7},{7,6},{8,9},{9,8},{10,11... | collective-permute-start | bytes 245768 | tf_op jit(solution)/shard_map/ppermute | solution.py:401
  39.6 7.0 %collective-permute-start.16 = (bf16[80,512]{1,0:T(8,128)(2,1)S(1)}, bf16[80,512]{1,0:T(8,128)(2,1)S(1)}, u32[]{:S(2)}, u32[]{:S(2)}) collective-permute-start(bf16[80,512]{1,0:T(8,128)(2,1)S(1)} %get-tuple-element.75), channel_id=1, source_target_pairs={{0,2},{1,3},{2,0},{3,1},{4,6},{5,7},{6,4},{7,5},{8,10},{9,11},{10,... | collective-permute-start | bytes 245768 | tf_op jit(solution)/shard_map/ppermute | solution.py:401
  41.7 6.3 %collective-permute-start.17 = (bf16[80,512]{1,0:T(8,128)(2,1)S(1)}, bf16[80,512]{1,0:T(8,128)(2,1)S(1)}, u32[]{:S(2)}, u32[]{:S(2)}) collective-permute-start(bf16[80,512]{1,0:T(8,128)(2,1)S(1)} %get-tuple-element.76), channel_id=1, source_target_pairs={{0,3},{1,2},{2,1},{3,0},{4,7},{5,6},{6,5},{7,4},{8,11},{9,10},{10,... | collective-permute-start | bytes 245768 | tf_op jit(solution)/shard_map/ppermute | solution.py:401
  48.1 6.4 %collective-permute-start.20 = (bf16[80,512]{1,0:T(8,128)(2,1)S(1)}, bf16[80,512]{1,0:T(8,128)(2,1)S(1)}, u32[]{:S(2)}, u32[]{:S(2)}) collective-permute-start(bf16[80,512]{1,0:T(8,128)(2,1)S(1)} %shard_map.212.refs_0_), channel_id=1, source_target_pairs={{0,3},{1,2},{2,1},{3,0},{4,7},{5,6},{6,5},{7,4},{8,11},{9,10},{10,... | collective-permute-start | bytes 245768 | tf_op jit(solution)/shard_map/ppermute | solution.py:401
  50.5 6.1 %collective-permute-start.19 = (bf16[80,512]{1,0:T(8,128)(2,1)S(1)}, bf16[80,512]{1,0:T(8,128)(2,1)S(1)}, u32[]{:S(2)}, u32[]{:S(2)}) collective-permute-start(bf16[80,512]{1,0:T(8,128)(2,1)S(1)} %shard_map.212.refs_0_), channel_id=1, source_target_pairs={{0,2},{1,3},{2,0},{3,1},{4,6},{5,7},{6,4},{7,5},{8,10},{9,11},{10,... | collective-permute-start | bytes 245768 | tf_op jit(solution)/shard_map/ppermute | solution.py:401
  51.4 5.3 %collective-permute-start.18 = (bf16[80,512]{1,0:T(8,128)(2,1)S(1)}, bf16[80,512]{1,0:T(8,128)(2,1)S(1)}, u32[]{:S(2)}, u32[]{:S(2)}) collective-permute-start(bf16[80,512]{1,0:T(8,128)(2,1)S(1)} %shard_map.212.refs_0_), channel_id=1, source_target_pairs={{0,1},{1,0},{2,3},{3,2},{4,5},{5,4},{6,7},{7,6},{8,9},{9,8},{10,11... | collective-permute-start | bytes 245768 | tf_op jit(solution)/shard_map/ppermute | solution.py:401
  56.7 7.1 %collective-permute-start.21 = (bf16[4,80,512]{2,1,0:T(8,128)(2,1)S(1)}, bf16[4,80,512]{2,1,0:T(8,128)(2,1)S(1)}, u32[]{:S(2)}, u32[]{:S(2)}) collective-permute-start(bf16[4,80,512]{2,1,0:T(8,128)(2,1)S(1)} %shard_map.213.refs_4_.own), channel_id=1, source_target_pairs={{0,8},{4,12},{8,0},{12,4},{1,9},{5,13},{9,1},{13,5},{2,10},{6,14},... | collective-permute-start | bytes 983048 | tf_op jit(solution)/shard_map/ppermute | solution.py:401
  58.3 1.4 %collective-permute-start.11 = (bf16[4,48,512]{2,1,0:T(8,128)(2,1)S(1)}, bf16[4,48,512]{2,1,0:T(8,128)(2,1)S(1)}, u32[]{:S(2)}, u32[]{:S(2)}) collective-permute-start(bf16[4,48,512]{2,1,0:T(8,128)(2,1)S(1)} %shard_map.209.refs_0_), channel_id=1, source_target_pairs={{0,4},{4,0},{8,12},{12,8},{1,5},{5,1},{9,13},{13,9},{2,6},{6,2},{1... | collective-permute-start | bytes 589832 | tf_op jit(solution)/shard_map/ppermute | solution.py:401
  58.3 1.7 %collective-permute-start.12 = (bf16[4,48,512]{2,1,0:T(8,128)(2,1)S(1)}, bf16[4,48,512]{2,1,0:T(8,128)(2,1)S(1)}, u32[]{:S(2)}, u32[]{:S(2)}) collective-permute-start(bf16[4,48,512]{2,1,0:T(8,128)(2,1)S(1)} %collective-permute-done.10._.refs_1_), channel_id=1, source_target_pairs={{0,4},{4,0},{8,12},{12,8},{1,5},{5,1},{9,13},{13,9},{2,6},{6,2},{1... | collective-permute-start | bytes 589832 | tf_op jit(solution)/shard_map/ppermute | solution.py:401
  61.2 2.7 %collective-permute-start.23 = (bf16[4,80,512]{2,1,0:T(8,128)(2,1)S(1)}, bf16[4,80,512]{2,1,0:T(8,128)(2,1)S(1)}, u32[]{:S(2)}, u32[]{:S(2)}) collective-permute-start(bf16[4,80,512]{2,1,0:T(8,128)(2,1)S(1)} %get-tuple-element.78), channel_id=1, source_target_pairs={{0,4},{4,0},{8,12},{12,8},{1,5},{5,1},{9,13},{13,9},{2,6},{6,2},{1... | collective-permute-start | bytes 983048 | tf_op jit(solution)/shard_map/ppermute | solution.py:401
  63.9 1.6 %collective-permute-start.22 = (bf16[4,80,512]{2,1,0:T(8,128)(2,1)S(1)}, bf16[4,80,512]{2,1,0:T(8,128)(2,1)S(1)}, u32[]{:S(2)}, u32[]{:S(2)}) collective-permute-start(bf16[4,80,512]{2,1,0:T(8,128)(2,1)S(1)} %collective-permute-done.21.over_x), channel_id=1, source_target_pairs={{0,4},{4,0},{8,12},{12,8},{1,5},{5,1},{9,13},{13,9},{2,6},{6,2},{1... | collective-permute-start | bytes 983048 | tf_op jit(solution)/shard_map/ppermute | solution.py:401
